TPU v7x, 512 devices: a whole 4x8x8 slice. The times are simulated.
512 devices in a mesh: dp: 64 (over y, z), mp: 8 (over x, core).
Axes of the slice: x: 4, y: 8, z: 8, core: 2. Of those that a mesh axis runs over, the one named last changes fastest.
Arguments:
- features: bfloat16 [128, 1024, 512], P('mp', 'dp'), may hold values from -6 to 6
- conv_weight: bfloat16 [2, 512, 512], replicated, may hold values from -0.1875 to 0.1875
- proj_weight: bfloat16 [512, 1280], replicated, may hold values from -0.25 to 0.25
- pos_weight: bfloat16 [128, 16, 80, 80], P('dp', 'mp'), may hold values from -0.0625 to 0.0625
- utt_len: int32 [128], replicated, may hold values from 5120 to 158720, as said below
- pack_order: int32 [128], replicated, may hold values from 0 to 127, as said below
Outputs:
- hidden: bfloat16 [32768, 1280], P('dp', 'mp')
Inputs may be any that keep to these rules, and one draw needn't show every extreme that they name: `utt_len`: each a multiple of 320. The two utterances pack_order[2 o] and pack_order[2 o + 1] together span at most 512 frames. `pack_order`: A permutation of the utterances.
All inputs are finite; a program needn't handle non-finite values.
Results may differ from a plain program's by a relative error of at most 0.0066.
Values may be sent and summed in bfloat16 or wider, within the bound.
No kernel may reach another device: no remote copies, remote signals or barrier semaphores. Data moves between devices by JAX's collectives and lax.ppermute only.
A program may use at most 128 MiB of HBM per device.

v0:
```python
import functools

import jax
import jax.numpy as jnp
from jax import lax
from jax.experimental import pallas as pl
from jax.experimental.pallas import tpu as pltpu
from jax.sharding import PartitionSpec as P

HOP = 320
EPS = 1e-05
LANES = 128
TAP_ROWS = 112
GAP = 64
STEP = 16


def iota(shape, dim):
    return lax.broadcasted_iota(jnp.int32, shape, dim)


def one_hot(condition):
    return jnp.where(condition, 1.0, 0.0).astype(jnp.bfloat16)


def dot(a, b, contract=((1,), (0,))):
    return lax.dot_general(a, b, (contract, ((), ())), preferred_element_type=jnp.float32)


def layer_norm(values):
    average = jnp.mean(values, axis=-1, keepdims=True)
    centred = values - average
    variance = jnp.mean(centred * centred, axis=-1, keepdims=True)
    return centred * lax.rsqrt(variance + EPS)


def gelu(values):
    return 0.5 * values * (1.0 + lax.erf(values * (0.5**0.5)))


def pack_taps_kernel(taps_ref, out_ref):
    packed = []
    for g in range(2):
        rest = taps_ref[1, g, :, 48:80]
        packed.append(
            jnp.concatenate(
                [
                    jnp.concatenate([taps_ref[0, g], taps_ref[1, g, :, 0:48]], axis=1),
                    jnp.concatenate([rest[16 * r : 16 * r + 16] for r in range(4)], axis=1),
                    jnp.concatenate([rest[64:80], jnp.zeros((16, 96), rest.dtype)], axis=1),
                ],
                axis=0,
            )
        )
    for device in range(out_ref.shape[0]):
        out_ref[device] = packed[device % 2]


def front_kernel(utts, frames, parts, features_hbm, conv_hbm, proj_hbm, out_ref, features_ref, conv_ref, proj_ref, sems):
    copies = [
        pltpu.make_async_copy(source, target, sems.at[n])
        for n, (source, target) in enumerate(
            [(features_hbm, features_ref), (conv_hbm, conv_ref), (proj_hbm, proj_ref)]
        )
    ]
    for copy in copies:
        copy.start()
    rows = utts * frames
    copies[0].wait()
    features = features_ref[...]
    row = iota((rows, 2 * rows), 0)
    column = iota((rows, 2 * rows), 1)
    source = (row % utts) * (2 * frames) + 2 * (row // utts)
    first = dot(one_hot(column == source), features).astype(jnp.bfloat16)
    second = dot(one_hot(column == source + 1), features).astype(jnp.bfloat16)
    copies[1].wait()
    conv_out = dot(first, conv_ref[0]) + dot(second, conv_ref[1])
    hidden = gelu(layer_norm(conv_out)).astype(jnp.bfloat16)
    normed = layer_norm(hidden.astype(jnp.float32)).astype(jnp.bfloat16)
    copies[2].wait()
    projected = dot(normed, proj_ref[...]).astype(jnp.bfloat16)
    group = projected.shape[1] // (2 * parts)
    for part in range(parts):
        pieces = [
            projected[f * utts : (f + 1) * utts, (2 * part + g) * group : (2 * part + g + 1) * group]
            for g in range(2)
            for f in range(frames)
        ]
        out_ref[part] = jnp.concatenate(pieces, axis=1)


def order_kernel(order_ref, spread_ref, out_ref):
    utts, lanes = spread_ref.shape
    rows, width = out_ref.shape
    width //= 2
    chosen = one_hot(iota((utts, utts), 0) == order_ref[...])
    ordered = dot(chosen, spread_ref[...], ((0,), (0,))).astype(jnp.bfloat16)
    row = iota((rows, utts), 0)
    eighth = (row // 8) % 2 * 4 + row % 4
    slot = row // 16 * 4 + row // 4 % 2
    for which in range(2):
        same = slot + 2 * which == iota((rows, utts), 1)
        total = None
        for e in range(0, lanes // width, 2):
            left = jnp.concatenate([one_hot(same & (eighth == e + n)) for n in range(2)], axis=1)
            right = [ordered[:, (e + n) * width : (e + n + 1) * width] for n in range(2)]
            term = dot(left, jnp.concatenate(right, axis=0))
            total = term if total is None else total + term
        out_ref[:, which * width : (which + 1) * width] = total.astype(out_ref.dtype)


def pair_lengths(owner_ref, order_ref, len_ref):
    slot = owner_ref[0] // 2 * 4
    return [[len_ref[order_ref[slot + 2 * which + n]] // HOP for n in range(2)] for which in range(2)]


def place_kernel(total, half, owner_ref, order_ref, len_ref, rows_ref, shifted_ref, packed_ref, placed):
    lengths = pair_lengths(owner_ref, order_ref, len_ref)
    _, spots, group = placed.shape
    columns = rows_ref.shape[0]
    column = iota((1, columns), 1)
    is_first = (column // 4) % 2 == 0
    spot = iota((spots, columns), 0)
    for which in range(2):
        first_len, second_len = lengths[which]
        acc = None
        for odd in range(2):
            frame = (column // 8) * 8 + (column % 4) * 2 + odd
            target = jnp.where(is_first, frame, frame + first_len + GAP) + half
            valid = frame < jnp.where(is_first, first_len, second_len)
            target = jnp.where(valid, target, -1)
            lane = (2 * which + odd) * group
            term = dot(one_hot(spot == target), rows_ref[:, lane : lane + group])
            acc = term if acc is None else acc + term
        placed[which] = acc

    length = shifted_ref.shape[1]
    for which in range(2):
        for third in range(3):
            pairs = [k for k in range(3 * third, 3 * third + 3) if k < 8]
            pieces = [placed[which, 2 * k : 2 * k + length, :].astype(jnp.bfloat16) for k in pairs]
            pieces.append(jnp.zeros((length, 256 - group * len(pairs)), jnp.bfloat16))
            shifted_ref[which, :, third * 256 : (third + 1) * 256] = jnp.concatenate(pieces, axis=1)
        packed_ref[which] = jnp.where(
            iota((total, 1), 0) < lengths[which][0],
            placed[which, half : half + total, :],
            placed[which, half + GAP : half + GAP + total, :],
        )


def positional_kernel(
    swap, owner_ref, order_ref, len_ref, shifted_ref, packed_ref, *refs
):
    taps_refs, (out_ref, sums) = refs[:-2], refs[-2:]
    parity = owner_ref[0] % 2
    which = 1 - parity if swap else parity
    ring = taps_refs[0].shape[0]
    blocks = [[(ref, n) for n in range(ring)] for ref in taps_refs[:4] + taps_refs[6:]]
    blocks.insert(4, [(ref, n) for ref in taps_refs[4:6] for n in range(ring // 2)])
    slot = 2 * (owner_ref[0] - parity + which)
    first_len = len_ref[order_ref[slot]] // HOP
    second_len = len_ref[order_ref[slot + 1]] // HOP
    _, total, group = packed_ref.shape
    reach = sums.shape[0]

    for away, pieces in enumerate(blocks):
        start = pl.multiple_of(lax.rem(owner_ref[0] // ring + ring - away, ring) * STEP, STEP)
        left, right = [], []
        for slot in range(9):
            taps_ref, piece = pieces[min(slot, 7)]
            size = 96 if slot % 3 == 2 else 80
            left.append(taps_ref[piece, 0:size, :])
            fold = taps_ref[piece, 80:96, :]
            right += [fold] + [jnp.roll(fold, -32 * r, axis=1) for r in range(1, 4)]
            right.append(taps_ref[piece, 96:112, :])
            if size == 96:
                right.append(fold)
        matrix = jnp.concatenate([jnp.concatenate(left, axis=0), jnp.concatenate(right, axis=0)], axis=1)
        term = dot(shifted_ref[which, pl.ds(start, reach), :], matrix)
        sums[...] = term if away == 0 else sums[...] + term

    spot = iota((total, 1), 0)
    near = sums[0:total, 0:group] + sums[1 : total + 1, group : 2 * group]
    far = sums[GAP : GAP + total, 0:group] + sums[GAP + 1 : GAP + total + 1, group : 2 * group]
    conv_sum = jnp.where(spot < first_len + second_len, jnp.where(spot < first_len, near, far), 0.0)
    hidden = packed_ref[which] + gelu(conv_sum)
    hidden = jnp.concatenate([hidden, jnp.zeros((total, -group % LANES), jnp.float32)], axis=1)
    start = 0 if swap else pl.multiple_of(parity * group, 16)
    out_ref[pl.ds(start, group), :] = hidden.T[:group].astype(out_ref.dtype)


def join_kernel(owner_ref, received_hbm, own_hbm, out_hbm, sem):
    group = received_hbm.shape[0]
    start = pl.multiple_of((1 - owner_ref[0] % 2) * group, 16)
    copy = pltpu.make_async_copy(received_hbm, out_hbm.at[pl.ds(start, group), :], sem)
    copy.start()
    copy.wait()


VMEM = pl.BlockSpec(memory_space=pltpu.VMEM)
SMEM = pl.BlockSpec(memory_space=pltpu.SMEM)
ANY = pl.BlockSpec(memory_space=pl.ANY)


def send(values, ring, step):
    return lax.ppermute(values, "dp", [(o, (o + step * ring) % (ring * ring)) for o in range(ring * ring)])


def shards(features, conv_weight, proj_weight, pos_weight, utt_len, pack_order):
    owners = lax.axis_size("dp")
    parts = lax.axis_size("mp")
    utts, slice_rows, channels = features.shape
    frames = slice_rows // 2
    model_width = proj_weight.shape[1]
    width = model_width // parts
    total = frames * owners
    half = pos_weight.shape[0] * owners // 2
    params = pltpu.CompilerParams(vmem_limit_bytes=48 * 1024 * 1024)
    large = pltpu.CompilerParams(vmem_limit_bytes=62 * 1024 * 1024)

    owner = lax.axis_index("dp").reshape(1)
    ring = round(owners**0.5)
    along_z = [[y * ring + z for z in range(ring)] for y in range(ring)]
    tap_copies = pl.pallas_call(
        pack_taps_kernel,
        out_shape=jax.ShapeDtypeStruct((ring, TAP_ROWS, LANES), jnp.bfloat16),
        in_specs=[VMEM],
        out_specs=VMEM,
        compiler_params=params,
    )(pos_weight)
    taps = lax.all_to_all(tap_copies, "dp", 0, 0, axis_index_groups=along_z, tiled=True)

    sent = pl.pallas_call(
        functools.partial(front_kernel, utts, frames, parts),
        out_shape=jax.ShapeDtypeStruct((parts, utts, frames * width), jnp.bfloat16),
        in_specs=[ANY] * 3,
        out_specs=VMEM,
        scratch_shapes=[
            pltpu.VMEM((utts * slice_rows, channels), jnp.bfloat16),
            pltpu.VMEM(conv_weight.shape, jnp.bfloat16),
            pltpu.VMEM(proj_weight.shape, jnp.bfloat16),
            pltpu.SemaphoreType.DMA((3,)),
        ],
        compiler_params=pltpu.CompilerParams(vmem_limit_bytes=66900000),
    )(features.reshape(utts * slice_rows, channels), conv_weight, proj_weight)
    taps, sent = lax.optimization_barrier((taps, sent))
    one, minus_one, two, minus_two = [send(taps, ring, step) for step in (1, -1, 2, -2)]
    spread = lax.all_to_all(sent, "mp", split_axis=0, concat_axis=0, tiled=True)

    ordered = pl.pallas_call(
        order_kernel,
        out_shape=jax.ShapeDtypeStruct((owners * 8, 2 * width), jnp.bfloat16),
        in_specs=[VMEM] * 2,
        out_specs=VMEM,
        compiler_params=params,
    )(pack_order.reshape(1, -1), spread.reshape(parts * utts, frames * width))
    two, minus_two, _ = lax.optimization_barrier((two, minus_two, ordered))
    three, minus_three = send(two, ring, 1), send(minus_two, ring, -1)
    low, high = send(two[: ring // 2], ring, 2), send(minus_two[ring // 2 :], ring, -2)
    taps = (taps, one, two, three, low, high, minus_three, minus_two, minus_one)
    pair_rows = lax.all_to_all(
        ordered.reshape(owners, 8, 2 * width), "dp", split_axis=0, concat_axis=0, tiled=True
    )

    reach = total + GAP + 16
    length = reach + 2 * half - STEP
    group = width // 2
    scalars = (owner, pack_order, utt_len)
    shifted, packed = pl.pallas_call(
        functools.partial(place_kernel, total, half),
        out_shape=[
            jax.ShapeDtypeStruct((2, length, 768), jnp.bfloat16),
            jax.ShapeDtypeStruct((2, total, group), jnp.float32),
        ],
        in_specs=[SMEM, SMEM, SMEM, VMEM],
        out_specs=[VMEM] * 2,
        scratch_shapes=[pltpu.VMEM((2, length + STEP, group), jnp.float32)],
        compiler_params=params,
    )(*scalars, pair_rows.reshape(owners * 8, 2 * width))
    convolve = lambda swap: pl.pallas_call(
        functools.partial(positional_kernel, swap),
        out_shape=jax.ShapeDtypeStruct((group if swap else width, total), jnp.bfloat16),
        in_specs=[SMEM, SMEM, SMEM, VMEM, VMEM] + [VMEM] * len(taps),
        out_specs=VMEM,
        scratch_shapes=[pltpu.VMEM((reach, 256), jnp.float32)],
        compiler_params=params,
    )
    other = convolve(True)(*scalars, shifted, packed, *taps)
    packed, other = lax.optimization_barrier((packed, other))
    received = lax.ppermute(other, "dp", [(o, o ^ 1) for o in range(owners)])
    own = convolve(False)(*scalars, shifted, packed, *taps)
    hidden = pl.pallas_call(
        join_kernel,
        out_shape=jax.ShapeDtypeStruct((width, total), jnp.bfloat16),
        in_specs=[SMEM, ANY, ANY],
        out_specs=ANY,
        scratch_shapes=[pltpu.SemaphoreType.DMA],
        input_output_aliases={2: 0},
        compiler_params=params,
    )(owner, received, own)
    return hidden.T


def solution(mesh):
    in_specs = (P("mp", "dp", None), P(), P(), P("dp", "mp", None, None), P(), P())
    out_specs = P("dp", "mp")
    return jax.shard_map(shards, mesh=mesh, in_specs=in_specs, out_specs=out_specs, check_vma=False)
```

profile of v0, /device:TPU:48, one launch (start us, length us, event | category | flops | bytes accessed | tf_op | source)
XLA Modules:
  0.0 98.3 jit_solution(16176404652504605730)
XLA Ops:
  0.0 0.0 copy-start
  0.0 0.9 copy-done
  0.9 0.0 copy-start.1
  0.9 0.8 shard_map.64
  1.7 10.3 %all-to-all-start = ((bf16[8,112,128]{2,1,0:T(8,128)(2,1)}), bf16[8,112,128]{2,1,0:T(8,128)(2,1)}, u32[]{:S(2)}, u32[]{:S(2)}) async-start(bf16[8,112,128]{2,1,0:T(8,128)(2,1)} %shard_map.64), calls=%async_computation | async-start | bytes 458752 | tf_op jit(solution)/shard_map/all_to_all | solution.py:231
  12.0 0.0 copy-start.2
  12.0 3.2 %shard_map.65 = bf16[8,16,1280]{2,1,0:T(8,128)(2,1)} custom-call(bf16[256,512]{1,0:T(8,128)(2,1)} %bitcast.10, bf16[2,512,512]{2,1,0:T(8,128)(2,1)} %conv_hbm.1, bf16[512,1280]{1,0:T(8,128)(2,1)} %proj_hbm.1), custom_call_target="tpu_custom_call" | custom-call | tf_op jit(solution)/shard_map/pallas_call | solution.py:233
  15.2 8.0 %all-to-all-done.refs_0_ = bf16[8,112,128]{2,1,0:T(8,128)(2,1)} async-done(((bf16[8,112,128]{2,1,0:T(8,128)(2,1)}), bf16[8,112,128]{2,1,0:T(8,128)(2,1)}, u32[]{:S(2)}, u32[]{:S(2)}) %all-to-all-start) | async-done | bytes 229408 | tf_op jit(solution)/shard_map/all_to_all | solution.py:231
  23.3 12.5 %all_to_all.15 = bf16[8,16,1280]{2,1,0:T(8,128)(2,1)S(1)} all-to-all(bf16[8,16,1280]{2,1,0:T(8,128)(2,1)} %shard_map.65), channel_id=1, replica_groups=mesh['dp'=64,'mp'=8] {'mp'}, dimensions={0} | all-to-all | bytes 655360 | tf_op jit(solution)/shard_map/all_to_all | solution.py:248
  35.8 0.0 copy-done.1
  35.8 1.9 %shard_map.66 = bf16[512,320]{1,0:T(8,128)(2,1)} custom-call(s32[1,128]{1,0:T(1,128)S(1)} %bitcast.9, bf16[128,1280]{1,0:T(8,128)(2,1)S(1)} %bitcast.8), custom_call_target="tpu_custom_call" | custom-call | tf_op jit(solution)/shard_map/pallas_call | solution.py:250
  37.7 7.7 %all-to-all-start.2 = ((bf16[64,8,320]{2,1,0:T(8,128)(2,1)}), bf16[64,8,320]{2,1,0:T(8,128)(2,1)S(1)}, u32[]{:S(2)}, u32[]{:S(2)}) async-start(bf16[64,8,320]{2,1,0:T(8,128)(2,1)} %bitcast.4), calls=%async_computation.2 | async-start | bytes 786432 | tf_op jit(solution)/shard_map/all_to_all | solution.py:261
  45.5 2.2 %collective-permute-start.1 = (bf16[8,112,128]{2,1,0:T(8,128)(2,1)}, bf16[8,112,128]{2,1,0:T(8,128)(2,1)S(1)}, u32[]{:S(2)}, u32[]{:S(2)}) collective-permute-start(bf16[8,112,128]{2,1,0:T(8,128)(2,1)} %all-to-all-done.refs_0_), channel_id=1, source_target_pairs={{0,128},{8,136},{16,144},{24,152},{32,160},{40,168},{48,176},{56,1... | collective-permute-start | bytes 688136 | tf_op jit(solution)/shard_map/ppermute | solution.py:206
  47.7 4.6 %collective-permute-start.2 = (bf16[8,112,128]{2,1,0:T(8,128)(2,1)}, bf16[8,112,128]{2,1,0:T(8,128)(2,1)S(1)}, u32[]{:S(2)}, u32[]{:S(2)}) collective-permute-start(bf16[8,112,128]{2,1,0:T(8,128)(2,1)} %all-to-all-done.refs_0_), channel_id=1, source_target_pairs={{0,384},{8,392},{16,400},{24,408},{32,416},{40,424},{48,432},{56,4... | collective-permute-start | bytes 688136 | tf_op jit(solution)/shard_map/ppermute | solution.py:206
  52.3 2.5 %collective-permute-start = (bf16[8,112,128]{2,1,0:T(8,128)(2,1)}, bf16[8,112,128]{2,1,0:T(8,128)(2,1)S(1)}, u32[]{:S(2)}, u32[]{:S(2)}) collective-permute-start(bf16[8,112,128]{2,1,0:T(8,128)(2,1)} %all-to-all-done.refs_0_), channel_id=1, source_target_pairs={{0,64},{8,72},{16,80},{24,88},{32,96},{40,104},{48,112},{56,120},{... | collective-permute-start | bytes 688136 | tf_op jit(solution)/shard_map/ppermute | solution.py:206
  54.8 3.9 %collective-permute-start.7 = (bf16[8,112,128]{2,1,0:T(8,128)(2,1)}, bf16[8,112,128]{2,1,0:T(8,128)(2,1)S(1)}, u32[]{:S(2)}, u32[]{:S(2)}) collective-permute-start(bf16[8,112,128]{2,1,0:T(8,128)(2,1)} %all-to-all-done.refs_0_), channel_id=1, source_target_pairs={{0,448},{8,456},{16,464},{24,472},{32,480},{40,488},{48,496},{56,5... | collective-permute-start | bytes 688136 | tf_op jit(solution)/shard_map/ppermute | solution.py:206
  58.7 8.2 %collective-permute-done.1.refs_2_ = bf16[8,112,128]{2,1,0:T(8,128)(2,1)S(1)} collective-permute-done((bf16[8,112,128]{2,1,0:T(8,128)(2,1)}, bf16[8,112,128]{2,1,0:T(8,128)(2,1)S(1)}, u32[]{:S(2)}, u32[]{:S(2)}) %collective-permute-start.1) | collective-permute-done | bytes 229408 | tf_op jit(solution)/shard_map/ppermute | solution.py:206
  66.9 0.0 collective-permute-done.2.refs_7_
  66.9 2.2 %collective-permute-start.3 = (bf16[8,112,128]{2,1,0:T(8,128)(2,1)S(1)}, bf16[8,112,128]{2,1,0:T(8,128)(2,1)S(1)}, u32[]{:S(2)}, u32[]{:S(2)}) collective-permute-start(bf16[8,112,128]{2,1,0:T(8,128)(2,1)S(1)} %collective-permute-done.1.refs_2_), channel_id=1, source_target_pairs={{0,64},{8,72},{16,80},{24,88},{32,96},{40,104},{48,112},{56,120},{... | collective-permute-start | bytes 688136 | tf_op jit(solution)/shard_map/ppermute | solution.py:206
  69.1 3.7 %collective-permute-start.6 = (bf16[8,112,128]{2,1,0:T(8,128)(2,1)S(1)}, bf16[8,112,128]{2,1,0:T(8,128)(2,1)S(1)}, u32[]{:S(2)}, u32[]{:S(2)}) collective-permute-start(bf16[8,112,128]{2,1,0:T(8,128)(2,1)S(1)} %collective-permute-done.2.refs_7_), channel_id=1, source_target_pairs={{0,448},{8,456},{16,464},{24,472},{32,480},{40,488},{48,496},{56,5... | collective-permute-start | bytes 688136 | tf_op jit(solution)/shard_map/ppermute | solution.py:206
  72.8 5.0 %collective-permute-start.4 = (bf16[4,112,128]{2,1,0:T(8,128)(2,1)S(1)}, bf16[4,112,128]{2,1,0:T(8,128)(2,1)S(1)}, u32[]{:S(2)}, u32[]{:S(2)}) collective-permute-start(bf16[4,112,128]{2,1,0:T(8,128)(2,1)S(1)} %slice.6), channel_id=1, source_target_pairs={{0,128},{8,136},{16,144},{24,152},{32,160},{40,168},{48,176},{56,1... | collective-permute-start | bytes 344072 | tf_op jit(solution)/shard_map/ppermute | solution.py:206
  77.9 0.0 collective-permute-done.refs_1_
  77.9 1.9 %collective-permute-start.5 = (bf16[4,112,128]{2,1,0:T(8,128)(2,1)S(1)}, bf16[4,112,128]{2,1,0:T(8,128)(2,1)S(1)}, u32[]{:S(2)}, u32[]{:S(2)}) collective-permute-start(bf16[4,112,128]{2,1,0:T(8,128)(2,1)S(1)} %slice.7), channel_id=1, source_target_pairs={{0,384},{8,392},{16,400},{24,408},{32,416},{40,424},{48,432},{56,4... | collective-permute-start | bytes 344072 | tf_op jit(solution)/shard_map/ppermute | solution.py:206
  79.8 0.0 all-to-all-done.2
  79.8 0.0 copy-done.2
  79.8 2.0 %shard_map.67 = (bf16[2,704,768]{2,1,0:T(8,128)(2,1)S(1)}, f32[2,512,80]{2,1,0:T(8,128)S(1)}) custom-call(s32[1]{0:T(128)} %bitcast.owner_ref, s32[128]{0:T(128)S(1)} %copy-done.1, s32[128]{0:T(128)S(1)} %copy-done.2, bf16[512,320]{1,0:T(8,128)(2,1)S(1)} %bitcast.7), custom_call_target="tpu_custom_call" | custom-call | tf_op jit(solution)/shard_map/pallas_call | solution.py:269
  81.8 0.0 collective-permute-done.7.refs_8_
  81.9 0.0 collective-permute-done.4.refs_4_
  81.9 5.2 %collective-permute-done.5.refs_5_ = bf16[4,112,128]{2,1,0:T(8,128)(2,1)S(1)} collective-permute-done((bf16[4,112,128]{2,1,0:T(8,128)(2,1)S(1)}, bf16[4,112,128]{2,1,0:T(8,128)(2,1)S(1)}, u32[]{:S(2)}, u32[]{:S(2)}) %collective-permute-start.5) | collective-permute-done | bytes 114720 | tf_op jit(solution)/shard_map/ppermute | solution.py:206
  87.1 0.0 collective-permute-done.3.refs_3_
  87.1 0.0 collective-permute-done.6.refs_6_
  87.1 3.3 %shard_map.68 = bf16[80,512]{1,0:T(8,128)(2,1)S(1)} custom-call(s32[1]{0:T(128)} %bitcast.owner_ref, s32[128]{0:T(128)S(1)} %copy-done.1, s32[128]{0:T(128)S(1)} %copy-done.2, bf16[2,704,768]{2,1,0:T(8,128)(2,1)S(1)} %get-tuple-element.15.shifted_ref, f32[2,512,80]{2,1,0:T(8,128)S(1)} %get-tuple-element.20.packed_ref, ...), custom_call_target="tpu_custom_call" | custom-call | tf_op jit(solution)/shard_map/pallas_call | solution.py:288
  90.4 3.3 %collective-permute-start.8 = (bf16[80,512]{1,0:T(8,128)(2,1)S(1)}, bf16[80,512]{1,0:T(8,128)(2,1)S(1)}, u32[]{:S(2)}, u32[]{:S(2)}) collective-permute-start(bf16[80,512]{1,0:T(8,128)(2,1)S(1)} %shard_map.68), channel_id=1, source_target_pairs={{0,8},{8,0},{16,24},{24,16},{32,40},{40,32},{48,56},{56,48},{64,72... | collective-permute-start | bytes 245768 | tf_op jit(solution)/shard_map/ppermute | solution.py:290
  93.7 3.9 %shard_map.69.own_hbm = bf16[160,512]{1,0:T(8,128)(2,1)} custom-call(s32[1]{0:T(128)} %bitcast.owner_ref, s32[128]{0:T(128)S(1)} %copy-done.1, s32[128]{0:T(128)S(1)} %copy-done.2, bf16[2,704,768]{2,1,0:T(8,128)(2,1)S(1)} %get-tuple-element.15.shifted_ref, f32[2,512,80]{2,1,0:T(8,128)S(1)} %get-tuple-element.20.packed_ref, ...), custom_call_target="tpu_custom_call" | custom-call | tf_op jit(solution)/shard_map/pallas_call | solution.py:291
  97.7 0.0 collective-permute-done.8.received_hbm
  97.7 0.6 shard_map.70
  (2 shorter events, 0.0 us)
Async XLA Ops:
  0.0 0.9 copy-start
  0.9 34.9 %copy-start.1 = (s32[128]{0:T(128)S(1)}, s32[128]{0:T(128)}, u32[]{:S(2)}) copy-start(s32[128]{0:T(128)} %order_ref.5) | copy-start | bytes 1540
  1.7 21.6 %all-to-all-start = ((bf16[8,112,128]{2,1,0:T(8,128)(2,1)}), bf16[8,112,128]{2,1,0:T(8,128)(2,1)}, u32[]{:S(2)}, u32[]{:S(2)}) async-start(bf16[8,112,128]{2,1,0:T(8,128)(2,1)} %shard_map.64), calls=%async_computation | async-start | bytes 458752 | tf_op jit(solution)/shard_map/all_to_all | solution.py:231
  12.0 67.8 %copy-start.2 = (s32[128]{0:T(128)S(1)}, s32[128]{0:T(128)}, u32[]{:S(2)}) copy-start(s32[128]{0:T(128)} %len_ref.5) | copy-start | bytes 1540
  37.7 42.1 %all-to-all-start.2 = ((bf16[64,8,320]{2,1,0:T(8,128)(2,1)}), bf16[64,8,320]{2,1,0:T(8,128)(2,1)S(1)}, u32[]{:S(2)}, u32[]{:S(2)}) async-start(bf16[64,8,320]{2,1,0:T(8,128)(2,1)} %bitcast.4), calls=%async_computation.2 | async-start | bytes 786432 | tf_op jit(solution)/shard_map/all_to_all | solution.py:261
  45.5 21.4 %collective-permute-start.1 = (bf16[8,112,128]{2,1,0:T(8,128)(2,1)}, bf16[8,112,128]{2,1,0:T(8,128)(2,1)S(1)}, u32[]{:S(2)}, u32[]{:S(2)}) collective-permute-start(bf16[8,112,128]{2,1,0:T(8,128)(2,1)} %all-to-all-done.refs_0_), channel_id=1, source_target_pairs={{0,128},{8,136},{16,144},{24,152},{32,160},{40,168},{48,176},{56,1... | collective-permute-start | bytes 688136 | tf_op jit(solution)/shard_map/ppermute | solution.py:206
  47.7 19.3 %collective-permute-start.2 = (bf16[8,112,128]{2,1,0:T(8,128)(2,1)}, bf16[8,112,128]{2,1,0:T(8,128)(2,1)S(1)}, u32[]{:S(2)}, u32[]{:S(2)}) collective-permute-start(bf16[8,112,128]{2,1,0:T(8,128)(2,1)} %all-to-all-done.refs_0_), channel_id=1, source_target_pairs={{0,384},{8,392},{16,400},{24,408},{32,416},{40,424},{48,432},{56,4... | collective-permute-start | bytes 688136 | tf_op jit(solution)/shard_map/ppermute | solution.py:206
  52.3 25.6 %collective-permute-start = (bf16[8,112,128]{2,1,0:T(8,128)(2,1)}, bf16[8,112,128]{2,1,0:T(8,128)(2,1)S(1)}, u32[]{:S(2)}, u32[]{:S(2)}) collective-permute-start(bf16[8,112,128]{2,1,0:T(8,128)(2,1)} %all-to-all-done.refs_0_), channel_id=1, source_target_pairs={{0,64},{8,72},{16,80},{24,88},{32,96},{40,104},{48,112},{56,120},{... | collective-permute-start | bytes 688136 | tf_op jit(solution)/shard_map/ppermute | solution.py:206
  54.8 27.1 %collective-permute-start.7 = (bf16[8,112,128]{2,1,0:T(8,128)(2,1)}, bf16[8,112,128]{2,1,0:T(8,128)(2,1)S(1)}, u32[]{:S(2)}, u32[]{:S(2)}) collective-permute-start(bf16[8,112,128]{2,1,0:T(8,128)(2,1)} %all-to-all-done.refs_0_), channel_id=1, source_target_pairs={{0,448},{8,456},{16,464},{24,472},{32,480},{40,488},{48,496},{56,5... | collective-permute-start | bytes 688136 | tf_op jit(solution)/shard_map/ppermute | solution.py:206
  66.9 20.2 %collective-permute-start.3 = (bf16[8,112,128]{2,1,0:T(8,128)(2,1)S(1)}, bf16[8,112,128]{2,1,0:T(8,128)(2,1)S(1)}, u32[]{:S(2)}, u32[]{:S(2)}) collective-permute-start(bf16[8,112,128]{2,1,0:T(8,128)(2,1)S(1)} %collective-permute-done.1.refs_2_), channel_id=1, source_target_pairs={{0,64},{8,72},{16,80},{24,88},{32,96},{40,104},{48,112},{56,120},{... | collective-permute-start | bytes 688136 | tf_op jit(solution)/shard_map/ppermute | solution.py:206
  69.1 18.0 %collective-permute-start.6 = (bf16[8,112,128]{2,1,0:T(8,128)(2,1)S(1)}, bf16[8,112,128]{2,1,0:T(8,128)(2,1)S(1)}, u32[]{:S(2)}, u32[]{:S(2)}) collective-permute-start(bf16[8,112,128]{2,1,0:T(8,128)(2,1)S(1)} %collective-permute-done.2.refs_7_), channel_id=1, source_target_pairs={{0,448},{8,456},{16,464},{24,472},{32,480},{40,488},{48,496},{56,5... | collective-permute-start | bytes 688136 | tf_op jit(solution)/shard_map/ppermute | solution.py:206
  72.8 9.0 %collective-permute-start.4 = (bf16[4,112,128]{2,1,0:T(8,128)(2,1)S(1)}, bf16[4,112,128]{2,1,0:T(8,128)(2,1)S(1)}, u32[]{:S(2)}, u32[]{:S(2)}) collective-permute-start(bf16[4,112,128]{2,1,0:T(8,128)(2,1)S(1)} %slice.6), channel_id=1, source_target_pairs={{0,128},{8,136},{16,144},{24,152},{32,160},{40,168},{48,176},{56,1... | collective-permute-start | bytes 344072 | tf_op jit(solution)/shard_map/ppermute | solution.py:206
  77.9 9.2 %collective-permute-start.5 = (bf16[4,112,128]{2,1,0:T(8,128)(2,1)S(1)}, bf16[4,112,128]{2,1,0:T(8,128)(2,1)S(1)}, u32[]{:S(2)}, u32[]{:S(2)}) collective-permute-start(bf16[4,112,128]{2,1,0:T(8,128)(2,1)S(1)} %slice.7), channel_id=1, source_target_pairs={{0,384},{8,392},{16,400},{24,408},{32,416},{40,424},{48,432},{56,4... | collective-permute-start | bytes 344072 | tf_op jit(solution)/shard_map/ppermute | solution.py:206
  90.4 7.3 %collective-permute-start.8 = (bf16[80,512]{1,0:T(8,128)(2,1)S(1)}, bf16[80,512]{1,0:T(8,128)(2,1)S(1)}, u32[]{:S(2)}, u32[]{:S(2)}) collective-permute-start(bf16[80,512]{1,0:T(8,128)(2,1)S(1)} %shard_map.68), channel_id=1, source_target_pairs={{0,8},{8,0},{16,24},{24,16},{32,40},{40,32},{48,56},{56,48},{64,72... | collective-permute-start | bytes 245768 | tf_op jit(solution)/shard_map/ppermute | solution.py:290
where the time goes:
time: 99 us; the launch traced here: 98.3 us
  starting transfers between devices  47.4 us (48%)
  waiting for transfers between devices  21.5 us (22%)
  Pallas kernels  15.8 us (16%)
  blocking collectives  12.5 us (13%)
    ppermute x8, starting transfers between devices, send(): lax.ppermute(values, 'dp', [(o, (o + step * ring) % (ring * ring)) for o...  26 us
    ppermute x8, waiting for transfers between devices, send(): lax.ppermute(values, 'dp', [(o, (o + step * ring) % (ring * ring)) for o...  13.5 us
    all_to_all x1, blocking collectives, shards(): spread = lax.all_to_all(sent, 'mp', split_axis=0, concat_axis=0, tiled=True)  12.5 us
    all_to_all x1, starting transfers between devices, shards(): lax.all_to_all(tap_copies, 'dp', 0, 0, axis_index_groups=along_z, tiled=T...  10.3 us
    all_to_all x1, waiting for transfers between devices, shards(): lax.all_to_all(tap_copies, 'dp', 0, 0, axis_index_groups=along_z, tiled=T...  8.05 us
    all_to_all x1, starting transfers between devices, shards(): lax.all_to_all(ordered.reshape(owners, 8, 2 * width), 'dp', split_axis=0,...  7.75 us
    pallas_call x1, Pallas kernels, shards(): own = convolve(False)(*scalars, shifted, packed, *taps)  3.93 us
    ppermute x1, starting transfers between devices, shards(): received = lax.ppermute(other, 'dp', [(o, o ^ 1) for o in range(owners)])  3.34 us
  transfers between devices with their start and end apart: 11, of which 3 were waited for; matrix products, arithmetic and copies ran while one was open for 0% of the time, Pallas kernels for 9%

commit v1 on v0

--- a/solution.py
+++ b/solution.py
@@ -254,7 +254,7 @@
         out_specs=VMEM,
         compiler_params=params,
     )(pack_order.reshape(1, -1), spread.reshape(parts * utts, frames * width))
-    two, minus_two, _ = lax.optimization_barrier((two, minus_two, ordered))
+    one, minus_one, two, minus_two, ordered = lax.optimization_barrier((one, minus_one, two, minus_two, ordered))
     three, minus_three = send(two, ring, 1), send(minus_two, ring, -1)
     low, high = send(two[: ring // 2], ring, 2), send(minus_two[ring // 2 :], ring, -2)
     taps = (taps, one, two, three, low, high, minus_three, minus_two, minus_one)

time: 99 us -> 94.2 us (0.952)
  the two profiles are of different devices: /device:TPU:48 before, /device:TPU:18 now
where the time goes in v1:
time: 94.2 us; the launch traced here: 93.5 us
  starting transfers between devices  52.8 us (56%)
  waiting for transfers between devices  23.9 us (25%)
  Pallas kernels  15.7 us (17%)
    ppermute x8, starting transfers between devices, send(): lax.ppermute(values, 'dp', [(o, (o + step * ring) % (ring * ring)) for o...  29.2 us
    ppermute x8, waiting for transfers between devices, send(): lax.ppermute(values, 'dp', [(o, (o + step * ring) % (ring * ring)) for o...  14.3 us
    all_to_all x1, starting transfers between devices, shards(): lax.all_to_all(tap_copies, 'dp', 0, 0, axis_index_groups=along_z, tiled=T...  10.3 us
    all_to_all x1, waiting for transfers between devices, shards(): lax.all_to_all(tap_copies, 'dp', 0, 0, axis_index_groups=along_z, tiled=T...  8.06 us
    all_to_all x1, starting transfers between devices, shards(): lax.all_to_all(ordered.reshape(owners, 8, 2 * width), 'dp', split_axis=0,...  5.63 us
    all_to_all x1, starting transfers between devices, shards(): spread = lax.all_to_all(sent, 'mp', split_axis=0, concat_axis=0, tiled=True)  4.83 us
    pallas_call x1, Pallas kernels, shards(): own = convolve(False)(*scalars, shifted, packed, *taps)  3.92 us
    pallas_call x1, Pallas kernels, shards(): other = convolve(True)(*scalars, shifted, packed, *taps)  3.25 us
  transfers between devices with their start and end apart: 12, of which 5 were waited for; matrix products, arithmetic and copies ran while one was open for 0% of the time, Pallas kernels for 12%

profile of v1, /device:TPU:18, one launch (start us, length us, event | category | flops | bytes accessed | tf_op | source)
XLA Modules:
  0.0 93.5 jit_solution(17964312931858484820)
XLA Ops:
  0.0 0.0 copy-start
  0.0 0.9 copy-done
  0.9 0.0 copy-start.1
  0.9 0.8 shard_map.64
  1.7 10.3 %all-to-all-start = ((bf16[8,112,128]{2,1,0:T(8,128)(2,1)}), bf16[8,112,128]{2,1,0:T(8,128)(2,1)}, u32[]{:S(2)}, u32[]{:S(2)}) async-start(bf16[8,112,128]{2,1,0:T(8,128)(2,1)} %shard_map.64), calls=%async_computation | async-start | bytes 458752 | tf_op jit(solution)/shard_map/all_to_all | solution.py:231
  12.0 0.0 copy-start.2
  12.0 3.2 %shard_map.65 = bf16[8,16,1280]{2,1,0:T(8,128)(2,1)} custom-call(bf16[256,512]{1,0:T(8,128)(2,1)} %bitcast.10, bf16[2,512,512]{2,1,0:T(8,128)(2,1)} %conv_hbm.1, bf16[512,1280]{1,0:T(8,128)(2,1)} %proj_hbm.1), custom_call_target="tpu_custom_call" | custom-call | tf_op jit(solution)/shard_map/pallas_call | solution.py:233
  15.2 8.1 %all-to-all-done.refs_0_ = bf16[8,112,128]{2,1,0:T(8,128)(2,1)} async-done(((bf16[8,112,128]{2,1,0:T(8,128)(2,1)}), bf16[8,112,128]{2,1,0:T(8,128)(2,1)}, u32[]{:S(2)}, u32[]{:S(2)}) %all-to-all-start) | async-done | bytes 229408 | tf_op jit(solution)/shard_map/all_to_all | solution.py:231
  23.3 4.8 %all-to-all-start.1 = ((bf16[8,16,1280]{2,1,0:T(8,128)(2,1)}), bf16[8,16,1280]{2,1,0:T(8,128)(2,1)S(1)}, u32[]{:S(2)}, u32[]{:S(2)}) async-start(bf16[8,16,1280]{2,1,0:T(8,128)(2,1)} %shard_map.65), calls=%async_computation.1 | async-start | bytes 655360 | tf_op jit(solution)/shard_map/all_to_all | solution.py:248
  28.1 3.5 %collective-permute-start = (bf16[8,112,128]{2,1,0:T(8,128)(2,1)}, bf16[8,112,128]{2,1,0:T(8,128)(2,1)S(1)}, u32[]{:S(2)}, u32[]{:S(2)}) collective-permute-start(bf16[8,112,128]{2,1,0:T(8,128)(2,1)} %all-to-all-done.refs_0_), channel_id=1, source_target_pairs={{0,64},{8,72},{16,80},{24,88},{32,96},{40,104},{48,112},{56,120},{... | collective-permute-start | bytes 688136 | tf_op jit(solution)/shard_map/ppermute | solution.py:206
  31.6 2.4 %collective-permute-start.1 = (bf16[8,112,128]{2,1,0:T(8,128)(2,1)}, bf16[8,112,128]{2,1,0:T(8,128)(2,1)S(1)}, u32[]{:S(2)}, u32[]{:S(2)}) collective-permute-start(bf16[8,112,128]{2,1,0:T(8,128)(2,1)} %all-to-all-done.refs_0_), channel_id=1, source_target_pairs={{0,448},{8,456},{16,464},{24,472},{32,480},{40,488},{48,496},{56,5... | collective-permute-start | bytes 688136 | tf_op jit(solution)/shard_map/ppermute | solution.py:206
  34.0 6.9 %collective-permute-start.2 = (bf16[8,112,128]{2,1,0:T(8,128)(2,1)}, bf16[8,112,128]{2,1,0:T(8,128)(2,1)S(1)}, u32[]{:S(2)}, u32[]{:S(2)}) collective-permute-start(bf16[8,112,128]{2,1,0:T(8,128)(2,1)} %all-to-all-done.refs_0_), channel_id=1, source_target_pairs={{0,128},{8,136},{16,144},{24,152},{32,160},{40,168},{48,176},{56,1... | collective-permute-start | bytes 688136 | tf_op jit(solution)/shard_map/ppermute | solution.py:206
  40.9 1.9 %collective-permute-start.3 = (bf16[8,112,128]{2,1,0:T(8,128)(2,1)}, bf16[8,112,128]{2,1,0:T(8,128)(2,1)S(1)}, u32[]{:S(2)}, u32[]{:S(2)}) collective-permute-start(bf16[8,112,128]{2,1,0:T(8,128)(2,1)} %all-to-all-done.refs_0_), channel_id=1, source_target_pairs={{0,384},{8,392},{16,400},{24,408},{32,416},{40,424},{48,432},{56,4... | collective-permute-start | bytes 688136 | tf_op jit(solution)/shard_map/ppermute | solution.py:206
  42.8 0.0 all-to-all-done.1
  42.8 0.0 copy-done.1
  42.8 1.9 %shard_map.66 = bf16[512,320]{1,0:T(8,128)(2,1)} custom-call(s32[1,128]{1,0:T(1,128)S(1)} %bitcast.9, bf16[128,1280]{1,0:T(8,128)(2,1)S(1)} %bitcast.8), custom_call_target="tpu_custom_call" | custom-call | tf_op jit(solution)/shard_map/pallas_call | solution.py:250
  44.7 0.0 collective-permute-done.refs_1_
  44.7 0.0 collective-permute-done.1.refs_8_
  44.7 4.5 %collective-permute-done.2.refs_2_ = bf16[8,112,128]{2,1,0:T(8,128)(2,1)S(1)} collective-permute-done((bf16[8,112,128]{2,1,0:T(8,128)(2,1)}, bf16[8,112,128]{2,1,0:T(8,128)(2,1)S(1)}, u32[]{:S(2)}, u32[]{:S(2)}) %collective-permute-start.2) | collective-permute-done | bytes 229408 | tf_op jit(solution)/shard_map/ppermute | solution.py:206
  49.3 5.7 %collective-permute-done.3.refs_7_ = bf16[8,112,128]{2,1,0:T(8,128)(2,1)S(1)} collective-permute-done((bf16[8,112,128]{2,1,0:T(8,128)(2,1)}, bf16[8,112,128]{2,1,0:T(8,128)(2,1)S(1)}, u32[]{:S(2)}, u32[]{:S(2)}) %collective-permute-start.3) | collective-permute-done | bytes 229408 | tf_op jit(solution)/shard_map/ppermute | solution.py:206
  54.9 5.6 %all-to-all-start.2 = ((bf16[64,8,320]{2,1,0:T(8,128)(2,1)}), bf16[64,8,320]{2,1,0:T(8,128)(2,1)S(1)}, u32[]{:S(2)}, u32[]{:S(2)}) async-start(bf16[64,8,320]{2,1,0:T(8,128)(2,1)} %bitcast.4), calls=%async_computation.2 | async-start | bytes 786432 | tf_op jit(solution)/shard_map/all_to_all | solution.py:261
  60.6 3.4 %collective-permute-start.4 = (bf16[8,112,128]{2,1,0:T(8,128)(2,1)S(1)}, bf16[8,112,128]{2,1,0:T(8,128)(2,1)S(1)}, u32[]{:S(2)}, u32[]{:S(2)}) collective-permute-start(bf16[8,112,128]{2,1,0:T(8,128)(2,1)S(1)} %collective-permute-done.2.refs_2_), channel_id=1, source_target_pairs={{0,64},{8,72},{16,80},{24,88},{32,96},{40,104},{48,112},{56,120},{... | collective-permute-start | bytes 688136 | tf_op jit(solution)/shard_map/ppermute | solution.py:206
  64.0 2.4 %collective-permute-start.7 = (bf16[8,112,128]{2,1,0:T(8,128)(2,1)S(1)}, bf16[8,112,128]{2,1,0:T(8,128)(2,1)S(1)}, u32[]{:S(2)}, u32[]{:S(2)}) collective-permute-start(bf16[8,112,128]{2,1,0:T(8,128)(2,1)S(1)} %collective-permute-done.3.refs_7_), channel_id=1, source_target_pairs={{0,448},{8,456},{16,464},{24,472},{32,480},{40,488},{48,496},{56,5... | collective-permute-start | bytes 688136 | tf_op jit(solution)/shard_map/ppermute | solution.py:206
  66.5 6.8 %collective-permute-start.5 = (bf16[4,112,128]{2,1,0:T(8,128)(2,1)S(1)}, bf16[4,112,128]{2,1,0:T(8,128)(2,1)S(1)}, u32[]{:S(2)}, u32[]{:S(2)}) collective-permute-start(bf16[4,112,128]{2,1,0:T(8,128)(2,1)S(1)} %slice.6), channel_id=1, source_target_pairs={{0,128},{8,136},{16,144},{24,152},{32,160},{40,168},{48,176},{56,1... | collective-permute-start | bytes 344072 | tf_op jit(solution)/shard_map/ppermute | solution.py:206
  73.2 1.9 %collective-permute-start.6 = (bf16[4,112,128]{2,1,0:T(8,128)(2,1)S(1)}, bf16[4,112,128]{2,1,0:T(8,128)(2,1)S(1)}, u32[]{:S(2)}, u32[]{:S(2)}) collective-permute-start(bf16[4,112,128]{2,1,0:T(8,128)(2,1)S(1)} %slice.7), channel_id=1, source_target_pairs={{0,384},{8,392},{16,400},{24,408},{32,416},{40,424},{48,432},{56,4... | collective-permute-start | bytes 344072 | tf_op jit(solution)/shard_map/ppermute | solution.py:206
  75.2 1.5 %all-to-all-done.2 = bf16[64,8,320]{2,1,0:T(8,128)(2,1)S(1)} async-done(((bf16[64,8,320]{2,1,0:T(8,128)(2,1)}), bf16[64,8,320]{2,1,0:T(8,128)(2,1)S(1)}, u32[]{:S(2)}, u32[]{:S(2)}) %all-to-all-start.2) | async-done | bytes 327712 | tf_op jit(solution)/shard_map/all_to_all | solution.py:261
  76.7 0.0 copy-done.2
  76.7 2.0 %shard_map.67 = (bf16[2,704,768]{2,1,0:T(8,128)(2,1)S(1)}, f32[2,512,80]{2,1,0:T(8,128)S(1)}) custom-call(s32[1]{0:T(128)} %bitcast.owner_ref, s32[128]{0:T(128)S(1)} %copy-done.1, s32[128]{0:T(128)S(1)} %copy-done.2, bf16[512,320]{1,0:T(8,128)(2,1)S(1)} %bitcast.7), custom_call_target="tpu_custom_call" | custom-call | tf_op jit(solution)/shard_map/pallas_call | solution.py:269
  78.7 0.0 collective-permute-done.5.refs_4_
  78.7 4.1 %collective-permute-done.6.refs_5_ = bf16[4,112,128]{2,1,0:T(8,128)(2,1)S(1)} collective-permute-done((bf16[4,112,128]{2,1,0:T(8,128)(2,1)S(1)}, bf16[4,112,128]{2,1,0:T(8,128)(2,1)S(1)}, u32[]{:S(2)}, u32[]{:S(2)}) %collective-permute-start.6) | collective-permute-done | bytes 114720 | tf_op jit(solution)/shard_map/ppermute | solution.py:206
  82.9 0.0 collective-permute-done.4.refs_3_
  82.9 0.0 collective-permute-done.7.refs_6_
  82.9 3.2 %shard_map.68 = bf16[80,512]{1,0:T(8,128)(2,1)S(1)} custom-call(s32[1]{0:T(128)} %bitcast.owner_ref, s32[128]{0:T(128)S(1)} %copy-done.1, s32[128]{0:T(128)S(1)} %copy-done.2, bf16[2,704,768]{2,1,0:T(8,128)(2,1)S(1)} %get-tuple-element.20.shifted_ref, f32[2,512,80]{2,1,0:T(8,128)S(1)} %get-tuple-element.26.packed_ref, ...), custom_call_target="tpu_custom_call" | custom-call | tf_op jit(solution)/shard_map/pallas_call | solution.py:288
  86.1 2.8 %collective-permute-start.8 = (bf16[80,512]{1,0:T(8,128)(2,1)S(1)}, bf16[80,512]{1,0:T(8,128)(2,1)S(1)}, u32[]{:S(2)}, u32[]{:S(2)}) collective-permute-start(bf16[80,512]{1,0:T(8,128)(2,1)S(1)} %shard_map.68), channel_id=1, source_target_pairs={{0,8},{8,0},{16,24},{24,16},{32,40},{40,32},{48,56},{56,48},{64,72... | collective-permute-start | bytes 245768 | tf_op jit(solution)/shard_map/ppermute | solution.py:290
  88.9 3.9 %shard_map.69.own_hbm = bf16[160,512]{1,0:T(8,128)(2,1)} custom-call(s32[1]{0:T(128)} %bitcast.owner_ref, s32[128]{0:T(128)S(1)} %copy-done.1, s32[128]{0:T(128)S(1)} %copy-done.2, bf16[2,704,768]{2,1,0:T(8,128)(2,1)S(1)} %get-tuple-element.20.shifted_ref, f32[2,512,80]{2,1,0:T(8,128)S(1)} %get-tuple-element.26.packed_ref, ...), custom_call_target="tpu_custom_call" | custom-call | tf_op jit(solution)/shard_map/pallas_call | solution.py:291
  92.8 0.0 collective-permute-done.8.received_hbm
  92.8 0.6 shard_map.70
  (2 shorter events, 0.0 us)
Async XLA Ops:
  0.0 0.9 copy-start
  0.9 41.9 %copy-start.1 = (s32[128]{0:T(128)S(1)}, s32[128]{0:T(128)}, u32[]{:S(2)}) copy-start(s32[128]{0:T(128)} %order_ref.5) | copy-start | bytes 1540
  1.7 21.6 %all-to-all-start = ((bf16[8,112,128]{2,1,0:T(8,128)(2,1)}), bf16[8,112,128]{2,1,0:T(8,128)(2,1)}, u32[]{:S(2)}, u32[]{:S(2)}) async-start(bf16[8,112,128]{2,1,0:T(8,128)(2,1)} %shard_map.64), calls=%async_computation | async-start | bytes 458752 | tf_op jit(solution)/shard_map/all_to_all | solution.py:231
  12.0 64.7 %copy-start.2 = (s32[128]{0:T(128)S(1)}, s32[128]{0:T(128)}, u32[]{:S(2)}) copy-start(s32[128]{0:T(128)} %len_ref.5) | copy-start | bytes 1540
  23.3 19.5 %all-to-all-start.1 = ((bf16[8,16,1280]{2,1,0:T(8,128)(2,1)}), bf16[8,16,1280]{2,1,0:T(8,128)(2,1)S(1)}, u32[]{:S(2)}, u32[]{:S(2)}) async-start(bf16[8,16,1280]{2,1,0:T(8,128)(2,1)} %shard_map.65), calls=%async_computation.1 | async-start | bytes 655360 | tf_op jit(solution)/shard_map/all_to_all | solution.py:248
  28.1 16.6 %collective-permute-start = (bf16[8,112,128]{2,1,0:T(8,128)(2,1)}, bf16[8,112,128]{2,1,0:T(8,128)(2,1)S(1)}, u32[]{:S(2)}, u32[]{:S(2)}) collective-permute-start(bf16[8,112,128]{2,1,0:T(8,128)(2,1)} %all-to-all-done.refs_0_), channel_id=1, source_target_pairs={{0,64},{8,72},{16,80},{24,88},{32,96},{40,104},{48,112},{56,120},{... | collective-permute-start | bytes 688136 | tf_op jit(solution)/shard_map/ppermute | solution.py:206
  31.6 13.2 %collective-permute-start.1 = (bf16[8,112,128]{2,1,0:T(8,128)(2,1)}, bf16[8,112,128]{2,1,0:T(8,128)(2,1)S(1)}, u32[]{:S(2)}, u32[]{:S(2)}) collective-permute-start(bf16[8,112,128]{2,1,0:T(8,128)(2,1)} %all-to-all-done.refs_0_), channel_id=1, source_target_pairs={{0,448},{8,456},{16,464},{24,472},{32,480},{40,488},{48,496},{56,5... | collective-permute-start | bytes 688136 | tf_op jit(solution)/shard_map/ppermute | solution.py:206
  34.0 15.3 %collective-permute-start.2 = (bf16[8,112,128]{2,1,0:T(8,128)(2,1)}, bf16[8,112,128]{2,1,0:T(8,128)(2,1)S(1)}, u32[]{:S(2)}, u32[]{:S(2)}) collective-permute-start(bf16[8,112,128]{2,1,0:T(8,128)(2,1)} %all-to-all-done.refs_0_), channel_id=1, source_target_pairs={{0,128},{8,136},{16,144},{24,152},{32,160},{40,168},{48,176},{56,1... | collective-permute-start | bytes 688136 | tf_op jit(solution)/shard_map/ppermute | solution.py:206
  40.9 14.0 %collective-permute-start.3 = (bf16[8,112,128]{2,1,0:T(8,128)(2,1)}, bf16[8,112,128]{2,1,0:T(8,128)(2,1)S(1)}, u32[]{:S(2)}, u32[]{:S(2)}) collective-permute-start(bf16[8,112,128]{2,1,0:T(8,128)(2,1)} %all-to-all-done.refs_0_), channel_id=1, source_target_pairs={{0,384},{8,392},{16,400},{24,408},{32,416},{40,424},{48,432},{56,4... | collective-permute-start | bytes 688136 | tf_op jit(solution)/shard_map/ppermute | solution.py:206
  54.9 21.8 %all-to-all-start.2 = ((bf16[64,8,320]{2,1,0:T(8,128)(2,1)}), bf16[64,8,320]{2,1,0:T(8,128)(2,1)S(1)}, u32[]{:S(2)}, u32[]{:S(2)}) async-start(bf16[64,8,320]{2,1,0:T(8,128)(2,1)} %bitcast.4), calls=%async_computation.2 | async-start | bytes 786432 | tf_op jit(solution)/shard_map/all_to_all | solution.py:261
  60.6 22.3 %collective-permute-start.4 = (bf16[8,112,128]{2,1,0:T(8,128)(2,1)S(1)}, bf16[8,112,128]{2,1,0:T(8,128)(2,1)S(1)}, u32[]{:S(2)}, u32[]{:S(2)}) collective-permute-start(bf16[8,112,128]{2,1,0:T(8,128)(2,1)S(1)} %collective-permute-done.2.refs_2_), channel_id=1, source_target_pairs={{0,64},{8,72},{16,80},{24,88},{32,96},{40,104},{48,112},{56,120},{... | collective-permute-start | bytes 688136 | tf_op jit(solution)/shard_map/ppermute | solution.py:206
  64.0 18.9 %collective-permute-start.7 = (bf16[8,112,128]{2,1,0:T(8,128)(2,1)S(1)}, bf16[8,112,128]{2,1,0:T(8,128)(2,1)S(1)}, u32[]{:S(2)}, u32[]{:S(2)}) collective-permute-start(bf16[8,112,128]{2,1,0:T(8,128)(2,1)S(1)} %collective-permute-done.3.refs_7_), channel_id=1, source_target_pairs={{0,448},{8,456},{16,464},{24,472},{32,480},{40,488},{48,496},{56,5... | collective-permute-start | bytes 688136 | tf_op jit(solution)/shard_map/ppermute | solution.py:206
  66.5 12.3 %collective-permute-start.5 = (bf16[4,112,128]{2,1,0:T(8,128)(2,1)S(1)}, bf16[4,112,128]{2,1,0:T(8,128)(2,1)S(1)}, u32[]{:S(2)}, u32[]{:S(2)}) collective-permute-start(bf16[4,112,128]{2,1,0:T(8,128)(2,1)S(1)} %slice.6), channel_id=1, source_target_pairs={{0,128},{8,136},{16,144},{24,152},{32,160},{40,168},{48,176},{56,1... | collective-permute-start | bytes 344072 | tf_op jit(solution)/shard_map/ppermute | solution.py:206
  73.2 9.6 %collective-permute-start.6 = (bf16[4,112,128]{2,1,0:T(8,128)(2,1)S(1)}, bf16[4,112,128]{2,1,0:T(8,128)(2,1)S(1)}, u32[]{:S(2)}, u32[]{:S(2)}) collective-permute-start(bf16[4,112,128]{2,1,0:T(8,128)(2,1)S(1)} %slice.7), channel_id=1, source_target_pairs={{0,384},{8,392},{16,400},{24,408},{32,416},{40,424},{48,432},{56,4... | collective-permute-start | bytes 344072 | tf_op jit(solution)/shard_map/ppermute | solution.py:206
  86.1 6.7 %collective-permute-start.8 = (bf16[80,512]{1,0:T(8,128)(2,1)S(1)}, bf16[80,512]{1,0:T(8,128)(2,1)S(1)}, u32[]{:S(2)}, u32[]{:S(2)}) collective-permute-start(bf16[80,512]{1,0:T(8,128)(2,1)S(1)} %shard_map.68), channel_id=1, source_target_pairs={{0,8},{8,0},{16,24},{24,16},{32,40},{40,32},{48,56},{56,48},{64,72... | collective-permute-start | bytes 245768 | tf_op jit(solution)/shard_map/ppermute | solution.py:290

commit v2 on v1

--- a/solution.py
+++ b/solution.py
@@ -244,7 +244,7 @@
         compiler_params=pltpu.CompilerParams(vmem_limit_bytes=66900000),
     )(features.reshape(utts * slice_rows, channels), conv_weight, proj_weight)
     taps, sent = lax.optimization_barrier((taps, sent))
-    one, minus_one, two, minus_two = [send(taps, ring, step) for step in (1, -1, 2, -2)]
+    one, minus_one = send(taps, ring, 1), send(taps, ring, -1)
     spread = lax.all_to_all(sent, "mp", split_axis=0, concat_axis=0, tiled=True)
 
     ordered = pl.pallas_call(
@@ -254,9 +254,11 @@
         out_specs=VMEM,
         compiler_params=params,
     )(pack_order.reshape(1, -1), spread.reshape(parts * utts, frames * width))
-    one, minus_one, two, minus_two, ordered = lax.optimization_barrier((one, minus_one, two, minus_two, ordered))
-    three, minus_three = send(two, ring, 1), send(minus_two, ring, -1)
-    low, high = send(two[: ring // 2], ring, 2), send(minus_two[ring // 2 :], ring, -2)
+    low, high = one[: ring // 2], minus_one[ring // 2 :]
+    low, high, one, minus_one, ordered = lax.optimization_barrier((low, high, one, minus_one, ordered))
+    low, high = send(low, ring, 3), send(high, ring, -3)
+    three, minus_three = send(one, ring, 2), send(minus_one, ring, -2)
+    two, minus_two = send(one, ring, 1), send(minus_one, ring, -1)
     taps = (taps, one, two, three, low, high, minus_three, minus_two, minus_one)
     pair_rows = lax.all_to_all(
         ordered.reshape(owners, 8, 2 * width), "dp", split_axis=0, concat_axis=0, tiled=True

time: 94.2 us -> 102 us (1.083)
  the two profiles are of different devices: /device:TPU:18 before, /device:TPU:40 now
where the time goes in v2:
time: 102 us; the launch traced here: 101 us
  starting transfers between devices  54.2 us (53%)
  waiting for transfers between devices  30.1 us (30%)
  Pallas kernels  15.7 us (15%)
    ppermute x8, starting transfers between devices, send(): lax.ppermute(values, 'dp', [(o, (o + step * ring) % (ring * ring)) for o...  27.2 us
    ppermute x8, waiting for transfers between devices, send(): lax.ppermute(values, 'dp', [(o, (o + step * ring) % (ring * ring)) for o...  22.1 us
    all_to_all x1, starting transfers between devices, shards(): lax.all_to_all(tap_copies, 'dp', 0, 0, axis_index_groups=along_z, tiled=T...  10.4 us
    all_to_all x1, starting transfers between devices, shards(): lax.all_to_all(ordered.reshape(owners, 8, 2 * width), 'dp', split_axis=0,...  8.9 us
    all_to_all x1, waiting for transfers between devices, shards(): lax.all_to_all(tap_copies, 'dp', 0, 0, axis_index_groups=along_z, tiled=T...  8.05 us
    all_to_all x1, starting transfers between devices, shards(): spread = lax.all_to_all(sent, 'mp', split_axis=0, concat_axis=0, tiled=True)  4.3 us
    pallas_call x1, Pallas kernels, shards(): own = convolve(False)(*scalars, shifted, packed, *taps)  3.92 us
    ppermute x1, starting transfers between devices, shards(): received = lax.ppermute(other, 'dp', [(o, o ^ 1) for o in range(owners)])  3.38 us
  transfers between devices with their start and end apart: 12, of which 5 were waited for; matrix products, arithmetic and copies ran while one was open for 0% of the time, Pallas kernels for 9%

profile of v2, /device:TPU:40, one launch (start us, length us, event | category | flops | bytes accessed | tf_op | source)
XLA Modules:
  0.0 101.1 jit_solution(11025596696745783593)
XLA Ops:
  0.0 0.0 copy-start
  0.0 0.9 copy-done
  0.9 0.8 shard_map.64
  1.7 0.0 copy-start.1
  1.7 10.4 %all-to-all-start = ((bf16[8,112,128]{2,1,0:T(8,128)(2,1)}), bf16[8,112,128]{2,1,0:T(8,128)(2,1)}, u32[]{:S(2)}, u32[]{:S(2)}) async-start(bf16[8,112,128]{2,1,0:T(8,128)(2,1)} %shard_map.64), calls=%async_computation | async-start | bytes 458752 | tf_op jit(solution)/shard_map/all_to_all | solution.py:231
  12.1 0.0 copy-start.2
  12.1 3.2 %shard_map.65 = bf16[8,16,1280]{2,1,0:T(8,128)(2,1)} custom-call(bf16[256,512]{1,0:T(8,128)(2,1)} %bitcast.10, bf16[2,512,512]{2,1,0:T(8,128)(2,1)} %conv_hbm.1, bf16[512,1280]{1,0:T(8,128)(2,1)} %proj_hbm.1), custom_call_target="tpu_custom_call" | custom-call | tf_op jit(solution)/shard_map/pallas_call | solution.py:233
  15.4 8.1 %all-to-all-done.refs_0_ = bf16[8,112,128]{2,1,0:T(8,128)(2,1)} async-done(((bf16[8,112,128]{2,1,0:T(8,128)(2,1)}), bf16[8,112,128]{2,1,0:T(8,128)(2,1)}, u32[]{:S(2)}, u32[]{:S(2)}) %all-to-all-start) | async-done | bytes 229408 | tf_op jit(solution)/shard_map/all_to_all | solution.py:231
  23.4 4.3 %all-to-all-start.1 = ((bf16[8,16,1280]{2,1,0:T(8,128)(2,1)}), bf16[8,16,1280]{2,1,0:T(8,128)(2,1)S(1)}, u32[]{:S(2)}, u32[]{:S(2)}) async-start(bf16[8,16,1280]{2,1,0:T(8,128)(2,1)} %shard_map.65), calls=%async_computation.1 | async-start | bytes 655360 | tf_op jit(solution)/shard_map/all_to_all | solution.py:248
  27.7 2.6 %collective-permute-start = (bf16[8,112,128]{2,1,0:T(8,128)(2,1)}, bf16[8,112,128]{2,1,0:T(8,128)(2,1)S(1)}, u32[]{:S(2)}, u32[]{:S(2)}) collective-permute-start(bf16[8,112,128]{2,1,0:T(8,128)(2,1)} %all-to-all-done.refs_0_), channel_id=1, source_target_pairs={{0,64},{8,72},{16,80},{24,88},{32,96},{40,104},{48,112},{56,120},{... | collective-permute-start | bytes 688136 | tf_op jit(solution)/shard_map/ppermute | solution.py:206
  30.3 3.3 %collective-permute-start.1 = (bf16[8,112,128]{2,1,0:T(8,128)(2,1)}, bf16[8,112,128]{2,1,0:T(8,128)(2,1)S(1)}, u32[]{:S(2)}, u32[]{:S(2)}) collective-permute-start(bf16[8,112,128]{2,1,0:T(8,128)(2,1)} %all-to-all-done.refs_0_), channel_id=1, source_target_pairs={{0,448},{8,456},{16,464},{24,472},{32,480},{40,488},{48,496},{56,5... | collective-permute-start | bytes 688136 | tf_op jit(solution)/shard_map/ppermute | solution.py:206
  33.6 4.3 %collective-permute-done.refs_1_ = bf16[8,112,128]{2,1,0:T(8,128)(2,1)S(1)} collective-permute-done((bf16[8,112,128]{2,1,0:T(8,128)(2,1)}, bf16[8,112,128]{2,1,0:T(8,128)(2,1)S(1)}, u32[]{:S(2)}, u32[]{:S(2)}) %collective-permute-start) | collective-permute-done | bytes 229408 | tf_op jit(solution)/shard_map/ppermute | solution.py:206
  37.8 2.3 %collective-permute-done.1.refs_8_ = bf16[8,112,128]{2,1,0:T(8,128)(2,1)S(1)} collective-permute-done((bf16[8,112,128]{2,1,0:T(8,128)(2,1)}, bf16[8,112,128]{2,1,0:T(8,128)(2,1)S(1)}, u32[]{:S(2)}, u32[]{:S(2)}) %collective-permute-start.1) | collective-permute-done | bytes 229408 | tf_op jit(solution)/shard_map/ppermute | solution.py:206
  40.1 0.0 all-to-all-done.1
  40.1 0.0 copy-done.1
  40.2 1.9 %shard_map.66 = bf16[512,320]{1,0:T(8,128)(2,1)} custom-call(s32[1,128]{1,0:T(1,128)S(1)} %bitcast.9, bf16[128,1280]{1,0:T(8,128)(2,1)S(1)} %bitcast.8), custom_call_target="tpu_custom_call" | custom-call | tf_op jit(solution)/shard_map/pallas_call | solution.py:250
  42.1 8.9 %all-to-all-start.2 = ((bf16[64,8,320]{2,1,0:T(8,128)(2,1)}), bf16[64,8,320]{2,1,0:T(8,128)(2,1)S(1)}, u32[]{:S(2)}, u32[]{:S(2)}) async-start(bf16[64,8,320]{2,1,0:T(8,128)(2,1)} %bitcast.4), calls=%async_computation.2 | async-start | bytes 786432 | tf_op jit(solution)/shard_map/all_to_all | solution.py:263
  51.0 2.2 %collective-permute-start.4 = (bf16[4,112,128]{2,1,0:T(8,128)(2,1)S(1)}, bf16[4,112,128]{2,1,0:T(8,128)(2,1)S(1)}, u32[]{:S(2)}, u32[]{:S(2)}) collective-permute-start(bf16[4,112,128]{2,1,0:T(8,128)(2,1)S(1)} %slice.8), channel_id=1, source_target_pairs={{0,192},{8,200},{16,208},{24,216},{32,224},{40,232},{48,240},{56,2... | collective-permute-start | bytes 344072 | tf_op jit(solution)/shard_map/ppermute | solution.py:206
  53.2 3.5 %collective-permute-start.2 = (bf16[8,112,128]{2,1,0:T(8,128)(2,1)S(1)}, bf16[8,112,128]{2,1,0:T(8,128)(2,1)S(1)}, u32[]{:S(2)}, u32[]{:S(2)}) collective-permute-start(bf16[8,112,128]{2,1,0:T(8,128)(2,1)S(1)} %collective-permute-done.refs_1_), channel_id=1, source_target_pairs={{0,64},{8,72},{16,80},{24,88},{32,96},{40,104},{48,112},{56,120},{... | collective-permute-start | bytes 688136 | tf_op jit(solution)/shard_map/ppermute | solution.py:206
  56.7 4.3 %collective-permute-start.3 = (bf16[8,112,128]{2,1,0:T(8,128)(2,1)S(1)}, bf16[8,112,128]{2,1,0:T(8,128)(2,1)S(1)}, u32[]{:S(2)}, u32[]{:S(2)}) collective-permute-start(bf16[8,112,128]{2,1,0:T(8,128)(2,1)S(1)} %collective-permute-done.refs_1_), channel_id=1, source_target_pairs={{0,128},{8,136},{16,144},{24,152},{32,160},{40,168},{48,176},{56,1... | collective-permute-start | bytes 688136 | tf_op jit(solution)/shard_map/ppermute | solution.py:206
  61.0 3.6 %collective-permute-start.6 = (bf16[8,112,128]{2,1,0:T(8,128)(2,1)S(1)}, bf16[8,112,128]{2,1,0:T(8,128)(2,1)S(1)}, u32[]{:S(2)}, u32[]{:S(2)}) collective-permute-start(bf16[8,112,128]{2,1,0:T(8,128)(2,1)S(1)} %collective-permute-done.1.refs_8_), channel_id=1, source_target_pairs={{0,384},{8,392},{16,400},{24,408},{32,416},{40,424},{48,432},{56,4... | collective-permute-start | bytes 688136 | tf_op jit(solution)/shard_map/ppermute | solution.py:206
  64.7 2.4 %collective-permute-start.7 = (bf16[8,112,128]{2,1,0:T(8,128)(2,1)S(1)}, bf16[8,112,128]{2,1,0:T(8,128)(2,1)S(1)}, u32[]{:S(2)}, u32[]{:S(2)}) collective-permute-start(bf16[8,112,128]{2,1,0:T(8,128)(2,1)S(1)} %collective-permute-done.1.refs_8_), channel_id=1, source_target_pairs={{0,448},{8,456},{16,464},{24,472},{32,480},{40,488},{48,496},{56,5... | collective-permute-start | bytes 688136 | tf_op jit(solution)/shard_map/ppermute | solution.py:206
  67.0 1.3 %collective-permute-done.4.refs_4_ = bf16[4,112,128]{2,1,0:T(8,128)(2,1)S(1)} collective-permute-done((bf16[4,112,128]{2,1,0:T(8,128)(2,1)S(1)}, bf16[4,112,128]{2,1,0:T(8,128)(2,1)S(1)}, u32[]{:S(2)}, u32[]{:S(2)}) %collective-permute-start.4) | collective-permute-done | bytes 114720 | tf_op jit(solution)/shard_map/ppermute | solution.py:206
  68.4 5.3 %collective-permute-start.5 = (bf16[4,112,128]{2,1,0:T(8,128)(2,1)S(1)}, bf16[4,112,128]{2,1,0:T(8,128)(2,1)S(1)}, u32[]{:S(2)}, u32[]{:S(2)}) collective-permute-start(bf16[4,112,128]{2,1,0:T(8,128)(2,1)S(1)} %slice.9), channel_id=1, source_target_pairs={{0,320},{8,328},{16,336},{24,344},{32,352},{40,360},{48,368},{56,3... | collective-permute-start | bytes 344072 | tf_op jit(solution)/shard_map/ppermute | solution.py:206
  73.7 0.0 all-to-all-done.2
  73.7 0.0 copy-done.2
  73.7 2.0 %shard_map.67 = (bf16[2,704,768]{2,1,0:T(8,128)(2,1)S(1)}, f32[2,512,80]{2,1,0:T(8,128)S(1)}) custom-call(s32[1]{0:T(128)} %bitcast.owner_ref, s32[128]{0:T(128)S(1)} %copy-done.1, s32[128]{0:T(128)S(1)} %copy-done.2, bf16[512,320]{1,0:T(8,128)(2,1)S(1)} %bitcast.7), custom_call_target="tpu_custom_call" | custom-call | tf_op jit(solution)/shard_map/pallas_call | solution.py:271
  75.7 14.2 %collective-permute-done.5.refs_5_ = bf16[4,112,128]{2,1,0:T(8,128)(2,1)S(1)} collective-permute-done((bf16[4,112,128]{2,1,0:T(8,128)(2,1)S(1)}, bf16[4,112,128]{2,1,0:T(8,128)(2,1)S(1)}, u32[]{:S(2)}, u32[]{:S(2)}) %collective-permute-start.5) | collective-permute-done | bytes 114720 | tf_op jit(solution)/shard_map/ppermute | solution.py:206
  89.9 0.0 collective-permute-done.2.refs_2_
  89.9 0.0 collective-permute-done.3.refs_3_
  89.9 0.0 collective-permute-done.6.refs_6_
  89.9 0.0 collective-permute-done.7.refs_7_
  89.9 3.2 %shard_map.68 = bf16[80,512]{1,0:T(8,128)(2,1)S(1)} custom-call(s32[1]{0:T(128)} %bitcast.owner_ref, s32[128]{0:T(128)S(1)} %copy-done.1, s32[128]{0:T(128)S(1)} %copy-done.2, bf16[2,704,768]{2,1,0:T(8,128)(2,1)S(1)} %get-tuple-element.20.shifted_ref, f32[2,512,80]{2,1,0:T(8,128)S(1)} %get-tuple-element.26.packed_ref, ...), custom_call_target="tpu_custom_call" | custom-call | tf_op jit(solution)/shard_map/pallas_call | solution.py:290
  93.2 3.4 %collective-permute-start.8 = (bf16[80,512]{1,0:T(8,128)(2,1)S(1)}, bf16[80,512]{1,0:T(8,128)(2,1)S(1)}, u32[]{:S(2)}, u32[]{:S(2)}) collective-permute-start(bf16[80,512]{1,0:T(8,128)(2,1)S(1)} %shard_map.68), channel_id=1, source_target_pairs={{0,8},{8,0},{16,24},{24,16},{32,40},{40,32},{48,56},{56,48},{64,72... | collective-permute-start | bytes 245768 | tf_op jit(solution)/shard_map/ppermute | solution.py:292
  96.6 3.9 %shard_map.69.own_hbm = bf16[160,512]{1,0:T(8,128)(2,1)} custom-call(s32[1]{0:T(128)} %bitcast.owner_ref, s32[128]{0:T(128)S(1)} %copy-done.1, s32[128]{0:T(128)S(1)} %copy-done.2, bf16[2,704,768]{2,1,0:T(8,128)(2,1)S(1)} %get-tuple-element.20.shifted_ref, f32[2,512,80]{2,1,0:T(8,128)S(1)} %get-tuple-element.26.packed_ref, ...), custom_call_target="tpu_custom_call" | custom-call | tf_op jit(solution)/shard_map/pallas_call | solution.py:293
  100.5 0.0 collective-permute-done.8.received_hbm
  100.5 0.6 shard_map.70
  (2 shorter events, 0.0 us)
Async XLA Ops:
  0.0 0.9 copy-start
  1.7 38.5 %copy-start.1 = (s32[128]{0:T(128)S(1)}, s32[128]{0:T(128)}, u32[]{:S(2)}) copy-start(s32[128]{0:T(128)} %order_ref.5) | copy-start | bytes 1540
  1.7 21.7 %all-to-all-start = ((bf16[8,112,128]{2,1,0:T(8,128)(2,1)}), bf16[8,112,128]{2,1,0:T(8,128)(2,1)}, u32[]{:S(2)}, u32[]{:S(2)}) async-start(bf16[8,112,128]{2,1,0:T(8,128)(2,1)} %shard_map.64), calls=%async_computation | async-start | bytes 458752 | tf_op jit(solution)/shard_map/all_to_all | solution.py:231
  12.1 61.6 %copy-start.2 = (s32[128]{0:T(128)S(1)}, s32[128]{0:T(128)}, u32[]{:S(2)}) copy-start(s32[128]{0:T(128)} %len_ref.5) | copy-start | bytes 1540
  23.4 16.7 %all-to-all-start.1 = ((bf16[8,16,1280]{2,1,0:T(8,128)(2,1)}), bf16[8,16,1280]{2,1,0:T(8,128)(2,1)S(1)}, u32[]{:S(2)}, u32[]{:S(2)}) async-start(bf16[8,16,1280]{2,1,0:T(8,128)(2,1)} %shard_map.65), calls=%async_computation.1 | async-start | bytes 655360 | tf_op jit(solution)/shard_map/all_to_all | solution.py:248
  27.7 10.1 %collective-permute-start = (bf16[8,112,128]{2,1,0:T(8,128)(2,1)}, bf16[8,112,128]{2,1,0:T(8,128)(2,1)S(1)}, u32[]{:S(2)}, u32[]{:S(2)}) collective-permute-start(bf16[8,112,128]{2,1,0:T(8,128)(2,1)} %all-to-all-done.refs_0_), channel_id=1, source_target_pairs={{0,64},{8,72},{16,80},{24,88},{32,96},{40,104},{48,112},{56,120},{... | collective-permute-start | bytes 688136 | tf_op jit(solution)/shard_map/ppermute | solution.py:206
  30.3 9.8 %collective-permute-start.1 = (bf16[8,112,128]{2,1,0:T(8,128)(2,1)}, bf16[8,112,128]{2,1,0:T(8,128)(2,1)S(1)}, u32[]{:S(2)}, u32[]{:S(2)}) collective-permute-start(bf16[8,112,128]{2,1,0:T(8,128)(2,1)} %all-to-all-done.refs_0_), channel_id=1, source_target_pairs={{0,448},{8,456},{16,464},{24,472},{32,480},{40,488},{48,496},{56,5... | collective-permute-start | bytes 688136 | tf_op jit(solution)/shard_map/ppermute | solution.py:206
  42.1 31.6 %all-to-all-start.2 = ((bf16[64,8,320]{2,1,0:T(8,128)(2,1)}), bf16[64,8,320]{2,1,0:T(8,128)(2,1)S(1)}, u32[]{:S(2)}, u32[]{:S(2)}) async-start(bf16[64,8,320]{2,1,0:T(8,128)(2,1)} %bitcast.4), calls=%async_computation.2 | async-start | bytes 786432 | tf_op jit(solution)/shard_map/all_to_all | solution.py:263
  51.0 17.4 %collective-permute-start.4 = (bf16[4,112,128]{2,1,0:T(8,128)(2,1)S(1)}, bf16[4,112,128]{2,1,0:T(8,128)(2,1)S(1)}, u32[]{:S(2)}, u32[]{:S(2)}) collective-permute-start(bf16[4,112,128]{2,1,0:T(8,128)(2,1)S(1)} %slice.8), channel_id=1, source_target_pairs={{0,192},{8,200},{16,208},{24,216},{32,224},{40,232},{48,240},{56,2... | collective-permute-start | bytes 344072 | tf_op jit(solution)/shard_map/ppermute | solution.py:206
  53.2 36.7 %collective-permute-start.2 = (bf16[8,112,128]{2,1,0:T(8,128)(2,1)S(1)}, bf16[8,112,128]{2,1,0:T(8,128)(2,1)S(1)}, u32[]{:S(2)}, u32[]{:S(2)}) collective-permute-start(bf16[8,112,128]{2,1,0:T(8,128)(2,1)S(1)} %collective-permute-done.refs_1_), channel_id=1, source_target_pairs={{0,64},{8,72},{16,80},{24,88},{32,96},{40,104},{48,112},{56,120},{... | collective-permute-start | bytes 688136 | tf_op jit(solution)/shard_map/ppermute | solution.py:206
  56.7 33.2 %collective-permute-start.3 = (bf16[8,112,128]{2,1,0:T(8,128)(2,1)S(1)}, bf16[8,112,128]{2,1,0:T(8,128)(2,1)S(1)}, u32[]{:S(2)}, u32[]{:S(2)}) collective-permute-start(bf16[8,112,128]{2,1,0:T(8,128)(2,1)S(1)} %collective-permute-done.refs_1_), channel_id=1, source_target_pairs={{0,128},{8,136},{16,144},{24,152},{32,160},{40,168},{48,176},{56,1... | collective-permute-start | bytes 688136 | tf_op jit(solution)/shard_map/ppermute | solution.py:206
  61.0 28.9 %collective-permute-start.6 = (bf16[8,112,128]{2,1,0:T(8,128)(2,1)S(1)}, bf16[8,112,128]{2,1,0:T(8,128)(2,1)S(1)}, u32[]{:S(2)}, u32[]{:S(2)}) collective-permute-start(bf16[8,112,128]{2,1,0:T(8,128)(2,1)S(1)} %collective-permute-done.1.refs_8_), channel_id=1, source_target_pairs={{0,384},{8,392},{16,400},{24,408},{32,416},{40,424},{48,432},{56,4... | collective-permute-start | bytes 688136 | tf_op jit(solution)/shard_map/ppermute | solution.py:206
  64.7 25.3 %collective-permute-start.7 = (bf16[8,112,128]{2,1,0:T(8,128)(2,1)S(1)}, bf16[8,112,128]{2,1,0:T(8,128)(2,1)S(1)}, u32[]{:S(2)}, u32[]{:S(2)}) collective-permute-start(bf16[8,112,128]{2,1,0:T(8,128)(2,1)S(1)} %collective-permute-done.1.refs_8_), channel_id=1, source_target_pairs={{0,448},{8,456},{16,464},{24,472},{32,480},{40,488},{48,496},{56,5... | collective-permute-start | bytes 688136 | tf_op jit(solution)/shard_map/ppermute | solution.py:206
  68.4 21.5 %collective-permute-start.5 = (bf16[4,112,128]{2,1,0:T(8,128)(2,1)S(1)}, bf16[4,112,128]{2,1,0:T(8,128)(2,1)S(1)}, u32[]{:S(2)}, u32[]{:S(2)}) collective-permute-start(bf16[4,112,128]{2,1,0:T(8,128)(2,1)S(1)} %slice.9), channel_id=1, source_target_pairs={{0,320},{8,328},{16,336},{24,344},{32,352},{40,360},{48,368},{56,3... | collective-permute-start | bytes 344072 | tf_op jit(solution)/shard_map/ppermute | solution.py:206
  93.2 7.3 %collective-permute-start.8 = (bf16[80,512]{1,0:T(8,128)(2,1)S(1)}, bf16[80,512]{1,0:T(8,128)(2,1)S(1)}, u32[]{:S(2)}, u32[]{:S(2)}) collective-permute-start(bf16[80,512]{1,0:T(8,128)(2,1)S(1)} %shard_map.68), channel_id=1, source_target_pairs={{0,8},{8,0},{16,24},{24,16},{32,40},{40,32},{48,56},{56,48},{64,72... | collective-permute-start | bytes 245768 | tf_op jit(solution)/shard_map/ppermute | solution.py:292

commit v3 on v1

--- a/solution.py
+++ b/solution.py
@@ -10,7 +10,7 @@
 HOP = 320
 EPS = 1e-05
 LANES = 128
-TAP_ROWS = 112
+TAP_ROWS = 104
 GAP = 64
 STEP = 16
 
@@ -41,17 +41,12 @@
 def pack_taps_kernel(taps_ref, out_ref):
     packed = []
     for g in range(2):
-        rest = taps_ref[1, g, :, 48:80]
-        packed.append(
-            jnp.concatenate(
-                [
-                    jnp.concatenate([taps_ref[0, g], taps_ref[1, g, :, 0:48]], axis=1),
-                    jnp.concatenate([rest[16 * r : 16 * r + 16] for r in range(4)], axis=1),
-                    jnp.concatenate([rest[64:80], jnp.zeros((16, 96), rest.dtype)], axis=1),
-                ],
-                axis=0,
-            )
-        )
+        first, second = taps_ref[0, g].astype(jnp.float32), taps_ref[1, g].astype(jnp.float32)
+        rest = second[:, 48:80]
+        blocks = [rest[8 * r : 8 * r + 8] for r in range(10)] + [jnp.zeros((8, 32), jnp.float32)] * 2
+        folded = [jnp.concatenate(blocks[4 * n : 4 * n + 4], axis=1) for n in range(3)]
+        wide = jnp.concatenate([first, second[:, 0:48]], axis=1)
+        packed.append(jnp.concatenate([wide] + folded, axis=0).astype(out_ref.dtype))
     for device in range(out_ref.shape[0]):
         out_ref[device] = packed[device % 2]
 
@@ -151,7 +146,7 @@
 def positional_kernel(
     swap, owner_ref, order_ref, len_ref, shifted_ref, packed_ref, *refs
 ):
-    taps_refs, (out_ref, sums) = refs[:-2], refs[-2:]
+    taps_refs, (out_ref, sums, result, sem) = refs[:-4], refs[-4:]
     parity = owner_ref[0] % 2
     which = 1 - parity if swap else parity
     ring = taps_refs[0].shape[0]
@@ -170,12 +165,12 @@
             taps_ref, piece = pieces[min(slot, 7)]
             size = 96 if slot % 3 == 2 else 80
             left.append(taps_ref[piece, 0:size, :])
-            fold = taps_ref[piece, 80:96, :]
-            right += [fold] + [jnp.roll(fold, -32 * r, axis=1) for r in range(1, 4)]
-            right.append(taps_ref[piece, 96:112, :])
+            fold = taps_ref[piece, 80:104, :].astype(jnp.float32)
+            turned = [fold] + [jnp.roll(fold, -32 * r, axis=1) for r in range(1, 4)]
+            right += [turned[r % 4][r // 4 * 8 : r // 4 * 8 + 8] for r in range(10)]
             if size == 96:
-                right.append(fold)
-        matrix = jnp.concatenate([jnp.concatenate(left, axis=0), jnp.concatenate(right, axis=0)], axis=1)
+                right += [fold[0:16]]
+        matrix = jnp.concatenate([jnp.concatenate(left, axis=0), jnp.concatenate(right, axis=0).astype(jnp.bfloat16)], axis=1)
         term = dot(shifted_ref[which, pl.ds(start, reach), :], matrix)
         sums[...] = term if away == 0 else sums[...] + term
 
@@ -185,8 +180,11 @@
     conv_sum = jnp.where(spot < first_len + second_len, jnp.where(spot < first_len, near, far), 0.0)
     hidden = packed_ref[which] + gelu(conv_sum)
     hidden = jnp.concatenate([hidden, jnp.zeros((total, -group % LANES), jnp.float32)], axis=1)
+    result[...] = hidden.T[:group].astype(result.dtype)
     start = 0 if swap else pl.multiple_of(parity * group, 16)
-    out_ref[pl.ds(start, group), :] = hidden.T[:group].astype(out_ref.dtype)
+    copy = pltpu.make_async_copy(result, out_ref.at[pl.ds(start, group), :], sem)
+    copy.start()
+    copy.wait()
 
 
 def join_kernel(owner_ref, received_hbm, own_hbm, out_hbm, sem):
@@ -281,8 +279,12 @@
         functools.partial(positional_kernel, swap),
         out_shape=jax.ShapeDtypeStruct((group if swap else width, total), jnp.bfloat16),
         in_specs=[SMEM, SMEM, SMEM, VMEM, VMEM] + [VMEM] * len(taps),
-        out_specs=VMEM,
-        scratch_shapes=[pltpu.VMEM((reach, 256), jnp.float32)],
+        out_specs=ANY,
+        scratch_shapes=[
+            pltpu.VMEM((reach, 256), jnp.float32),
+            pltpu.VMEM((group, total), jnp.bfloat16),
+            pltpu.SemaphoreType.DMA,
+        ],
         compiler_params=params,
     )
     other = convolve(True)(*scalars, shifted, packed, *taps)

time: 94.2 us -> 93.4 us (level)
  waiting for transfers between devices: 23.9 us -> 22.3 us
    ppermute x8, waiting for transfers between devices: 14.3 us -> 13.1 us  [send(): lax.ppermute(values, 'dp', [(o, (o + step * ring) % (ring * ring)) for o...]
where the time goes in v3:
time: 93.4 us; the launch traced here: 92.7 us
  starting transfers between devices  53.4 us (57%)
  waiting for transfers between devices  22.3 us (24%)
  Pallas kernels  15.9 us (17%)
    ppermute x8, starting transfers between devices, send(): lax.ppermute(values, 'dp', [(o, (o + step * ring) % (ring * ring)) for o...  29.2 us
    ppermute x8, waiting for transfers between devices, send(): lax.ppermute(values, 'dp', [(o, (o + step * ring) % (ring * ring)) for o...  13.1 us
    all_to_all x1, starting transfers between devices, shards(): lax.all_to_all(tap_copies, 'dp', 0, 0, axis_index_groups=along_z, tiled=T...  10.3 us
    all_to_all x1, waiting for transfers between devices, shards(): lax.all_to_all(tap_copies, 'dp', 0, 0, axis_index_groups=along_z, tiled=T...  7.7 us
    all_to_all x1, starting transfers between devices, shards(): lax.all_to_all(ordered.reshape(owners, 8, 2 * width), 'dp', split_axis=0,...  5.63 us
    all_to_all x1, starting transfers between devices, shards(): spread = lax.all_to_all(sent, 'mp', split_axis=0, concat_axis=0, tiled=True)  4.83 us
    pallas_call x1, Pallas kernels, shards(): own = convolve(False)(*scalars, shifted, packed, *taps)  3.92 us
    pallas_call x1, Pallas kernels, shards(): other = convolve(True)(*scalars, shifted, packed, *taps)  3.38 us
  transfers between devices with their start and end apart: 12, of which 5 were waited for; matrix products, arithmetic and copies ran while one was open for 0% of the time, Pallas kernels for 12%

profile of v3, /device:TPU:18, one launch (start us, length us, event | category | flops | bytes accessed | tf_op | source)
XLA Modules:
  0.0 92.7 jit_solution(12549107754851925262)
XLA Ops:
  0.0 0.0 copy-start
  0.0 0.9 copy-done
  0.9 0.0 copy-start.1
  0.9 0.8 shard_map.64
  1.7 10.3 %all-to-all-start = ((bf16[8,104,128]{2,1,0:T(8,128)(2,1)}), bf16[8,104,128]{2,1,0:T(8,128)(2,1)}, u32[]{:S(2)}, u32[]{:S(2)}) async-start(bf16[8,104,128]{2,1,0:T(8,128)(2,1)} %shard_map.64), calls=%async_computation | async-start | bytes 425984 | tf_op jit(solution)/shard_map/all_to_all | solution.py:229
  12.0 0.0 copy-start.2
  12.0 3.2 %shard_map.65 = bf16[8,16,1280]{2,1,0:T(8,128)(2,1)} custom-call(bf16[256,512]{1,0:T(8,128)(2,1)} %bitcast.10, bf16[2,512,512]{2,1,0:T(8,128)(2,1)} %conv_hbm.1, bf16[512,1280]{1,0:T(8,128)(2,1)} %proj_hbm.1), custom_call_target="tpu_custom_call" | custom-call | tf_op jit(solution)/shard_map/pallas_call | solution.py:231
  15.2 7.7 %all-to-all-done.refs_0_ = bf16[8,104,128]{2,1,0:T(8,128)(2,1)} async-done(((bf16[8,104,128]{2,1,0:T(8,128)(2,1)}), bf16[8,104,128]{2,1,0:T(8,128)(2,1)}, u32[]{:S(2)}, u32[]{:S(2)}) %all-to-all-start) | async-done | bytes 213024 | tf_op jit(solution)/shard_map/all_to_all | solution.py:229
  22.9 4.8 %all-to-all-start.1 = ((bf16[8,16,1280]{2,1,0:T(8,128)(2,1)}), bf16[8,16,1280]{2,1,0:T(8,128)(2,1)S(1)}, u32[]{:S(2)}, u32[]{:S(2)}) async-start(bf16[8,16,1280]{2,1,0:T(8,128)(2,1)} %shard_map.65), calls=%async_computation.1 | async-start | bytes 655360 | tf_op jit(solution)/shard_map/all_to_all | solution.py:246
  27.7 3.5 %collective-permute-start = (bf16[8,104,128]{2,1,0:T(8,128)(2,1)}, bf16[8,104,128]{2,1,0:T(8,128)(2,1)S(1)}, u32[]{:S(2)}, u32[]{:S(2)}) collective-permute-start(bf16[8,104,128]{2,1,0:T(8,128)(2,1)} %all-to-all-done.refs_0_), channel_id=1, source_target_pairs={{0,64},{8,72},{16,80},{24,88},{32,96},{40,104},{48,112},{56,120},{... | collective-permute-start | bytes 638984 | tf_op jit(solution)/shard_map/ppermute | solution.py:204
  31.2 2.4 %collective-permute-start.1 = (bf16[8,104,128]{2,1,0:T(8,128)(2,1)}, bf16[8,104,128]{2,1,0:T(8,128)(2,1)S(1)}, u32[]{:S(2)}, u32[]{:S(2)}) collective-permute-start(bf16[8,104,128]{2,1,0:T(8,128)(2,1)} %all-to-all-done.refs_0_), channel_id=1, source_target_pairs={{0,448},{8,456},{16,464},{24,472},{32,480},{40,488},{48,496},{56,5... | collective-permute-start | bytes 638984 | tf_op jit(solution)/shard_map/ppermute | solution.py:204
  33.6 6.9 %collective-permute-start.2 = (bf16[8,104,128]{2,1,0:T(8,128)(2,1)}, bf16[8,104,128]{2,1,0:T(8,128)(2,1)S(1)}, u32[]{:S(2)}, u32[]{:S(2)}) collective-permute-start(bf16[8,104,128]{2,1,0:T(8,128)(2,1)} %all-to-all-done.refs_0_), channel_id=1, source_target_pairs={{0,128},{8,136},{16,144},{24,152},{32,160},{40,168},{48,176},{56,1... | collective-permute-start | bytes 638984 | tf_op jit(solution)/shard_map/ppermute | solution.py:204
  40.5 1.9 %collective-permute-start.3 = (bf16[8,104,128]{2,1,0:T(8,128)(2,1)}, bf16[8,104,128]{2,1,0:T(8,128)(2,1)S(1)}, u32[]{:S(2)}, u32[]{:S(2)}) collective-permute-start(bf16[8,104,128]{2,1,0:T(8,128)(2,1)} %all-to-all-done.refs_0_), channel_id=1, source_target_pairs={{0,384},{8,392},{16,400},{24,408},{32,416},{40,424},{48,432},{56,4... | collective-permute-start | bytes 638984 | tf_op jit(solution)/shard_map/ppermute | solution.py:204
  42.4 0.0 all-to-all-done.1
  42.5 0.0 copy-done.1
  42.5 1.9 %shard_map.66 = bf16[512,320]{1,0:T(8,128)(2,1)} custom-call(s32[1,128]{1,0:T(1,128)S(1)} %bitcast.9, bf16[128,1280]{1,0:T(8,128)(2,1)S(1)} %bitcast.8), custom_call_target="tpu_custom_call" | custom-call | tf_op jit(solution)/shard_map/pallas_call | solution.py:248
  44.4 0.0 collective-permute-done.refs_1_
  44.4 0.0 collective-permute-done.1.refs_8_
  44.4 3.8 %collective-permute-done.2.refs_2_ = bf16[8,104,128]{2,1,0:T(8,128)(2,1)S(1)} collective-permute-done((bf16[8,104,128]{2,1,0:T(8,128)(2,1)}, bf16[8,104,128]{2,1,0:T(8,128)(2,1)S(1)}, u32[]{:S(2)}, u32[]{:S(2)}) %collective-permute-start.2) | collective-permute-done | bytes 213024 | tf_op jit(solution)/shard_map/ppermute | solution.py:204
  48.2 5.7 %collective-permute-done.3.refs_7_ = bf16[8,104,128]{2,1,0:T(8,128)(2,1)S(1)} collective-permute-done((bf16[8,104,128]{2,1,0:T(8,128)(2,1)}, bf16[8,104,128]{2,1,0:T(8,128)(2,1)S(1)}, u32[]{:S(2)}, u32[]{:S(2)}) %collective-permute-start.3) | collective-permute-done | bytes 213024 | tf_op jit(solution)/shard_map/ppermute | solution.py:204
  53.9 5.6 %all-to-all-start.2 = ((bf16[64,8,320]{2,1,0:T(8,128)(2,1)}), bf16[64,8,320]{2,1,0:T(8,128)(2,1)S(1)}, u32[]{:S(2)}, u32[]{:S(2)}) async-start(bf16[64,8,320]{2,1,0:T(8,128)(2,1)} %bitcast.4), calls=%async_computation.2 | async-start | bytes 786432 | tf_op jit(solution)/shard_map/all_to_all | solution.py:259
  59.5 3.4 %collective-permute-start.4 = (bf16[8,104,128]{2,1,0:T(8,128)(2,1)S(1)}, bf16[8,104,128]{2,1,0:T(8,128)(2,1)S(1)}, u32[]{:S(2)}, u32[]{:S(2)}) collective-permute-start(bf16[8,104,128]{2,1,0:T(8,128)(2,1)S(1)} %collective-permute-done.2.refs_2_), channel_id=1, source_target_pairs={{0,64},{8,72},{16,80},{24,88},{32,96},{40,104},{48,112},{56,120},{... | collective-permute-start | bytes 638984 | tf_op jit(solution)/shard_map/ppermute | solution.py:204
  62.9 2.4 %collective-permute-start.7 = (bf16[8,104,128]{2,1,0:T(8,128)(2,1)S(1)}, bf16[8,104,128]{2,1,0:T(8,128)(2,1)S(1)}, u32[]{:S(2)}, u32[]{:S(2)}) collective-permute-start(bf16[8,104,128]{2,1,0:T(8,128)(2,1)S(1)} %collective-permute-done.3.refs_7_), channel_id=1, source_target_pairs={{0,448},{8,456},{16,464},{24,472},{32,480},{40,488},{48,496},{56,5... | collective-permute-start | bytes 638984 | tf_op jit(solution)/shard_map/ppermute | solution.py:204
  65.4 6.8 %collective-permute-start.5 = (bf16[4,104,128]{2,1,0:T(8,128)(2,1)S(1)}, bf16[4,104,128]{2,1,0:T(8,128)(2,1)S(1)}, u32[]{:S(2)}, u32[]{:S(2)}) collective-permute-start(bf16[4,104,128]{2,1,0:T(8,128)(2,1)S(1)} %slice.6), channel_id=1, source_target_pairs={{0,128},{8,136},{16,144},{24,152},{32,160},{40,168},{48,176},{56,1... | collective-permute-start | bytes 319496 | tf_op jit(solution)/shard_map/ppermute | solution.py:204
  72.2 1.9 %collective-permute-start.6 = (bf16[4,104,128]{2,1,0:T(8,128)(2,1)S(1)}, bf16[4,104,128]{2,1,0:T(8,128)(2,1)S(1)}, u32[]{:S(2)}, u32[]{:S(2)}) collective-permute-start(bf16[4,104,128]{2,1,0:T(8,128)(2,1)S(1)} %slice.7), channel_id=1, source_target_pairs={{0,384},{8,392},{16,400},{24,408},{32,416},{40,424},{48,432},{56,4... | collective-permute-start | bytes 319496 | tf_op jit(solution)/shard_map/ppermute | solution.py:204
  74.1 1.5 %all-to-all-done.2 = bf16[64,8,320]{2,1,0:T(8,128)(2,1)S(1)} async-done(((bf16[64,8,320]{2,1,0:T(8,128)(2,1)}), bf16[64,8,320]{2,1,0:T(8,128)(2,1)S(1)}, u32[]{:S(2)}, u32[]{:S(2)}) %all-to-all-start.2) | async-done | bytes 327712 | tf_op jit(solution)/shard_map/all_to_all | solution.py:259
  75.7 0.0 copy-done.2
  75.7 2.0 %shard_map.67 = (bf16[2,704,768]{2,1,0:T(8,128)(2,1)S(1)}, f32[2,512,80]{2,1,0:T(8,128)S(1)}) custom-call(s32[1]{0:T(128)} %bitcast.owner_ref, s32[128]{0:T(128)S(1)} %copy-done.1, s32[128]{0:T(128)S(1)} %copy-done.2, bf16[512,320]{1,0:T(8,128)(2,1)S(1)} %bitcast.7), custom_call_target="tpu_custom_call" | custom-call | tf_op jit(solution)/shard_map/pallas_call | solution.py:267
  77.7 0.0 collective-permute-done.5.refs_4_
  77.7 3.6 %collective-permute-done.6.refs_5_ = bf16[4,104,128]{2,1,0:T(8,128)(2,1)S(1)} collective-permute-done((bf16[4,104,128]{2,1,0:T(8,128)(2,1)S(1)}, bf16[4,104,128]{2,1,0:T(8,128)(2,1)S(1)}, u32[]{:S(2)}, u32[]{:S(2)}) %collective-permute-start.6) | collective-permute-done | bytes 106528 | tf_op jit(solution)/shard_map/ppermute | solution.py:204
  81.3 0.0 collective-permute-done.4.refs_3_
  81.3 0.0 collective-permute-done.7.refs_6_
  81.3 3.4 %shard_map.68 = bf16[80,512]{1,0:T(8,128)(2,1)S(1)} custom-call(s32[1]{0:T(128)} %bitcast.owner_ref, s32[128]{0:T(128)S(1)} %copy-done.1, s32[128]{0:T(128)S(1)} %copy-done.2, bf16[2,704,768]{2,1,0:T(8,128)(2,1)S(1)} %get-tuple-element.20.shifted_ref, f32[2,512,80]{2,1,0:T(8,128)S(1)} %get-tuple-element.26.packed_ref, ...), custom_call_target="tpu_custom_call" | custom-call | tf_op jit(solution)/shard_map/pallas_call | solution.py:290
  84.7 3.4 %collective-permute-start.8 = (bf16[80,512]{1,0:T(8,128)(2,1)S(1)}, bf16[80,512]{1,0:T(8,128)(2,1)S(1)}, u32[]{:S(2)}, u32[]{:S(2)}) collective-permute-start(bf16[80,512]{1,0:T(8,128)(2,1)S(1)} %shard_map.68), channel_id=1, source_target_pairs={{0,8},{8,0},{16,24},{24,16},{32,40},{40,32},{48,56},{56,48},{64,72... | collective-permute-start | bytes 245768 | tf_op jit(solution)/shard_map/ppermute | solution.py:292
  88.1 3.9 %shard_map.69.own_hbm = bf16[160,512]{1,0:T(8,128)(2,1)} custom-call(s32[1]{0:T(128)} %bitcast.owner_ref, s32[128]{0:T(128)S(1)} %copy-done.1, s32[128]{0:T(128)S(1)} %copy-done.2, bf16[2,704,768]{2,1,0:T(8,128)(2,1)S(1)} %get-tuple-element.20.shifted_ref, f32[2,512,80]{2,1,0:T(8,128)S(1)} %get-tuple-element.26.packed_ref, ...), custom_call_target="tpu_custom_call" | custom-call | tf_op jit(solution)/shard_map/pallas_call | solution.py:293
  92.0 0.0 collective-permute-done.8.received_hbm
  92.0 0.7 shard_map.70
  (2 shorter events, 0.0 us)
Async XLA Ops:
  0.0 0.9 copy-start
  0.9 41.6 %copy-start.1 = (s32[128]{0:T(128)S(1)}, s32[128]{0:T(128)}, u32[]{:S(2)}) copy-start(s32[128]{0:T(128)} %order_ref.5) | copy-start | bytes 1540
  1.7 21.2 %all-to-all-start = ((bf16[8,104,128]{2,1,0:T(8,128)(2,1)}), bf16[8,104,128]{2,1,0:T(8,128)(2,1)}, u32[]{:S(2)}, u32[]{:S(2)}) async-start(bf16[8,104,128]{2,1,0:T(8,128)(2,1)} %shard_map.64), calls=%async_computation | async-start | bytes 425984 | tf_op jit(solution)/shard_map/all_to_all | solution.py:229
  12.0 63.7 %copy-start.2 = (s32[128]{0:T(128)S(1)}, s32[128]{0:T(128)}, u32[]{:S(2)}) copy-start(s32[128]{0:T(128)} %len_ref.5) | copy-start | bytes 1540
  22.9 19.5 %all-to-all-start.1 = ((bf16[8,16,1280]{2,1,0:T(8,128)(2,1)}), bf16[8,16,1280]{2,1,0:T(8,128)(2,1)S(1)}, u32[]{:S(2)}, u32[]{:S(2)}) async-start(bf16[8,16,1280]{2,1,0:T(8,128)(2,1)} %shard_map.65), calls=%async_computation.1 | async-start | bytes 655360 | tf_op jit(solution)/shard_map/all_to_all | solution.py:246
  27.7 16.7 %collective-permute-start = (bf16[8,104,128]{2,1,0:T(8,128)(2,1)}, bf16[8,104,128]{2,1,0:T(8,128)(2,1)S(1)}, u32[]{:S(2)}, u32[]{:S(2)}) collective-permute-start(bf16[8,104,128]{2,1,0:T(8,128)(2,1)} %all-to-all-done.refs_0_), channel_id=1, source_target_pairs={{0,64},{8,72},{16,80},{24,88},{32,96},{40,104},{48,112},{56,120},{... | collective-permute-start | bytes 638984 | tf_op jit(solution)/shard_map/ppermute | solution.py:204
  31.2 13.2 %collective-permute-start.1 = (bf16[8,104,128]{2,1,0:T(8,128)(2,1)}, bf16[8,104,128]{2,1,0:T(8,128)(2,1)S(1)}, u32[]{:S(2)}, u32[]{:S(2)}) collective-permute-start(bf16[8,104,128]{2,1,0:T(8,128)(2,1)} %all-to-all-done.refs_0_), channel_id=1, source_target_pairs={{0,448},{8,456},{16,464},{24,472},{32,480},{40,488},{48,496},{56,5... | collective-permute-start | bytes 638984 | tf_op jit(solution)/shard_map/ppermute | solution.py:204
  33.6 14.6 %collective-permute-start.2 = (bf16[8,104,128]{2,1,0:T(8,128)(2,1)}, bf16[8,104,128]{2,1,0:T(8,128)(2,1)S(1)}, u32[]{:S(2)}, u32[]{:S(2)}) collective-permute-start(bf16[8,104,128]{2,1,0:T(8,128)(2,1)} %all-to-all-done.refs_0_), channel_id=1, source_target_pairs={{0,128},{8,136},{16,144},{24,152},{32,160},{40,168},{48,176},{56,1... | collective-permute-start | bytes 638984 | tf_op jit(solution)/shard_map/ppermute | solution.py:204
  40.5 13.3 %collective-permute-start.3 = (bf16[8,104,128]{2,1,0:T(8,128)(2,1)}, bf16[8,104,128]{2,1,0:T(8,128)(2,1)S(1)}, u32[]{:S(2)}, u32[]{:S(2)}) collective-permute-start(bf16[8,104,128]{2,1,0:T(8,128)(2,1)} %all-to-all-done.refs_0_), channel_id=1, source_target_pairs={{0,384},{8,392},{16,400},{24,408},{32,416},{40,424},{48,432},{56,4... | collective-permute-start | bytes 638984 | tf_op jit(solution)/shard_map/ppermute | solution.py:204
  53.9 21.8 %all-to-all-start.2 = ((bf16[64,8,320]{2,1,0:T(8,128)(2,1)}), bf16[64,8,320]{2,1,0:T(8,128)(2,1)S(1)}, u32[]{:S(2)}, u32[]{:S(2)}) async-start(bf16[64,8,320]{2,1,0:T(8,128)(2,1)} %bitcast.4), calls=%async_computation.2 | async-start | bytes 786432 | tf_op jit(solution)/shard_map/all_to_all | solution.py:259
  59.5 21.8 %collective-permute-start.4 = (bf16[8,104,128]{2,1,0:T(8,128)(2,1)S(1)}, bf16[8,104,128]{2,1,0:T(8,128)(2,1)S(1)}, u32[]{:S(2)}, u32[]{:S(2)}) collective-permute-start(bf16[8,104,128]{2,1,0:T(8,128)(2,1)S(1)} %collective-permute-done.2.refs_2_), channel_id=1, source_target_pairs={{0,64},{8,72},{16,80},{24,88},{32,96},{40,104},{48,112},{56,120},{... | collective-permute-start | bytes 638984 | tf_op jit(solution)/shard_map/ppermute | solution.py:204
  62.9 18.4 %collective-permute-start.7 = (bf16[8,104,128]{2,1,0:T(8,128)(2,1)S(1)}, bf16[8,104,128]{2,1,0:T(8,128)(2,1)S(1)}, u32[]{:S(2)}, u32[]{:S(2)}) collective-permute-start(bf16[8,104,128]{2,1,0:T(8,128)(2,1)S(1)} %collective-permute-done.3.refs_7_), channel_id=1, source_target_pairs={{0,448},{8,456},{16,464},{24,472},{32,480},{40,488},{48,496},{56,5... | collective-permute-start | bytes 638984 | tf_op jit(solution)/shard_map/ppermute | solution.py:204
  65.4 12.3 %collective-permute-start.5 = (bf16[4,104,128]{2,1,0:T(8,128)(2,1)S(1)}, bf16[4,104,128]{2,1,0:T(8,128)(2,1)S(1)}, u32[]{:S(2)}, u32[]{:S(2)}) collective-permute-start(bf16[4,104,128]{2,1,0:T(8,128)(2,1)S(1)} %slice.6), channel_id=1, source_target_pairs={{0,128},{8,136},{16,144},{24,152},{32,160},{40,168},{48,176},{56,1... | collective-permute-start | bytes 319496 | tf_op jit(solution)/shard_map/ppermute | solution.py:204
  72.2 9.1 %collective-permute-start.6 = (bf16[4,104,128]{2,1,0:T(8,128)(2,1)S(1)}, bf16[4,104,128]{2,1,0:T(8,128)(2,1)S(1)}, u32[]{:S(2)}, u32[]{:S(2)}) collective-permute-start(bf16[4,104,128]{2,1,0:T(8,128)(2,1)S(1)} %slice.7), channel_id=1, source_target_pairs={{0,384},{8,392},{16,400},{24,408},{32,416},{40,424},{48,432},{56,4... | collective-permute-start | bytes 319496 | tf_op jit(solution)/shard_map/ppermute | solution.py:204
  84.7 7.3 %collective-permute-start.8 = (bf16[80,512]{1,0:T(8,128)(2,1)S(1)}, bf16[80,512]{1,0:T(8,128)(2,1)S(1)}, u32[]{:S(2)}, u32[]{:S(2)}) collective-permute-start(bf16[80,512]{1,0:T(8,128)(2,1)S(1)} %shard_map.68), channel_id=1, source_target_pairs={{0,8},{8,0},{16,24},{24,16},{32,40},{40,32},{48,56},{56,48},{64,72... | collective-permute-start | bytes 245768 | tf_op jit(solution)/shard_map/ppermute | solution.py:292

commit v4 on v3

--- a/solution.py
+++ b/solution.py
@@ -143,22 +143,12 @@
         )
 
 
-def positional_kernel(
-    swap, owner_ref, order_ref, len_ref, shifted_ref, packed_ref, *refs
-):
-    taps_refs, (out_ref, sums, result, sem) = refs[:-4], refs[-4:]
-    parity = owner_ref[0] % 2
-    which = 1 - parity if swap else parity
-    ring = taps_refs[0].shape[0]
-    blocks = [[(ref, n) for n in range(ring)] for ref in taps_refs[:4] + taps_refs[6:]]
-    blocks.insert(4, [(ref, n) for ref in taps_refs[4:6] for n in range(ring // 2)])
-    slot = 2 * (owner_ref[0] - parity + which)
-    first_len = len_ref[order_ref[slot]] // HOP
-    second_len = len_ref[order_ref[slot + 1]] // HOP
-    _, total, group = packed_ref.shape
-    reach = sums.shape[0]
-
-    for away, pieces in enumerate(blocks):
+def add_blocks(which, ring, distances, owner_ref, shifted_ref, refs, before, sums):
+    refs = list(refs)
+    for away in distances:
+        count = 2 if away == ring // 2 else 1
+        pieces = [(ref, n) for ref in refs[:count] for n in range(ring // count)]
+        refs = refs[count:]
         start = pl.multiple_of(lax.rem(owner_ref[0] // ring + ring - away, ring) * STEP, STEP)
         left, right = [], []
         for slot in range(9):
@@ -170,9 +160,27 @@
             right += [turned[r % 4][r // 4 * 8 : r // 4 * 8 + 8] for r in range(10)]
             if size == 96:
                 right += [fold[0:16]]
-        matrix = jnp.concatenate([jnp.concatenate(left, axis=0), jnp.concatenate(right, axis=0).astype(jnp.bfloat16)], axis=1)
-        term = dot(shifted_ref[which, pl.ds(start, reach), :], matrix)
-        sums[...] = term if away == 0 else sums[...] + term
+        right = jnp.concatenate(right, axis=0).astype(jnp.bfloat16)
+        matrix = jnp.concatenate([jnp.concatenate(left, axis=0), right], axis=1)
+        term = dot(shifted_ref[which, pl.ds(start, sums.shape[0]), :], matrix)
+        sums[...] = term if before is None else before[...] + term
+        before = sums
+
+
+def near_kernel(ring, distances, owner_ref, shifted_ref, *refs):
+    add_blocks(1 - owner_ref[0] % 2, ring, distances, owner_ref, shifted_ref, refs[:-1], None, refs[-1])
+
+
+def positional_kernel(swap, ring, distances, owner_ref, order_ref, len_ref, shifted_ref, packed_ref, *refs):
+    taps_refs, (out_ref, sums, result, sem) = refs[:-4], refs[-4:]
+    parity = owner_ref[0] % 2
+    which = 1 - parity if swap else parity
+    before, taps_refs = (taps_refs[0], taps_refs[1:]) if swap else (None, taps_refs)
+    slot = 2 * (owner_ref[0] - parity + which)
+    first_len = len_ref[order_ref[slot]] // HOP
+    second_len = len_ref[order_ref[slot + 1]] // HOP
+    _, total, group = packed_ref.shape
+    add_blocks(which, ring, distances, owner_ref, shifted_ref, taps_refs, before, sums)
 
     spot = iota((total, 1), 0)
     near = sums[0:total, 0:group] + sums[1 : total + 1, group : 2 * group]
@@ -242,7 +250,7 @@
         compiler_params=pltpu.CompilerParams(vmem_limit_bytes=66900000),
     )(features.reshape(utts * slice_rows, channels), conv_weight, proj_weight)
     taps, sent = lax.optimization_barrier((taps, sent))
-    one, minus_one, two, minus_two = [send(taps, ring, step) for step in (1, -1, 2, -2)]
+    two, minus_two, one, minus_one = [send(taps, ring, step) for step in (2, -2, 1, -1)]
     spread = lax.all_to_all(sent, "mp", split_axis=0, concat_axis=0, tiled=True)
 
     ordered = pl.pallas_call(
@@ -255,7 +263,7 @@
     one, minus_one, two, minus_two, ordered = lax.optimization_barrier((one, minus_one, two, minus_two, ordered))
     three, minus_three = send(two, ring, 1), send(minus_two, ring, -1)
     low, high = send(two[: ring // 2], ring, 2), send(minus_two[ring // 2 :], ring, -2)
-    taps = (taps, one, two, three, low, high, minus_three, minus_two, minus_one)
+    early_taps, late_taps = (taps, one, two, minus_two, minus_one), (three, low, high, minus_three)
     pair_rows = lax.all_to_all(
         ordered.reshape(owners, 8, 2 * width), "dp", split_axis=0, concat_axis=0, tiled=True
     )
@@ -275,22 +283,33 @@
         scratch_shapes=[pltpu.VMEM((2, length + STEP, group), jnp.float32)],
         compiler_params=params,
     )(*scalars, pair_rows.reshape(owners * 8, 2 * width))
-    convolve = lambda swap: pl.pallas_call(
-        functools.partial(positional_kernel, swap),
-        out_shape=jax.ShapeDtypeStruct((group if swap else width, total), jnp.bfloat16),
-        in_specs=[SMEM, SMEM, SMEM, VMEM, VMEM] + [VMEM] * len(taps),
-        out_specs=ANY,
-        scratch_shapes=[
-            pltpu.VMEM((reach, 256), jnp.float32),
-            pltpu.VMEM((group, total), jnp.bfloat16),
-            pltpu.SemaphoreType.DMA,
-        ],
-        compiler_params=params,
-    )
-    other = convolve(True)(*scalars, shifted, packed, *taps)
+    early, late = (0, 1, 2, 6, 7), (3, 4, 5)
+    begun = pl.pallas_call(
+        functools.partial(near_kernel, ring, early),
+        out_shape=jax.ShapeDtypeStruct((reach, 256), jnp.float32),
+        in_specs=[SMEM] + [VMEM] * 6,
+        out_specs=VMEM,
+        compiler_params=params,
+    )(owner, shifted, *early_taps)
+
+    def convolve(swap, distances, *taps):
+        return pl.pallas_call(
+            functools.partial(positional_kernel, swap, ring, distances),
+            out_shape=jax.ShapeDtypeStruct((group if swap else width, total), jnp.bfloat16),
+            in_specs=[SMEM, SMEM, SMEM, VMEM, VMEM] + [VMEM] * len(taps),
+            out_specs=ANY,
+            scratch_shapes=[
+                pltpu.VMEM((reach, 256), jnp.float32),
+                pltpu.VMEM((group, total), jnp.bfloat16),
+                pltpu.SemaphoreType.DMA,
+            ],
+            compiler_params=params,
+        )(*scalars, shifted, packed, *taps)
+
+    other = convolve(True, late, begun, *late_taps)
     packed, other = lax.optimization_barrier((packed, other))
     received = lax.ppermute(other, "dp", [(o, o ^ 1) for o in range(owners)])
-    own = convolve(False)(*scalars, shifted, packed, *taps)
+    own = convolve(False, early + late, *early_taps, *late_taps)
     hidden = pl.pallas_call(
         join_kernel,
         out_shape=jax.ShapeDtypeStruct((width, total), jnp.bfloat16),

time: 93.4 us -> 90.7 us (0.971)
  the two profiles are of different devices: /device:TPU:18 before, /device:TPU:2 now
where the time goes in v4:
time: 90.7 us; the launch traced here: 90 us
  starting transfers between devices  52.1 us (57%)
  waiting for transfers between devices  20.1 us (22%)
  Pallas kernels  16.7 us (18%)
  local copies, waits for them, and re-layouts  0.91 us (1%)
    ppermute x8, starting transfers between devices, send(): lax.ppermute(values, 'dp', [(o, (o + step * ring) % (ring * ring)) for o...  29 us
    all_to_all x1, starting transfers between devices, shards(): lax.all_to_all(tap_copies, 'dp', 0, 0, axis_index_groups=along_z, tiled=T...  10.3 us
    ppermute x8, waiting for transfers between devices, send(): lax.ppermute(values, 'dp', [(o, (o + step * ring) % (ring * ring)) for o...  8.53 us
    all_to_all x1, waiting for transfers between devices, shards(): lax.all_to_all(tap_copies, 'dp', 0, 0, axis_index_groups=along_z, tiled=T...  7.69 us
    pallas_call x2, Pallas kernels, convolve(): pl.pallas_call(functools.partial(positional_kernel, swap, ring, distances...  5.72 us
    all_to_all x1, starting transfers between devices, shards(): lax.all_to_all(ordered.reshape(owners, 8, 2 * width), 'dp', split_axis=0,...  5.09 us
    all_to_all x1, starting transfers between devices, shards(): spread = lax.all_to_all(sent, 'mp', split_axis=0, concat_axis=0, tiled=True)  4.83 us
    all_to_all x1, waiting for transfers between devices, shards(): lax.all_to_all(ordered.reshape(owners, 8, 2 * width), 'dp', split_axis=0,...  3.88 us
  transfers between devices with their start and end apart: 12, of which 4 were waited for; matrix products, arithmetic and copies ran while one was open for 0% of the time, Pallas kernels for 15%

profile of v4, /device:TPU:2, one launch (start us, length us, event | category | flops | bytes accessed | tf_op | source)
XLA Modules:
  0.0 90.0 jit_solution(896893113455356022)
XLA Ops:
  0.0 0.0 copy-start
  0.0 0.9 copy-done
  0.9 0.0 copy-start.1
  0.9 0.8 shard_map.64
  1.7 10.3 %all-to-all-start = ((bf16[8,104,128]{2,1,0:T(8,128)(2,1)}), bf16[8,104,128]{2,1,0:T(8,128)(2,1)}, u32[]{:S(2)}, u32[]{:S(2)}) async-start(bf16[8,104,128]{2,1,0:T(8,128)(2,1)} %shard_map.64), calls=%async_computation | async-start | bytes 425984 | tf_op jit(solution)/shard_map/all_to_all | solution.py:237
  12.0 0.0 copy-start.2
  12.0 3.2 %shard_map.65 = bf16[8,16,1280]{2,1,0:T(8,128)(2,1)} custom-call(bf16[256,512]{1,0:T(8,128)(2,1)} %bitcast.10, bf16[2,512,512]{2,1,0:T(8,128)(2,1)} %conv_hbm.1, bf16[512,1280]{1,0:T(8,128)(2,1)} %proj_hbm.1), custom_call_target="tpu_custom_call" | custom-call | tf_op jit(solution)/shard_map/pallas_call | solution.py:239
  15.2 7.7 %all-to-all-done.refs_0_ = bf16[8,104,128]{2,1,0:T(8,128)(2,1)} async-done(((bf16[8,104,128]{2,1,0:T(8,128)(2,1)}), bf16[8,104,128]{2,1,0:T(8,128)(2,1)}, u32[]{:S(2)}, u32[]{:S(2)}) %all-to-all-start) | async-done | bytes 213024 | tf_op jit(solution)/shard_map/all_to_all | solution.py:237
  22.9 4.8 %all-to-all-start.1 = ((bf16[8,16,1280]{2,1,0:T(8,128)(2,1)}), bf16[8,16,1280]{2,1,0:T(8,128)(2,1)S(1)}, u32[]{:S(2)}, u32[]{:S(2)}) async-start(bf16[8,16,1280]{2,1,0:T(8,128)(2,1)} %shard_map.65), calls=%async_computation.1 | async-start | bytes 655360 | tf_op jit(solution)/shard_map/all_to_all | solution.py:254
  27.7 6.2 %collective-permute-start.3 = (bf16[8,104,128]{2,1,0:T(8,128)(2,1)}, bf16[8,104,128]{2,1,0:T(8,128)(2,1)S(1)}, u32[]{:S(2)}, u32[]{:S(2)}) collective-permute-start(bf16[8,104,128]{2,1,0:T(8,128)(2,1)} %all-to-all-done.refs_0_), channel_id=1, source_target_pairs={{0,384},{8,392},{16,400},{24,408},{32,416},{40,424},{48,432},{56,4... | collective-permute-start | bytes 638984 | tf_op jit(solution)/shard_map/ppermute | solution.py:212
  33.9 1.9 %collective-permute-start.2 = (bf16[8,104,128]{2,1,0:T(8,128)(2,1)}, bf16[8,104,128]{2,1,0:T(8,128)(2,1)S(1)}, u32[]{:S(2)}, u32[]{:S(2)}) collective-permute-start(bf16[8,104,128]{2,1,0:T(8,128)(2,1)} %all-to-all-done.refs_0_), channel_id=1, source_target_pairs={{0,128},{8,136},{16,144},{24,152},{32,160},{40,168},{48,176},{56,1... | collective-permute-start | bytes 638984 | tf_op jit(solution)/shard_map/ppermute | solution.py:212
  35.8 5.2 %collective-permute-start.1 = (bf16[8,104,128]{2,1,0:T(8,128)(2,1)}, bf16[8,104,128]{2,1,0:T(8,128)(2,1)S(1)}, u32[]{:S(2)}, u32[]{:S(2)}) collective-permute-start(bf16[8,104,128]{2,1,0:T(8,128)(2,1)} %all-to-all-done.refs_0_), channel_id=1, source_target_pairs={{0,448},{8,456},{16,464},{24,472},{32,480},{40,488},{48,496},{56,5... | collective-permute-start | bytes 638984 | tf_op jit(solution)/shard_map/ppermute | solution.py:212
  41.1 1.9 %collective-permute-start = (bf16[8,104,128]{2,1,0:T(8,128)(2,1)}, bf16[8,104,128]{2,1,0:T(8,128)(2,1)S(1)}, u32[]{:S(2)}, u32[]{:S(2)}) collective-permute-start(bf16[8,104,128]{2,1,0:T(8,128)(2,1)} %all-to-all-done.refs_0_), channel_id=1, source_target_pairs={{0,64},{8,72},{16,80},{24,88},{32,96},{40,104},{48,112},{56,120},{... | collective-permute-start | bytes 638984 | tf_op jit(solution)/shard_map/ppermute | solution.py:212
  43.0 0.0 all-to-all-done.1
  43.0 0.0 copy-done.1
  43.0 1.9 %shard_map.66 = bf16[512,320]{1,0:T(8,128)(2,1)} custom-call(s32[1,128]{1,0:T(1,128)S(1)} %bitcast.9, bf16[128,1280]{1,0:T(8,128)(2,1)S(1)} %bitcast.8), custom_call_target="tpu_custom_call" | custom-call | tf_op jit(solution)/shard_map/pallas_call | solution.py:256
  45.0 0.0 collective-permute-done.3.refs_3_
  45.0 4.8 %collective-permute-done.2.refs_2_ = bf16[8,104,128]{2,1,0:T(8,128)(2,1)S(1)} collective-permute-done((bf16[8,104,128]{2,1,0:T(8,128)(2,1)}, bf16[8,104,128]{2,1,0:T(8,128)(2,1)S(1)}, u32[]{:S(2)}, u32[]{:S(2)}) %collective-permute-start.2) | collective-permute-done | bytes 213024 | tf_op jit(solution)/shard_map/ppermute | solution.py:212
  49.8 0.0 collective-permute-done.1.refs_4_
  49.8 3.7 %collective-permute-done.refs_1_ = bf16[8,104,128]{2,1,0:T(8,128)(2,1)S(1)} collective-permute-done((bf16[8,104,128]{2,1,0:T(8,128)(2,1)}, bf16[8,104,128]{2,1,0:T(8,128)(2,1)S(1)}, u32[]{:S(2)}, u32[]{:S(2)}) %collective-permute-start) | collective-permute-done | bytes 213024 | tf_op jit(solution)/shard_map/ppermute | solution.py:212
  53.5 5.1 %all-to-all-start.2 = ((bf16[64,8,320]{2,1,0:T(8,128)(2,1)}), bf16[64,8,320]{2,1,0:T(8,128)(2,1)S(1)}, u32[]{:S(2)}, u32[]{:S(2)}) async-start(bf16[64,8,320]{2,1,0:T(8,128)(2,1)} %bitcast.4), calls=%async_computation.2 | async-start | bytes 786432 | tf_op jit(solution)/shard_map/all_to_all | solution.py:267
  58.6 3.5 %collective-permute-start.4 = (bf16[8,104,128]{2,1,0:T(8,128)(2,1)S(1)}, bf16[8,104,128]{2,1,0:T(8,128)(2,1)S(1)}, u32[]{:S(2)}, u32[]{:S(2)}) collective-permute-start(bf16[8,104,128]{2,1,0:T(8,128)(2,1)S(1)} %collective-permute-done.2.refs_2_), channel_id=1, source_target_pairs={{0,64},{8,72},{16,80},{24,88},{32,96},{40,104},{48,112},{56,120},{... | collective-permute-start | bytes 638984 | tf_op jit(solution)/shard_map/ppermute | solution.py:212
  62.1 3.6 %collective-permute-start.7 = (bf16[8,104,128]{2,1,0:T(8,128)(2,1)S(1)}, bf16[8,104,128]{2,1,0:T(8,128)(2,1)S(1)}, u32[]{:S(2)}, u32[]{:S(2)}) collective-permute-start(bf16[8,104,128]{2,1,0:T(8,128)(2,1)S(1)} %collective-permute-done.3.refs_3_), channel_id=1, source_target_pairs={{0,448},{8,456},{16,464},{24,472},{32,480},{40,488},{48,496},{56,5... | collective-permute-start | bytes 638984 | tf_op jit(solution)/shard_map/ppermute | solution.py:212
  65.7 4.6 %collective-permute-start.6 = (bf16[4,104,128]{2,1,0:T(8,128)(2,1)S(1)}, bf16[4,104,128]{2,1,0:T(8,128)(2,1)S(1)}, u32[]{:S(2)}, u32[]{:S(2)}) collective-permute-start(bf16[4,104,128]{2,1,0:T(8,128)(2,1)S(1)} %slice.7), channel_id=1, source_target_pairs={{0,384},{8,392},{16,400},{24,408},{32,416},{40,424},{48,432},{56,4... | collective-permute-start | bytes 319496 | tf_op jit(solution)/shard_map/ppermute | solution.py:212
  70.3 2.2 %collective-permute-start.5 = (bf16[4,104,128]{2,1,0:T(8,128)(2,1)S(1)}, bf16[4,104,128]{2,1,0:T(8,128)(2,1)S(1)}, u32[]{:S(2)}, u32[]{:S(2)}) collective-permute-start(bf16[4,104,128]{2,1,0:T(8,128)(2,1)S(1)} %slice.6), channel_id=1, source_target_pairs={{0,128},{8,136},{16,144},{24,152},{32,160},{40,168},{48,176},{56,1... | collective-permute-start | bytes 319496 | tf_op jit(solution)/shard_map/ppermute | solution.py:212
  72.4 3.9 %all-to-all-done.2 = bf16[64,8,320]{2,1,0:T(8,128)(2,1)S(1)} async-done(((bf16[64,8,320]{2,1,0:T(8,128)(2,1)}), bf16[64,8,320]{2,1,0:T(8,128)(2,1)S(1)}, u32[]{:S(2)}, u32[]{:S(2)}) %all-to-all-start.2) | async-done | bytes 327712 | tf_op jit(solution)/shard_map/all_to_all | solution.py:267
  76.3 0.0 copy-done.2
  76.3 2.0 %shard_map.67 = (bf16[2,704,768]{2,1,0:T(8,128)(2,1)S(1)}, f32[2,512,80]{2,1,0:T(8,128)S(1)}) custom-call(s32[1]{0:T(128)} %bitcast.owner_ref, s32[128]{0:T(128)S(1)} %copy-done.1, s32[128]{0:T(128)S(1)} %copy-done.2, bf16[512,320]{1,0:T(8,128)(2,1)S(1)} %bitcast.7), custom_call_target="tpu_custom_call" | custom-call | tf_op jit(solution)/shard_map/pallas_call | solution.py:275
  78.3 2.4 %shard_map.68.refs_0_ = f32[592,256]{1,0:T(8,128)S(1)} custom-call(s32[1]{0:T(128)} %bitcast.owner_ref, bf16[2,704,768]{2,1,0:T(8,128)(2,1)S(1)} %get-tuple-element.20.shifted_ref, bf16[8,104,128]{2,1,0:T(8,128)(2,1)} %all-to-all-done.refs_0_, bf16[8,104,128]{2,1,0:T(8,128)(2,1)S(1)} %collective-permute-done.refs_1_, ...), custom_call_target="tpu_custom_call" | custom-call | tf_op jit(solution)/shard_map/pallas_call | solution.py:287
  80.7 0.0 collective-permute-done.6.refs_3_.refs_7_
  80.7 0.0 collective-permute-done.5.refs_2_.refs_6_
  80.7 0.0 collective-permute-done.4.refs_1_.refs_5_
  80.8 0.0 collective-permute-done.7.refs_4_.refs_8_
  80.8 1.8 %shard_map.69 = bf16[80,512]{1,0:T(8,128)(2,1)S(1)} custom-call(s32[1]{0:T(128)} %bitcast.owner_ref, s32[128]{0:T(128)S(1)} %copy-done.1, s32[128]{0:T(128)S(1)} %copy-done.2, bf16[2,704,768]{2,1,0:T(8,128)(2,1)S(1)} %get-tuple-element.20.shifted_ref, f32[2,512,80]{2,1,0:T(8,128)S(1)} %get-tuple-element.26.packed_ref, f32[592,256]{1,0:T(8,128)S(1)} %shard_map.68.refs_0_, ...), custom_call_target="tpu_custom_call" | custom-call | tf_op jit(solution)/shard_map/pallas_call | solution.py:296
  82.6 2.9 %collective-permute-start.8 = (bf16[80,512]{1,0:T(8,128)(2,1)S(1)}, bf16[80,512]{1,0:T(8,128)(2,1)S(1)}, u32[]{:S(2)}, u32[]{:S(2)}) collective-permute-start(bf16[80,512]{1,0:T(8,128)(2,1)S(1)} %shard_map.69), channel_id=1, source_target_pairs={{0,8},{8,0},{16,24},{24,16},{32,40},{40,32},{48,56},{56,48},{64,72... | collective-permute-start | bytes 245768 | tf_op jit(solution)/shard_map/ppermute | solution.py:311
  85.4 3.9 %shard_map.70.own_hbm = bf16[160,512]{1,0:T(8,128)(2,1)} custom-call(s32[1]{0:T(128)} %bitcast.owner_ref, s32[128]{0:T(128)S(1)} %copy-done.1, s32[128]{0:T(128)S(1)} %copy-done.2, bf16[2,704,768]{2,1,0:T(8,128)(2,1)S(1)} %get-tuple-element.20.shifted_ref, f32[2,512,80]{2,1,0:T(8,128)S(1)} %get-tuple-element.26.packed_ref, ...), custom_call_target="tpu_custom_call" | custom-call | tf_op jit(solution)/shard_map/pallas_call | solution.py:296
  89.4 0.0 collective-permute-done.8.received_hbm
  89.4 0.7 shard_map.71
  (2 shorter events, 0.0 us)
Async XLA Ops:
  0.0 0.9 copy-start
  0.9 42.1 %copy-start.1 = (s32[128]{0:T(128)S(1)}, s32[128]{0:T(128)}, u32[]{:S(2)}) copy-start(s32[128]{0:T(128)} %order_ref.5) | copy-start | bytes 1540
  1.7 21.2 %all-to-all-start = ((bf16[8,104,128]{2,1,0:T(8,128)(2,1)}), bf16[8,104,128]{2,1,0:T(8,128)(2,1)}, u32[]{:S(2)}, u32[]{:S(2)}) async-start(bf16[8,104,128]{2,1,0:T(8,128)(2,1)} %shard_map.64), calls=%async_computation | async-start | bytes 425984 | tf_op jit(solution)/shard_map/all_to_all | solution.py:237
  12.0 64.3 %copy-start.2 = (s32[128]{0:T(128)S(1)}, s32[128]{0:T(128)}, u32[]{:S(2)}) copy-start(s32[128]{0:T(128)} %len_ref.5) | copy-start | bytes 1540
  22.9 20.1 %all-to-all-start.1 = ((bf16[8,16,1280]{2,1,0:T(8,128)(2,1)}), bf16[8,16,1280]{2,1,0:T(8,128)(2,1)S(1)}, u32[]{:S(2)}, u32[]{:S(2)}) async-start(bf16[8,16,1280]{2,1,0:T(8,128)(2,1)} %shard_map.65), calls=%async_computation.1 | async-start | bytes 655360 | tf_op jit(solution)/shard_map/all_to_all | solution.py:254
  27.7 17.2 %collective-permute-start.3 = (bf16[8,104,128]{2,1,0:T(8,128)(2,1)}, bf16[8,104,128]{2,1,0:T(8,128)(2,1)S(1)}, u32[]{:S(2)}, u32[]{:S(2)}) collective-permute-start(bf16[8,104,128]{2,1,0:T(8,128)(2,1)} %all-to-all-done.refs_0_), channel_id=1, source_target_pairs={{0,384},{8,392},{16,400},{24,408},{32,416},{40,424},{48,432},{56,4... | collective-permute-start | bytes 638984 | tf_op jit(solution)/shard_map/ppermute | solution.py:212
  33.9 15.9 %collective-permute-start.2 = (bf16[8,104,128]{2,1,0:T(8,128)(2,1)}, bf16[8,104,128]{2,1,0:T(8,128)(2,1)S(1)}, u32[]{:S(2)}, u32[]{:S(2)}) collective-permute-start(bf16[8,104,128]{2,1,0:T(8,128)(2,1)} %all-to-all-done.refs_0_), channel_id=1, source_target_pairs={{0,128},{8,136},{16,144},{24,152},{32,160},{40,168},{48,176},{56,1... | collective-permute-start | bytes 638984 | tf_op jit(solution)/shard_map/ppermute | solution.py:212
  35.8 14.0 %collective-permute-start.1 = (bf16[8,104,128]{2,1,0:T(8,128)(2,1)}, bf16[8,104,128]{2,1,0:T(8,128)(2,1)S(1)}, u32[]{:S(2)}, u32[]{:S(2)}) collective-permute-start(bf16[8,104,128]{2,1,0:T(8,128)(2,1)} %all-to-all-done.refs_0_), channel_id=1, source_target_pairs={{0,448},{8,456},{16,464},{24,472},{32,480},{40,488},{48,496},{56,5... | collective-permute-start | bytes 638984 | tf_op jit(solution)/shard_map/ppermute | solution.py:212
  41.1 12.4 %collective-permute-start = (bf16[8,104,128]{2,1,0:T(8,128)(2,1)}, bf16[8,104,128]{2,1,0:T(8,128)(2,1)S(1)}, u32[]{:S(2)}, u32[]{:S(2)}) collective-permute-start(bf16[8,104,128]{2,1,0:T(8,128)(2,1)} %all-to-all-done.refs_0_), channel_id=1, source_target_pairs={{0,64},{8,72},{16,80},{24,88},{32,96},{40,104},{48,112},{56,120},{... | collective-permute-start | bytes 638984 | tf_op jit(solution)/shard_map/ppermute | solution.py:212
  53.5 22.8 %all-to-all-start.2 = ((bf16[64,8,320]{2,1,0:T(8,128)(2,1)}), bf16[64,8,320]{2,1,0:T(8,128)(2,1)S(1)}, u32[]{:S(2)}, u32[]{:S(2)}) async-start(bf16[64,8,320]{2,1,0:T(8,128)(2,1)} %bitcast.4), calls=%async_computation.2 | async-start | bytes 786432 | tf_op jit(solution)/shard_map/all_to_all | solution.py:267
  58.6 22.2 %collective-permute-start.4 = (bf16[8,104,128]{2,1,0:T(8,128)(2,1)S(1)}, bf16[8,104,128]{2,1,0:T(8,128)(2,1)S(1)}, u32[]{:S(2)}, u32[]{:S(2)}) collective-permute-start(bf16[8,104,128]{2,1,0:T(8,128)(2,1)S(1)} %collective-permute-done.2.refs_2_), channel_id=1, source_target_pairs={{0,64},{8,72},{16,80},{24,88},{32,96},{40,104},{48,112},{56,120},{... | collective-permute-start | bytes 638984 | tf_op jit(solution)/shard_map/ppermute | solution.py:212
  62.1 18.7 %collective-permute-start.7 = (bf16[8,104,128]{2,1,0:T(8,128)(2,1)S(1)}, bf16[8,104,128]{2,1,0:T(8,128)(2,1)S(1)}, u32[]{:S(2)}, u32[]{:S(2)}) collective-permute-start(bf16[8,104,128]{2,1,0:T(8,128)(2,1)S(1)} %collective-permute-done.3.refs_3_), channel_id=1, source_target_pairs={{0,448},{8,456},{16,464},{24,472},{32,480},{40,488},{48,496},{56,5... | collective-permute-start | bytes 638984 | tf_op jit(solution)/shard_map/ppermute | solution.py:212
  65.7 15.0 %collective-permute-start.6 = (bf16[4,104,128]{2,1,0:T(8,128)(2,1)S(1)}, bf16[4,104,128]{2,1,0:T(8,128)(2,1)S(1)}, u32[]{:S(2)}, u32[]{:S(2)}) collective-permute-start(bf16[4,104,128]{2,1,0:T(8,128)(2,1)S(1)} %slice.7), channel_id=1, source_target_pairs={{0,384},{8,392},{16,400},{24,408},{32,416},{40,424},{48,432},{56,4... | collective-permute-start | bytes 319496 | tf_op jit(solution)/shard_map/ppermute | solution.py:212
  70.3 10.4 %collective-permute-start.5 = (bf16[4,104,128]{2,1,0:T(8,128)(2,1)S(1)}, bf16[4,104,128]{2,1,0:T(8,128)(2,1)S(1)}, u32[]{:S(2)}, u32[]{:S(2)}) collective-permute-start(bf16[4,104,128]{2,1,0:T(8,128)(2,1)S(1)} %slice.6), channel_id=1, source_target_pairs={{0,128},{8,136},{16,144},{24,152},{32,160},{40,168},{48,176},{56,1... | collective-permute-start | bytes 319496 | tf_op jit(solution)/shard_map/ppermute | solution.py:212
  82.6 6.8 %collective-permute-start.8 = (bf16[80,512]{1,0:T(8,128)(2,1)S(1)}, bf16[80,512]{1,0:T(8,128)(2,1)S(1)}, u32[]{:S(2)}, u32[]{:S(2)}) collective-permute-start(bf16[80,512]{1,0:T(8,128)(2,1)S(1)} %shard_map.69), channel_id=1, source_target_pairs={{0,8},{8,0},{16,24},{24,16},{32,40},{40,32},{48,56},{56,48},{64,72... | collective-permute-start | bytes 245768 | tf_op jit(solution)/shard_map/ppermute | solution.py:311

commit v5 on v4

--- a/solution.py
+++ b/solution.py
@@ -260,7 +260,7 @@
         out_specs=VMEM,
         compiler_params=params,
     )(pack_order.reshape(1, -1), spread.reshape(parts * utts, frames * width))
-    one, minus_one, two, minus_two, ordered = lax.optimization_barrier((one, minus_one, two, minus_two, ordered))
+    two, minus_two, ordered = lax.optimization_barrier((two, minus_two, ordered))
     three, minus_three = send(two, ring, 1), send(minus_two, ring, -1)
     low, high = send(two[: ring // 2], ring, 2), send(minus_two[ring // 2 :], ring, -2)
     early_taps, late_taps = (taps, one, two, minus_two, minus_one), (three, low, high, minus_three)

time: 90.7 us -> 92.2 us (1.017)
  the two profiles are of different devices: /device:TPU:2 before, /device:TPU:10 now
where the time goes in v5:
time: 92.2 us; the launch traced here: 91.5 us
  starting transfers between devices  51.5 us (56%)
  waiting for transfers between devices  22.2 us (24%)
  Pallas kernels  16.7 us (18%)
    ppermute x8, starting transfers between devices, send(): lax.ppermute(values, 'dp', [(o, (o + step * ring) % (ring * ring)) for o...  27.7 us
    ppermute x8, waiting for transfers between devices, send(): lax.ppermute(values, 'dp', [(o, (o + step * ring) % (ring * ring)) for o...  14.5 us
    all_to_all x1, starting transfers between devices, shards(): lax.all_to_all(tap_copies, 'dp', 0, 0, axis_index_groups=along_z, tiled=T...  10.3 us
    all_to_all x1, waiting for transfers between devices, shards(): lax.all_to_all(tap_copies, 'dp', 0, 0, axis_index_groups=along_z, tiled=T...  7.69 us
    pallas_call x2, Pallas kernels, convolve(): pl.pallas_call(functools.partial(positional_kernel, swap, ring, distances...  5.71 us
    all_to_all x1, starting transfers between devices, shards(): lax.all_to_all(ordered.reshape(owners, 8, 2 * width), 'dp', split_axis=0,...  5.2 us
    all_to_all x1, starting transfers between devices, shards(): spread = lax.all_to_all(sent, 'mp', split_axis=0, concat_axis=0, tiled=True)  4.83 us
    ppermute x1, starting transfers between devices, shards(): received = lax.ppermute(other, 'dp', [(o, o ^ 1) for o in range(owners)])  3.39 us
  transfers between devices with their start and end apart: 12, of which 4 were waited for; matrix products, arithmetic and copies ran while one was open for 0% of the time, Pallas kernels for 15%

profile of v5, /device:TPU:10, one launch (start us, length us, event | category | flops | bytes accessed | tf_op | source)
XLA Modules:
  0.0 91.5 jit_solution(8352230519600543787)
XLA Ops:
  0.0 0.0 copy-start
  0.0 0.9 copy-done
  0.9 0.0 copy-start.1
  0.9 0.8 shard_map.64
  1.7 10.3 %all-to-all-start = ((bf16[8,104,128]{2,1,0:T(8,128)(2,1)}), bf16[8,104,128]{2,1,0:T(8,128)(2,1)}, u32[]{:S(2)}, u32[]{:S(2)}) async-start(bf16[8,104,128]{2,1,0:T(8,128)(2,1)} %shard_map.64), calls=%async_computation | async-start | bytes 425984 | tf_op jit(solution)/shard_map/all_to_all | solution.py:237
  12.0 0.0 copy-start.2
  12.0 3.2 %shard_map.65 = bf16[8,16,1280]{2,1,0:T(8,128)(2,1)} custom-call(bf16[256,512]{1,0:T(8,128)(2,1)} %bitcast.10, bf16[2,512,512]{2,1,0:T(8,128)(2,1)} %conv_hbm.1, bf16[512,1280]{1,0:T(8,128)(2,1)} %proj_hbm.1), custom_call_target="tpu_custom_call" | custom-call | tf_op jit(solution)/shard_map/pallas_call | solution.py:239
  15.2 7.7 %all-to-all-done.refs_0_ = bf16[8,104,128]{2,1,0:T(8,128)(2,1)} async-done(((bf16[8,104,128]{2,1,0:T(8,128)(2,1)}), bf16[8,104,128]{2,1,0:T(8,128)(2,1)}, u32[]{:S(2)}, u32[]{:S(2)}) %all-to-all-start) | async-done | bytes 213024 | tf_op jit(solution)/shard_map/all_to_all | solution.py:237
  22.9 4.8 %all-to-all-start.1 = ((bf16[8,16,1280]{2,1,0:T(8,128)(2,1)}), bf16[8,16,1280]{2,1,0:T(8,128)(2,1)S(1)}, u32[]{:S(2)}, u32[]{:S(2)}) async-start(bf16[8,16,1280]{2,1,0:T(8,128)(2,1)} %shard_map.65), calls=%async_computation.1 | async-start | bytes 655360 | tf_op jit(solution)/shard_map/all_to_all | solution.py:254
  27.7 5.3 %collective-permute-start.1 = (bf16[8,104,128]{2,1,0:T(8,128)(2,1)}, bf16[8,104,128]{2,1,0:T(8,128)(2,1)S(1)}, u32[]{:S(2)}, u32[]{:S(2)}) collective-permute-start(bf16[8,104,128]{2,1,0:T(8,128)(2,1)} %all-to-all-done.refs_0_), channel_id=1, source_target_pairs={{0,384},{8,392},{16,400},{24,408},{32,416},{40,424},{48,432},{56,4... | collective-permute-start | bytes 638984 | tf_op jit(solution)/shard_map/ppermute | solution.py:212
  33.0 1.9 %collective-permute-start = (bf16[8,104,128]{2,1,0:T(8,128)(2,1)}, bf16[8,104,128]{2,1,0:T(8,128)(2,1)S(1)}, u32[]{:S(2)}, u32[]{:S(2)}) collective-permute-start(bf16[8,104,128]{2,1,0:T(8,128)(2,1)} %all-to-all-done.refs_0_), channel_id=1, source_target_pairs={{0,128},{8,136},{16,144},{24,152},{32,160},{40,168},{48,176},{56,1... | collective-permute-start | bytes 638984 | tf_op jit(solution)/shard_map/ppermute | solution.py:212
  34.9 0.0 all-to-all-done.1
  34.9 0.0 copy-done.1
  35.0 1.9 %shard_map.66 = bf16[512,320]{1,0:T(8,128)(2,1)} custom-call(s32[1,128]{1,0:T(1,128)S(1)} %bitcast.9, bf16[128,1280]{1,0:T(8,128)(2,1)S(1)} %bitcast.8), custom_call_target="tpu_custom_call" | custom-call | tf_op jit(solution)/shard_map/pallas_call | solution.py:256
  36.9 4.8 %collective-permute-done.1.refs_3_ = bf16[8,104,128]{2,1,0:T(8,128)(2,1)S(1)} collective-permute-done((bf16[8,104,128]{2,1,0:T(8,128)(2,1)}, bf16[8,104,128]{2,1,0:T(8,128)(2,1)S(1)}, u32[]{:S(2)}, u32[]{:S(2)}) %collective-permute-start.1) | collective-permute-done | bytes 213024 | tf_op jit(solution)/shard_map/ppermute | solution.py:212
  41.7 7.1 %collective-permute-done.refs_2_ = bf16[8,104,128]{2,1,0:T(8,128)(2,1)S(1)} collective-permute-done((bf16[8,104,128]{2,1,0:T(8,128)(2,1)}, bf16[8,104,128]{2,1,0:T(8,128)(2,1)S(1)}, u32[]{:S(2)}, u32[]{:S(2)}) %collective-permute-start) | collective-permute-done | bytes 213024 | tf_op jit(solution)/shard_map/ppermute | solution.py:212
  48.8 5.2 %all-to-all-start.2 = ((bf16[64,8,320]{2,1,0:T(8,128)(2,1)}), bf16[64,8,320]{2,1,0:T(8,128)(2,1)S(1)}, u32[]{:S(2)}, u32[]{:S(2)}) async-start(bf16[64,8,320]{2,1,0:T(8,128)(2,1)} %bitcast.4), calls=%async_computation.2 | async-start | bytes 786432 | tf_op jit(solution)/shard_map/all_to_all | solution.py:267
  54.0 2.4 %collective-permute-start.3 = (bf16[8,104,128]{2,1,0:T(8,128)(2,1)}, bf16[8,104,128]{2,1,0:T(8,128)(2,1)S(1)}, u32[]{:S(2)}, u32[]{:S(2)}) collective-permute-start(bf16[8,104,128]{2,1,0:T(8,128)(2,1)} %all-to-all-done.refs_0_), channel_id=1, source_target_pairs={{0,448},{8,456},{16,464},{24,472},{32,480},{40,488},{48,496},{56,5... | collective-permute-start | bytes 638984 | tf_op jit(solution)/shard_map/ppermute | solution.py:212
  56.4 3.5 %collective-permute-start.2 = (bf16[8,104,128]{2,1,0:T(8,128)(2,1)}, bf16[8,104,128]{2,1,0:T(8,128)(2,1)S(1)}, u32[]{:S(2)}, u32[]{:S(2)}) collective-permute-start(bf16[8,104,128]{2,1,0:T(8,128)(2,1)} %all-to-all-done.refs_0_), channel_id=1, source_target_pairs={{0,64},{8,72},{16,80},{24,88},{32,96},{40,104},{48,112},{56,120},{... | collective-permute-start | bytes 638984 | tf_op jit(solution)/shard_map/ppermute | solution.py:212
  59.9 3.4 %collective-permute-start.4 = (bf16[8,104,128]{2,1,0:T(8,128)(2,1)S(1)}, bf16[8,104,128]{2,1,0:T(8,128)(2,1)S(1)}, u32[]{:S(2)}, u32[]{:S(2)}) collective-permute-start(bf16[8,104,128]{2,1,0:T(8,128)(2,1)S(1)} %collective-permute-done.refs_2_), channel_id=1, source_target_pairs={{0,64},{8,72},{16,80},{24,88},{32,96},{40,104},{48,112},{56,120},{... | collective-permute-start | bytes 638984 | tf_op jit(solution)/shard_map/ppermute | solution.py:212
  63.3 2.5 %collective-permute-start.7 = (bf16[8,104,128]{2,1,0:T(8,128)(2,1)S(1)}, bf16[8,104,128]{2,1,0:T(8,128)(2,1)S(1)}, u32[]{:S(2)}, u32[]{:S(2)}) collective-permute-start(bf16[8,104,128]{2,1,0:T(8,128)(2,1)S(1)} %collective-permute-done.1.refs_3_), channel_id=1, source_target_pairs={{0,448},{8,456},{16,464},{24,472},{32,480},{40,488},{48,496},{56,5... | collective-permute-start | bytes 638984 | tf_op jit(solution)/shard_map/ppermute | solution.py:212
  65.8 6.1 %collective-permute-start.6 = (bf16[4,104,128]{2,1,0:T(8,128)(2,1)S(1)}, bf16[4,104,128]{2,1,0:T(8,128)(2,1)S(1)}, u32[]{:S(2)}, u32[]{:S(2)}) collective-permute-start(bf16[4,104,128]{2,1,0:T(8,128)(2,1)S(1)} %slice.7), channel_id=1, source_target_pairs={{0,384},{8,392},{16,400},{24,408},{32,416},{40,424},{48,432},{56,4... | collective-permute-start | bytes 319496 | tf_op jit(solution)/shard_map/ppermute | solution.py:212
  71.8 0.0 collective-permute-done.3.refs_4_
  71.8 2.8 %collective-permute-start.5 = (bf16[4,104,128]{2,1,0:T(8,128)(2,1)S(1)}, bf16[4,104,128]{2,1,0:T(8,128)(2,1)S(1)}, u32[]{:S(2)}, u32[]{:S(2)}) collective-permute-start(bf16[4,104,128]{2,1,0:T(8,128)(2,1)S(1)} %slice.6), channel_id=1, source_target_pairs={{0,128},{8,136},{16,144},{24,152},{32,160},{40,168},{48,176},{56,1... | collective-permute-start | bytes 319496 | tf_op jit(solution)/shard_map/ppermute | solution.py:212
  74.7 0.0 all-to-all-done.2
  74.7 0.0 copy-done.2
  74.7 2.0 %shard_map.67 = (bf16[2,704,768]{2,1,0:T(8,128)(2,1)S(1)}, f32[2,512,80]{2,1,0:T(8,128)S(1)}) custom-call(s32[1]{0:T(128)} %bitcast.owner_ref, s32[128]{0:T(128)S(1)} %copy-done.1, s32[128]{0:T(128)S(1)} %copy-done.2, bf16[512,320]{1,0:T(8,128)(2,1)S(1)} %bitcast.7), custom_call_target="tpu_custom_call" | custom-call | tf_op jit(solution)/shard_map/pallas_call | solution.py:275
  76.7 0.0 collective-permute-done.2.refs_1_
  76.7 2.4 %shard_map.68.refs_0_ = f32[592,256]{1,0:T(8,128)S(1)} custom-call(s32[1]{0:T(128)} %bitcast.owner_ref, bf16[2,704,768]{2,1,0:T(8,128)(2,1)S(1)} %get-tuple-element.18.shifted_ref, bf16[8,104,128]{2,1,0:T(8,128)(2,1)} %all-to-all-done.refs_0_, bf16[8,104,128]{2,1,0:T(8,128)(2,1)S(1)} %collective-permute-done.2.refs_1_, ...), custom_call_target="tpu_custom_call" | custom-call | tf_op jit(solution)/shard_map/pallas_call | solution.py:287
  79.1 0.0 collective-permute-done.6.refs_3_.refs_7_
  79.1 2.6 %collective-permute-done.5.refs_2_.refs_6_ = bf16[4,104,128]{2,1,0:T(8,128)(2,1)S(1)} collective-permute-done((bf16[4,104,128]{2,1,0:T(8,128)(2,1)S(1)}, bf16[4,104,128]{2,1,0:T(8,128)(2,1)S(1)}, u32[]{:S(2)}, u32[]{:S(2)}) %collective-permute-start.5) | collective-permute-done | bytes 106528 | tf_op jit(solution)/shard_map/ppermute | solution.py:212
  81.7 0.0 collective-permute-done.4.refs_1_.refs_5_
  81.7 0.0 collective-permute-done.7.refs_4_.refs_8_
  81.7 1.8 %shard_map.69 = bf16[80,512]{1,0:T(8,128)(2,1)S(1)} custom-call(s32[1]{0:T(128)} %bitcast.owner_ref, s32[128]{0:T(128)S(1)} %copy-done.1, s32[128]{0:T(128)S(1)} %copy-done.2, bf16[2,704,768]{2,1,0:T(8,128)(2,1)S(1)} %get-tuple-element.18.shifted_ref, f32[2,512,80]{2,1,0:T(8,128)S(1)} %get-tuple-element.22.packed_ref, f32[592,256]{1,0:T(8,128)S(1)} %shard_map.68.refs_0_, ...), custom_call_target="tpu_custom_call" | custom-call | tf_op jit(solution)/shard_map/pallas_call | solution.py:296
  83.5 3.4 %collective-permute-start.8 = (bf16[80,512]{1,0:T(8,128)(2,1)S(1)}, bf16[80,512]{1,0:T(8,128)(2,1)S(1)}, u32[]{:S(2)}, u32[]{:S(2)}) collective-permute-start(bf16[80,512]{1,0:T(8,128)(2,1)S(1)} %shard_map.69), channel_id=1, source_target_pairs={{0,8},{8,0},{16,24},{24,16},{32,40},{40,32},{48,56},{56,48},{64,72... | collective-permute-start | bytes 245768 | tf_op jit(solution)/shard_map/ppermute | solution.py:311
  86.9 3.9 %shard_map.70.own_hbm = bf16[160,512]{1,0:T(8,128)(2,1)} custom-call(s32[1]{0:T(128)} %bitcast.owner_ref, s32[128]{0:T(128)S(1)} %copy-done.1, s32[128]{0:T(128)S(1)} %copy-done.2, bf16[2,704,768]{2,1,0:T(8,128)(2,1)S(1)} %get-tuple-element.18.shifted_ref, f32[2,512,80]{2,1,0:T(8,128)S(1)} %get-tuple-element.22.packed_ref, ...), custom_call_target="tpu_custom_call" | custom-call | tf_op jit(solution)/shard_map/pallas_call | solution.py:296
  90.8 0.0 collective-permute-done.8.received_hbm
  90.8 0.7 shard_map.71
  (2 shorter events, 0.0 us)
Async XLA Ops:
  0.0 0.9 copy-start
  0.9 34.1 %copy-start.1 = (s32[128]{0:T(128)S(1)}, s32[128]{0:T(128)}, u32[]{:S(2)}) copy-start(s32[128]{0:T(128)} %order_ref.5) | copy-start | bytes 1540
  1.7 21.2 %all-to-all-start = ((bf16[8,104,128]{2,1,0:T(8,128)(2,1)}), bf16[8,104,128]{2,1,0:T(8,128)(2,1)}, u32[]{:S(2)}, u32[]{:S(2)}) async-start(bf16[8,104,128]{2,1,0:T(8,128)(2,1)} %shard_map.64), calls=%async_computation | async-start | bytes 425984 | tf_op jit(solution)/shard_map/all_to_all | solution.py:237
  12.0 62.7 %copy-start.2 = (s32[128]{0:T(128)S(1)}, s32[128]{0:T(128)}, u32[]{:S(2)}) copy-start(s32[128]{0:T(128)} %len_ref.5) | copy-start | bytes 1540
  22.9 12.0 %all-to-all-start.1 = ((bf16[8,16,1280]{2,1,0:T(8,128)(2,1)}), bf16[8,16,1280]{2,1,0:T(8,128)(2,1)S(1)}, u32[]{:S(2)}, u32[]{:S(2)}) async-start(bf16[8,16,1280]{2,1,0:T(8,128)(2,1)} %shard_map.65), calls=%async_computation.1 | async-start | bytes 655360 | tf_op jit(solution)/shard_map/all_to_all | solution.py:254
  27.7 13.9 %collective-permute-start.1 = (bf16[8,104,128]{2,1,0:T(8,128)(2,1)}, bf16[8,104,128]{2,1,0:T(8,128)(2,1)S(1)}, u32[]{:S(2)}, u32[]{:S(2)}) collective-permute-start(bf16[8,104,128]{2,1,0:T(8,128)(2,1)} %all-to-all-done.refs_0_), channel_id=1, source_target_pairs={{0,384},{8,392},{16,400},{24,408},{32,416},{40,424},{48,432},{56,4... | collective-permute-start | bytes 638984 | tf_op jit(solution)/shard_map/ppermute | solution.py:212
  33.0 15.8 %collective-permute-start = (bf16[8,104,128]{2,1,0:T(8,128)(2,1)}, bf16[8,104,128]{2,1,0:T(8,128)(2,1)S(1)}, u32[]{:S(2)}, u32[]{:S(2)}) collective-permute-start(bf16[8,104,128]{2,1,0:T(8,128)(2,1)} %all-to-all-done.refs_0_), channel_id=1, source_target_pairs={{0,128},{8,136},{16,144},{24,152},{32,160},{40,168},{48,176},{56,1... | collective-permute-start | bytes 638984 | tf_op jit(solution)/shard_map/ppermute | solution.py:212
  48.8 25.9 %all-to-all-start.2 = ((bf16[64,8,320]{2,1,0:T(8,128)(2,1)}), bf16[64,8,320]{2,1,0:T(8,128)(2,1)S(1)}, u32[]{:S(2)}, u32[]{:S(2)}) async-start(bf16[64,8,320]{2,1,0:T(8,128)(2,1)} %bitcast.4), calls=%async_computation.2 | async-start | bytes 786432 | tf_op jit(solution)/shard_map/all_to_all | solution.py:267
  54.0 17.8 %collective-permute-start.3 = (bf16[8,104,128]{2,1,0:T(8,128)(2,1)}, bf16[8,104,128]{2,1,0:T(8,128)(2,1)S(1)}, u32[]{:S(2)}, u32[]{:S(2)}) collective-permute-start(bf16[8,104,128]{2,1,0:T(8,128)(2,1)} %all-to-all-done.refs_0_), channel_id=1, source_target_pairs={{0,448},{8,456},{16,464},{24,472},{32,480},{40,488},{48,496},{56,5... | collective-permute-start | bytes 638984 | tf_op jit(solution)/shard_map/ppermute | solution.py:212
  56.4 20.3 %collective-permute-start.2 = (bf16[8,104,128]{2,1,0:T(8,128)(2,1)}, bf16[8,104,128]{2,1,0:T(8,128)(2,1)S(1)}, u32[]{:S(2)}, u32[]{:S(2)}) collective-permute-start(bf16[8,104,128]{2,1,0:T(8,128)(2,1)} %all-to-all-done.refs_0_), channel_id=1, source_target_pairs={{0,64},{8,72},{16,80},{24,88},{32,96},{40,104},{48,112},{56,120},{... | collective-permute-start | bytes 638984 | tf_op jit(solution)/shard_map/ppermute | solution.py:212
  59.9 21.8 %collective-permute-start.4 = (bf16[8,104,128]{2,1,0:T(8,128)(2,1)S(1)}, bf16[8,104,128]{2,1,0:T(8,128)(2,1)S(1)}, u32[]{:S(2)}, u32[]{:S(2)}) collective-permute-start(bf16[8,104,128]{2,1,0:T(8,128)(2,1)S(1)} %collective-permute-done.refs_2_), channel_id=1, source_target_pairs={{0,64},{8,72},{16,80},{24,88},{32,96},{40,104},{48,112},{56,120},{... | collective-permute-start | bytes 638984 | tf_op jit(solution)/shard_map/ppermute | solution.py:212
  63.3 18.4 %collective-permute-start.7 = (bf16[8,104,128]{2,1,0:T(8,128)(2,1)S(1)}, bf16[8,104,128]{2,1,0:T(8,128)(2,1)S(1)}, u32[]{:S(2)}, u32[]{:S(2)}) collective-permute-start(bf16[8,104,128]{2,1,0:T(8,128)(2,1)S(1)} %collective-permute-done.1.refs_3_), channel_id=1, source_target_pairs={{0,448},{8,456},{16,464},{24,472},{32,480},{40,488},{48,496},{56,5... | collective-permute-start | bytes 638984 | tf_op jit(solution)/shard_map/ppermute | solution.py:212
  65.8 13.3 %collective-permute-start.6 = (bf16[4,104,128]{2,1,0:T(8,128)(2,1)S(1)}, bf16[4,104,128]{2,1,0:T(8,128)(2,1)S(1)}, u32[]{:S(2)}, u32[]{:S(2)}) collective-permute-start(bf16[4,104,128]{2,1,0:T(8,128)(2,1)S(1)} %slice.7), channel_id=1, source_target_pairs={{0,384},{8,392},{16,400},{24,408},{32,416},{40,424},{48,432},{56,4... | collective-permute-start | bytes 319496 | tf_op jit(solution)/shard_map/ppermute | solution.py:212
  71.8 9.8 %collective-permute-start.5 = (bf16[4,104,128]{2,1,0:T(8,128)(2,1)S(1)}, bf16[4,104,128]{2,1,0:T(8,128)(2,1)S(1)}, u32[]{:S(2)}, u32[]{:S(2)}) collective-permute-start(bf16[4,104,128]{2,1,0:T(8,128)(2,1)S(1)} %slice.6), channel_id=1, source_target_pairs={{0,128},{8,136},{16,144},{24,152},{32,160},{40,168},{48,176},{56,1... | collective-permute-start | bytes 319496 | tf_op jit(solution)/shard_map/ppermute | solution.py:212
  83.5 7.3 %collective-permute-start.8 = (bf16[80,512]{1,0:T(8,128)(2,1)S(1)}, bf16[80,512]{1,0:T(8,128)(2,1)S(1)}, u32[]{:S(2)}, u32[]{:S(2)}) collective-permute-start(bf16[80,512]{1,0:T(8,128)(2,1)S(1)} %shard_map.69), channel_id=1, source_target_pairs={{0,8},{8,0},{16,24},{24,16},{32,40},{40,32},{48,56},{56,48},{64,72... | collective-permute-start | bytes 245768 | tf_op jit(solution)/shard_map/ppermute | solution.py:311

commit v6 on v5

--- a/solution.py
+++ b/solution.py
@@ -260,9 +260,12 @@
         out_specs=VMEM,
         compiler_params=params,
     )(pack_order.reshape(1, -1), spread.reshape(parts * utts, frames * width))
-    two, minus_two, ordered = lax.optimization_barrier((two, minus_two, ordered))
+    low, high = two[: ring // 2], minus_two[ring // 2 :]
+    low, high, two, minus_two, one, minus_one, ordered = lax.optimization_barrier(
+        (low, high, two, minus_two, one, minus_one, ordered)
+    )
+    low, high = send(low, ring, 2), send(high, ring, -2)
     three, minus_three = send(two, ring, 1), send(minus_two, ring, -1)
-    low, high = send(two[: ring // 2], ring, 2), send(minus_two[ring // 2 :], ring, -2)
     early_taps, late_taps = (taps, one, two, minus_two, minus_one), (three, low, high, minus_three)
     pair_rows = lax.all_to_all(
         ordered.reshape(owners, 8, 2 * width), "dp", split_axis=0, concat_axis=0, tiled=True

time: 92.2 us -> 91.3 us (level)
  the two profiles are of different devices: /device:TPU:10 before, /device:TPU:18 now
where the time goes in v6:
time: 91.3 us; the launch traced here: 90.6 us
  starting transfers between devices  55.4 us (61%)
  waiting for transfers between devices  17.5 us (19%)
  Pallas kernels  16.7 us (18%)
    ppermute x8, starting transfers between devices, send(): lax.ppermute(values, 'dp', [(o, (o + step * ring) % (ring * ring)) for o...  28.3 us
    all_to_all x1, starting transfers between devices, shards(): lax.all_to_all(tap_copies, 'dp', 0, 0, axis_index_groups=along_z, tiled=T...  10.4 us
    all_to_all x1, starting transfers between devices, shards(): lax.all_to_all(ordered.reshape(owners, 8, 2 * width), 'dp', split_axis=0,...  8.39 us
    all_to_all x1, waiting for transfers between devices, shards(): lax.all_to_all(tap_copies, 'dp', 0, 0, axis_index_groups=along_z, tiled=T...  7.7 us
    ppermute x8, waiting for transfers between devices, send(): lax.ppermute(values, 'dp', [(o, (o + step * ring) % (ring * ring)) for o...  7.56 us
    pallas_call x2, Pallas kernels, convolve(): pl.pallas_call(functools.partial(positional_kernel, swap, ring, distances...  5.73 us
    all_to_all x1, starting transfers between devices, shards(): spread = lax.all_to_all(sent, 'mp', split_axis=0, concat_axis=0, tiled=True)  4.83 us
    ppermute x1, starting transfers between devices, shards(): received = lax.ppermute(other, 'dp', [(o, o ^ 1) for o in range(owners)])  3.37 us
  transfers between devices with their start and end apart: 12, of which 7 were waited for; matrix products, arithmetic and copies ran while one was open for 0% of the time, Pallas kernels for 15%

profile of v6, /device:TPU:18, one launch (start us, length us, event | category | flops | bytes accessed | tf_op | source)
XLA Modules:
  0.0 90.6 jit_solution(911036057223432211)
XLA Ops:
  0.0 0.0 copy-start
  0.0 0.9 copy-done
  0.9 0.8 shard_map.64
  1.7 0.0 copy-start.1
  1.7 10.4 %all-to-all-start = ((bf16[8,104,128]{2,1,0:T(8,128)(2,1)}), bf16[8,104,128]{2,1,0:T(8,128)(2,1)}, u32[]{:S(2)}, u32[]{:S(2)}) async-start(bf16[8,104,128]{2,1,0:T(8,128)(2,1)} %shard_map.64), calls=%async_computation | async-start | bytes 425984 | tf_op jit(solution)/shard_map/all_to_all | solution.py:237
  12.1 0.0 copy-start.2
  12.1 3.2 %shard_map.65 = bf16[8,16,1280]{2,1,0:T(8,128)(2,1)} custom-call(bf16[256,512]{1,0:T(8,128)(2,1)} %bitcast.10, bf16[2,512,512]{2,1,0:T(8,128)(2,1)} %conv_hbm.1, bf16[512,1280]{1,0:T(8,128)(2,1)} %proj_hbm.1), custom_call_target="tpu_custom_call" | custom-call | tf_op jit(solution)/shard_map/pallas_call | solution.py:239
  15.3 7.7 %all-to-all-done.refs_0_ = bf16[8,104,128]{2,1,0:T(8,128)(2,1)} async-done(((bf16[8,104,128]{2,1,0:T(8,128)(2,1)}), bf16[8,104,128]{2,1,0:T(8,128)(2,1)}, u32[]{:S(2)}, u32[]{:S(2)}) %all-to-all-start) | async-done | bytes 213024 | tf_op jit(solution)/shard_map/all_to_all | solution.py:237
  23.0 4.8 %all-to-all-start.1 = ((bf16[8,16,1280]{2,1,0:T(8,128)(2,1)}), bf16[8,16,1280]{2,1,0:T(8,128)(2,1)S(1)}, u32[]{:S(2)}, u32[]{:S(2)}) async-start(bf16[8,16,1280]{2,1,0:T(8,128)(2,1)} %shard_map.65), calls=%async_computation.1 | async-start | bytes 655360 | tf_op jit(solution)/shard_map/all_to_all | solution.py:254
  27.9 2.2 %collective-permute-start.1 = (bf16[8,104,128]{2,1,0:T(8,128)(2,1)}, bf16[8,104,128]{2,1,0:T(8,128)(2,1)S(1)}, u32[]{:S(2)}, u32[]{:S(2)}) collective-permute-start(bf16[8,104,128]{2,1,0:T(8,128)(2,1)} %all-to-all-done.refs_0_), channel_id=1, source_target_pairs={{0,384},{8,392},{16,400},{24,408},{32,416},{40,424},{48,432},{56,4... | collective-permute-start | bytes 638984 | tf_op jit(solution)/shard_map/ppermute | solution.py:212
  30.1 5.7 %collective-permute-start = (bf16[8,104,128]{2,1,0:T(8,128)(2,1)}, bf16[8,104,128]{2,1,0:T(8,128)(2,1)S(1)}, u32[]{:S(2)}, u32[]{:S(2)}) collective-permute-start(bf16[8,104,128]{2,1,0:T(8,128)(2,1)} %all-to-all-done.refs_0_), channel_id=1, source_target_pairs={{0,128},{8,136},{16,144},{24,152},{32,160},{40,168},{48,176},{56,1... | collective-permute-start | bytes 638984 | tf_op jit(solution)/shard_map/ppermute | solution.py:212
  35.8 1.9 %collective-permute-start.3 = (bf16[8,104,128]{2,1,0:T(8,128)(2,1)}, bf16[8,104,128]{2,1,0:T(8,128)(2,1)S(1)}, u32[]{:S(2)}, u32[]{:S(2)}) collective-permute-start(bf16[8,104,128]{2,1,0:T(8,128)(2,1)} %all-to-all-done.refs_0_), channel_id=1, source_target_pairs={{0,448},{8,456},{16,464},{24,472},{32,480},{40,488},{48,496},{56,5... | collective-permute-start | bytes 638984 | tf_op jit(solution)/shard_map/ppermute | solution.py:212
  37.8 3.9 %collective-permute-start.2 = (bf16[8,104,128]{2,1,0:T(8,128)(2,1)}, bf16[8,104,128]{2,1,0:T(8,128)(2,1)S(1)}, u32[]{:S(2)}, u32[]{:S(2)}) collective-permute-start(bf16[8,104,128]{2,1,0:T(8,128)(2,1)} %all-to-all-done.refs_0_), channel_id=1, source_target_pairs={{0,64},{8,72},{16,80},{24,88},{32,96},{40,104},{48,112},{56,120},{... | collective-permute-start | bytes 638984 | tf_op jit(solution)/shard_map/ppermute | solution.py:212
  41.7 3.0 %collective-permute-done.1.refs_3_ = bf16[8,104,128]{2,1,0:T(8,128)(2,1)S(1)} collective-permute-done((bf16[8,104,128]{2,1,0:T(8,128)(2,1)}, bf16[8,104,128]{2,1,0:T(8,128)(2,1)S(1)}, u32[]{:S(2)}, u32[]{:S(2)}) %collective-permute-start.1) | collective-permute-done | bytes 213024 | tf_op jit(solution)/shard_map/ppermute | solution.py:212
  44.8 0.3 collective-permute-done.refs_2_
  45.1 0.0 all-to-all-done.1
  45.1 0.0 copy-done.1
  45.1 1.9 %shard_map.66 = bf16[512,320]{1,0:T(8,128)(2,1)} custom-call(s32[1,128]{1,0:T(1,128)S(1)} %bitcast.9, bf16[128,1280]{1,0:T(8,128)(2,1)S(1)} %bitcast.8), custom_call_target="tpu_custom_call" | custom-call | tf_op jit(solution)/shard_map/pallas_call | solution.py:256
  47.1 0.7 collective-permute-done.3.refs_4_
  47.7 2.5 %collective-permute-done.2.refs_1_ = bf16[8,104,128]{2,1,0:T(8,128)(2,1)S(1)} collective-permute-done((bf16[8,104,128]{2,1,0:T(8,128)(2,1)}, bf16[8,104,128]{2,1,0:T(8,128)(2,1)S(1)}, u32[]{:S(2)}, u32[]{:S(2)}) %collective-permute-start.2) | collective-permute-done | bytes 213024 | tf_op jit(solution)/shard_map/ppermute | solution.py:212
  50.2 8.4 %all-to-all-start.2 = ((bf16[64,8,320]{2,1,0:T(8,128)(2,1)}), bf16[64,8,320]{2,1,0:T(8,128)(2,1)S(1)}, u32[]{:S(2)}, u32[]{:S(2)}) async-start(bf16[64,8,320]{2,1,0:T(8,128)(2,1)} %bitcast.4), calls=%async_computation.2 | async-start | bytes 786432 | tf_op jit(solution)/shard_map/all_to_all | solution.py:270
  58.6 3.4 %collective-permute-start.4 = (bf16[8,104,128]{2,1,0:T(8,128)(2,1)S(1)}, bf16[8,104,128]{2,1,0:T(8,128)(2,1)S(1)}, u32[]{:S(2)}, u32[]{:S(2)}) collective-permute-start(bf16[8,104,128]{2,1,0:T(8,128)(2,1)S(1)} %collective-permute-done.refs_2_), channel_id=1, source_target_pairs={{0,64},{8,72},{16,80},{24,88},{32,96},{40,104},{48,112},{56,120},{... | collective-permute-start | bytes 638984 | tf_op jit(solution)/shard_map/ppermute | solution.py:212
  62.0 2.4 %collective-permute-start.7 = (bf16[8,104,128]{2,1,0:T(8,128)(2,1)S(1)}, bf16[8,104,128]{2,1,0:T(8,128)(2,1)S(1)}, u32[]{:S(2)}, u32[]{:S(2)}) collective-permute-start(bf16[8,104,128]{2,1,0:T(8,128)(2,1)S(1)} %collective-permute-done.1.refs_3_), channel_id=1, source_target_pairs={{0,448},{8,456},{16,464},{24,472},{32,480},{40,488},{48,496},{56,5... | collective-permute-start | bytes 638984 | tf_op jit(solution)/shard_map/ppermute | solution.py:212
  64.5 6.8 %collective-permute-start.5 = (bf16[4,104,128]{2,1,0:T(8,128)(2,1)S(1)}, bf16[4,104,128]{2,1,0:T(8,128)(2,1)S(1)}, u32[]{:S(2)}, u32[]{:S(2)}) collective-permute-start(bf16[4,104,128]{2,1,0:T(8,128)(2,1)S(1)} %slice.8), channel_id=1, source_target_pairs={{0,128},{8,136},{16,144},{24,152},{32,160},{40,168},{48,176},{56,1... | collective-permute-start | bytes 319496 | tf_op jit(solution)/shard_map/ppermute | solution.py:212
  71.3 1.9 %collective-permute-start.6 = (bf16[4,104,128]{2,1,0:T(8,128)(2,1)S(1)}, bf16[4,104,128]{2,1,0:T(8,128)(2,1)S(1)}, u32[]{:S(2)}, u32[]{:S(2)}) collective-permute-start(bf16[4,104,128]{2,1,0:T(8,128)(2,1)S(1)} %slice.9), channel_id=1, source_target_pairs={{0,384},{8,392},{16,400},{24,408},{32,416},{40,424},{48,432},{56,4... | collective-permute-start | bytes 319496 | tf_op jit(solution)/shard_map/ppermute | solution.py:212
  73.2 2.2 %all-to-all-done.2 = bf16[64,8,320]{2,1,0:T(8,128)(2,1)S(1)} async-done(((bf16[64,8,320]{2,1,0:T(8,128)(2,1)}), bf16[64,8,320]{2,1,0:T(8,128)(2,1)S(1)}, u32[]{:S(2)}, u32[]{:S(2)}) %all-to-all-start.2) | async-done | bytes 327712 | tf_op jit(solution)/shard_map/all_to_all | solution.py:270
  75.4 0.0 copy-done.2
  75.4 2.0 %shard_map.67 = (bf16[2,704,768]{2,1,0:T(8,128)(2,1)S(1)}, f32[2,512,80]{2,1,0:T(8,128)S(1)}) custom-call(s32[1]{0:T(128)} %bitcast.owner_ref, s32[128]{0:T(128)S(1)} %copy-done.1, s32[128]{0:T(128)S(1)} %copy-done.2, bf16[512,320]{1,0:T(8,128)(2,1)S(1)} %bitcast.7), custom_call_target="tpu_custom_call" | custom-call | tf_op jit(solution)/shard_map/pallas_call | solution.py:278
  77.4 2.4 %shard_map.68.refs_0_ = f32[592,256]{1,0:T(8,128)S(1)} custom-call(s32[1]{0:T(128)} %bitcast.owner_ref, bf16[2,704,768]{2,1,0:T(8,128)(2,1)S(1)} %get-tuple-element.22.shifted_ref, bf16[8,104,128]{2,1,0:T(8,128)(2,1)} %all-to-all-done.refs_0_, bf16[8,104,128]{2,1,0:T(8,128)(2,1)S(1)} %collective-permute-done.2.refs_1_, ...), custom_call_target="tpu_custom_call" | custom-call | tf_op jit(solution)/shard_map/pallas_call | solution.py:290
  79.8 0.0 collective-permute-done.5.refs_2_.refs_6_
  79.8 1.0 %collective-permute-done.6.refs_3_.refs_7_ = bf16[4,104,128]{2,1,0:T(8,128)(2,1)S(1)} collective-permute-done((bf16[4,104,128]{2,1,0:T(8,128)(2,1)S(1)}, bf16[4,104,128]{2,1,0:T(8,128)(2,1)S(1)}, u32[]{:S(2)}, u32[]{:S(2)}) %collective-permute-start.6) | collective-permute-done | bytes 106528 | tf_op jit(solution)/shard_map/ppermute | solution.py:212
  80.8 0.0 collective-permute-done.4.refs_1_.refs_5_
  80.8 0.0 collective-permute-done.7.refs_4_.refs_8_
  80.8 1.8 %shard_map.69 = bf16[80,512]{1,0:T(8,128)(2,1)S(1)} custom-call(s32[1]{0:T(128)} %bitcast.owner_ref, s32[128]{0:T(128)S(1)} %copy-done.1, s32[128]{0:T(128)S(1)} %copy-done.2, bf16[2,704,768]{2,1,0:T(8,128)(2,1)S(1)} %get-tuple-element.22.shifted_ref, f32[2,512,80]{2,1,0:T(8,128)S(1)} %get-tuple-element.30.packed_ref, f32[592,256]{1,0:T(8,128)S(1)} %shard_map.68.refs_0_, ...), custom_call_target="tpu_custom_call" | custom-call | tf_op jit(solution)/shard_map/pallas_call | solution.py:299
  82.6 3.4 %collective-permute-start.8 = (bf16[80,512]{1,0:T(8,128)(2,1)S(1)}, bf16[80,512]{1,0:T(8,128)(2,1)S(1)}, u32[]{:S(2)}, u32[]{:S(2)}) collective-permute-start(bf16[80,512]{1,0:T(8,128)(2,1)S(1)} %shard_map.69), channel_id=1, source_target_pairs={{0,8},{8,0},{16,24},{24,16},{32,40},{40,32},{48,56},{56,48},{64,72... | collective-permute-start | bytes 245768 | tf_op jit(solution)/shard_map/ppermute | solution.py:314
  86.0 3.9 %shard_map.70.own_hbm = bf16[160,512]{1,0:T(8,128)(2,1)} custom-call(s32[1]{0:T(128)} %bitcast.owner_ref, s32[128]{0:T(128)S(1)} %copy-done.1, s32[128]{0:T(128)S(1)} %copy-done.2, bf16[2,704,768]{2,1,0:T(8,128)(2,1)S(1)} %get-tuple-element.22.shifted_ref, f32[2,512,80]{2,1,0:T(8,128)S(1)} %get-tuple-element.30.packed_ref, ...), custom_call_target="tpu_custom_call" | custom-call | tf_op jit(solution)/shard_map/pallas_call | solution.py:299
  89.9 0.0 collective-permute-done.8.received_hbm
  89.9 0.7 shard_map.71
  (2 shorter events, 0.0 us)
Async XLA Ops:
  0.0 0.9 copy-start
  1.7 43.4 %copy-start.1 = (s32[128]{0:T(128)S(1)}, s32[128]{0:T(128)}, u32[]{:S(2)}) copy-start(s32[128]{0:T(128)} %order_ref.5) | copy-start | bytes 1540
  1.7 21.4 %all-to-all-start = ((bf16[8,104,128]{2,1,0:T(8,128)(2,1)}), bf16[8,104,128]{2,1,0:T(8,128)(2,1)}, u32[]{:S(2)}, u32[]{:S(2)}) async-start(bf16[8,104,128]{2,1,0:T(8,128)(2,1)} %shard_map.64), calls=%async_computation | async-start | bytes 425984 | tf_op jit(solution)/shard_map/all_to_all | solution.py:237
  12.1 63.3 %copy-start.2 = (s32[128]{0:T(128)S(1)}, s32[128]{0:T(128)}, u32[]{:S(2)}) copy-start(s32[128]{0:T(128)} %len_ref.5) | copy-start | bytes 1540
  23.0 22.1 %all-to-all-start.1 = ((bf16[8,16,1280]{2,1,0:T(8,128)(2,1)}), bf16[8,16,1280]{2,1,0:T(8,128)(2,1)S(1)}, u32[]{:S(2)}, u32[]{:S(2)}) async-start(bf16[8,16,1280]{2,1,0:T(8,128)(2,1)} %shard_map.65), calls=%async_computation.1 | async-start | bytes 655360 | tf_op jit(solution)/shard_map/all_to_all | solution.py:254
  27.9 16.9 %collective-permute-start.1 = (bf16[8,104,128]{2,1,0:T(8,128)(2,1)}, bf16[8,104,128]{2,1,0:T(8,128)(2,1)S(1)}, u32[]{:S(2)}, u32[]{:S(2)}) collective-permute-start(bf16[8,104,128]{2,1,0:T(8,128)(2,1)} %all-to-all-done.refs_0_), channel_id=1, source_target_pairs={{0,384},{8,392},{16,400},{24,408},{32,416},{40,424},{48,432},{56,4... | collective-permute-start | bytes 638984 | tf_op jit(solution)/shard_map/ppermute | solution.py:212
  30.1 15.0 %collective-permute-start = (bf16[8,104,128]{2,1,0:T(8,128)(2,1)}, bf16[8,104,128]{2,1,0:T(8,128)(2,1)S(1)}, u32[]{:S(2)}, u32[]{:S(2)}) collective-permute-start(bf16[8,104,128]{2,1,0:T(8,128)(2,1)} %all-to-all-done.refs_0_), channel_id=1, source_target_pairs={{0,128},{8,136},{16,144},{24,152},{32,160},{40,168},{48,176},{56,1... | collective-permute-start | bytes 638984 | tf_op jit(solution)/shard_map/ppermute | solution.py:212
  35.8 11.9 %collective-permute-start.3 = (bf16[8,104,128]{2,1,0:T(8,128)(2,1)}, bf16[8,104,128]{2,1,0:T(8,128)(2,1)S(1)}, u32[]{:S(2)}, u32[]{:S(2)}) collective-permute-start(bf16[8,104,128]{2,1,0:T(8,128)(2,1)} %all-to-all-done.refs_0_), channel_id=1, source_target_pairs={{0,448},{8,456},{16,464},{24,472},{32,480},{40,488},{48,496},{56,5... | collective-permute-start | bytes 638984 | tf_op jit(solution)/shard_map/ppermute | solution.py:212
  37.8 12.4 %collective-permute-start.2 = (bf16[8,104,128]{2,1,0:T(8,128)(2,1)}, bf16[8,104,128]{2,1,0:T(8,128)(2,1)S(1)}, u32[]{:S(2)}, u32[]{:S(2)}) collective-permute-start(bf16[8,104,128]{2,1,0:T(8,128)(2,1)} %all-to-all-done.refs_0_), channel_id=1, source_target_pairs={{0,64},{8,72},{16,80},{24,88},{32,96},{40,104},{48,112},{56,120},{... | collective-permute-start | bytes 638984 | tf_op jit(solution)/shard_map/ppermute | solution.py:212
  50.2 25.2 %all-to-all-start.2 = ((bf16[64,8,320]{2,1,0:T(8,128)(2,1)}), bf16[64,8,320]{2,1,0:T(8,128)(2,1)S(1)}, u32[]{:S(2)}, u32[]{:S(2)}) async-start(bf16[64,8,320]{2,1,0:T(8,128)(2,1)} %bitcast.4), calls=%async_computation.2 | async-start | bytes 786432 | tf_op jit(solution)/shard_map/all_to_all | solution.py:270
  58.6 22.2 %collective-permute-start.4 = (bf16[8,104,128]{2,1,0:T(8,128)(2,1)S(1)}, bf16[8,104,128]{2,1,0:T(8,128)(2,1)S(1)}, u32[]{:S(2)}, u32[]{:S(2)}) collective-permute-start(bf16[8,104,128]{2,1,0:T(8,128)(2,1)S(1)} %collective-permute-done.refs_2_), channel_id=1, source_target_pairs={{0,64},{8,72},{16,80},{24,88},{32,96},{40,104},{48,112},{56,120},{... | collective-permute-start | bytes 638984 | tf_op jit(solution)/shard_map/ppermute | solution.py:212
  62.0 18.8 %collective-permute-start.7 = (bf16[8,104,128]{2,1,0:T(8,128)(2,1)S(1)}, bf16[8,104,128]{2,1,0:T(8,128)(2,1)S(1)}, u32[]{:S(2)}, u32[]{:S(2)}) collective-permute-start(bf16[8,104,128]{2,1,0:T(8,128)(2,1)S(1)} %collective-permute-done.1.refs_3_), channel_id=1, source_target_pairs={{0,448},{8,456},{16,464},{24,472},{32,480},{40,488},{48,496},{56,5... | collective-permute-start | bytes 638984 | tf_op jit(solution)/shard_map/ppermute | solution.py:212
  64.5 15.3 %collective-permute-start.5 = (bf16[4,104,128]{2,1,0:T(8,128)(2,1)S(1)}, bf16[4,104,128]{2,1,0:T(8,128)(2,1)S(1)}, u32[]{:S(2)}, u32[]{:S(2)}) collective-permute-start(bf16[4,104,128]{2,1,0:T(8,128)(2,1)S(1)} %slice.8), channel_id=1, source_target_pairs={{0,128},{8,136},{16,144},{24,152},{32,160},{40,168},{48,176},{56,1... | collective-permute-start | bytes 319496 | tf_op jit(solution)/shard_map/ppermute | solution.py:212
  71.3 9.5 %collective-permute-start.6 = (bf16[4,104,128]{2,1,0:T(8,128)(2,1)S(1)}, bf16[4,104,128]{2,1,0:T(8,128)(2,1)S(1)}, u32[]{:S(2)}, u32[]{:S(2)}) collective-permute-start(bf16[4,104,128]{2,1,0:T(8,128)(2,1)S(1)} %slice.9), channel_id=1, source_target_pairs={{0,384},{8,392},{16,400},{24,408},{32,416},{40,424},{48,432},{56,4... | collective-permute-start | bytes 319496 | tf_op jit(solution)/shard_map/ppermute | solution.py:212
  82.6 7.3 %collective-permute-start.8 = (bf16[80,512]{1,0:T(8,128)(2,1)S(1)}, bf16[80,512]{1,0:T(8,128)(2,1)S(1)}, u32[]{:S(2)}, u32[]{:S(2)}) collective-permute-start(bf16[80,512]{1,0:T(8,128)(2,1)S(1)} %shard_map.69), channel_id=1, source_target_pairs={{0,8},{8,0},{16,24},{24,16},{32,40},{40,32},{48,56},{56,48},{64,72... | collective-permute-start | bytes 245768 | tf_op jit(solution)/shard_map/ppermute | solution.py:314

commit v7 on v4

--- a/solution.py
+++ b/solution.py
@@ -247,7 +247,7 @@
             pltpu.VMEM(proj_weight.shape, jnp.bfloat16),
             pltpu.SemaphoreType.DMA((3,)),
         ],
-        compiler_params=pltpu.CompilerParams(vmem_limit_bytes=66900000),
+        compiler_params=params,
     )(features.reshape(utts * slice_rows, channels), conv_weight, proj_weight)
     taps, sent = lax.optimization_barrier((taps, sent))
     two, minus_two, one, minus_one = [send(taps, ring, step) for step in (2, -2, 1, -1)]

time: 90.7 us -> 90.5 us (level)
  local copies, waits for them, and re-layouts: 0.91 us -> 4.4 us
  waiting for transfers between devices: 20.1 us -> 17.7 us
  Pallas kernels: 16.7 us -> 14.5 us
    unnamed x6 -> x12, local copies, waits for them, and re-layouts: 0.89 us -> 4.38 us
    all_to_all x1, waiting for transfers between devices: 7.69 us -> 4.97 us  [shards(): lax.all_to_all(tap_copies, 'dp', 0, 0, axis_index_groups=along_z, tiled=T...]
    pallas_call x1, Pallas kernels: 2.37 us -> 1.43 us  [shards(): pl.pallas_call(functools.partial(near_kernel, ring, early), out_shape=jax...]
  transfers between devices with their start and end apart: 12 -> 12, of which waited for: 4 -> 5; matrix products, arithmetic and copies ran while one was open for 0% -> 0% of each run, Pallas kernels for 15% -> 13%
where the time goes in v7:
time: 90.5 us; the launch traced here: 89.7 us
  starting transfers between devices  53 us (59%)
  waiting for transfers between devices  17.7 us (20%)
  Pallas kernels  14.5 us (16%)
  local copies, waits for them, and re-layouts  4.4 us (5%)
    ppermute x8, starting transfers between devices, send(): lax.ppermute(values, 'dp', [(o, (o + step * ring) % (ring * ring)) for o...  29 us
    all_to_all x1, starting transfers between devices, shards(): lax.all_to_all(tap_copies, 'dp', 0, 0, axis_index_groups=along_z, tiled=T...  10.3 us
    ppermute x8, waiting for transfers between devices, send(): lax.ppermute(values, 'dp', [(o, (o + step * ring) % (ring * ring)) for o...  8.82 us
    all_to_all x1, starting transfers between devices, shards(): lax.all_to_all(ordered.reshape(owners, 8, 2 * width), 'dp', split_axis=0,...  5.5 us
    pallas_call x2, Pallas kernels, convolve(): pl.pallas_call(functools.partial(positional_kernel, swap, ring, distances...  5.32 us
    all_to_all x1, waiting for transfers between devices, shards(): lax.all_to_all(tap_copies, 'dp', 0, 0, axis_index_groups=along_z, tiled=T...  4.97 us
    all_to_all x1, starting transfers between devices, shards(): spread = lax.all_to_all(sent, 'mp', split_axis=0, concat_axis=0, tiled=True)  4.83 us
    unnamed x12, local copies, waits for them, and re-layouts  4.38 us
  transfers between devices with their start and end apart: 12, of which 5 were waited for; matrix products, arithmetic and copies ran while one was open for 0% of the time, Pallas kernels for 13%

profile of v7, /device:TPU:2, one launch (start us, length us, event | category | flops | bytes accessed | tf_op | source)
XLA Modules:
  0.0 89.7 jit_solution(17606602312005670152)
XLA Ops:
  0.0 0.0 copy-start.3
  0.0 0.9 copy-done.3
  0.9 0.0 copy-start.4
  0.9 0.8 shard_map.64
  1.7 10.3 %all-to-all-start = ((bf16[8,104,128]{2,1,0:T(8,128)(2,1)}), bf16[8,104,128]{2,1,0:T(8,128)(2,1)S(1)}, u32[]{:S(2)}, u32[]{:S(2)}) async-start(bf16[8,104,128]{2,1,0:T(8,128)(2,1)} %shard_map.64), calls=%async_computation | async-start | bytes 425984 | tf_op jit(solution)/shard_map/all_to_all | solution.py:237
  12.0 0.0 copy-start
  12.0 1.3 %copy-done = bf16[512,1280]{1,0:T(8,128)(2,1)S(1)} copy-done((bf16[512,1280]{1,0:T(8,128)(2,1)S(1)}, bf16[512,1280]{1,0:T(8,128)(2,1)}, u32[]{:S(2)}) %copy-start) | copy-done | bytes 1310744
  13.3 0.0 copy-start.1
  13.3 1.2 %copy-done.1 = bf16[2,512,512]{2,1,0:T(8,128)(2,1)S(1)} copy-done((bf16[2,512,512]{2,1,0:T(8,128)(2,1)S(1)}, bf16[2,512,512]{2,1,0:T(8,128)(2,1)}, u32[]{:S(2)}) %copy-start.1) | copy-done | bytes 1048600
  14.5 0.0 copy-start.2
  14.5 0.9 %copy-done.2 = bf16[16,16,512]{2,1,0:T(8,128)(2,1)S(1)} copy-done((bf16[16,16,512]{2,1,0:T(8,128)(2,1)S(1)}, bf16[16,16,512]{2,1,0:T(8,128)(2,1)}, u32[]{:S(2)}) %copy-start.2) | copy-done | bytes 262168
  15.5 0.0 copy-start.5
  15.5 2.4 %shard_map.65 = bf16[8,16,1280]{2,1,0:T(8,128)(2,1)} custom-call(bf16[256,512]{1,0:T(8,128)(2,1)S(1)} %bitcast.9, bf16[2,512,512]{2,1,0:T(8,128)(2,1)S(1)} %copy-done.1, bf16[512,1280]{1,0:T(8,128)(2,1)S(1)} %copy-done), custom_call_target="tpu_custom_call" | custom-call | tf_op jit(solution)/shard_map/pallas_call | solution.py:239
  17.8 5.0 %all-to-all-done.refs_0_ = bf16[8,104,128]{2,1,0:T(8,128)(2,1)S(1)} async-done(((bf16[8,104,128]{2,1,0:T(8,128)(2,1)}), bf16[8,104,128]{2,1,0:T(8,128)(2,1)S(1)}, u32[]{:S(2)}, u32[]{:S(2)}) %all-to-all-start) | async-done | bytes 213024 | tf_op jit(solution)/shard_map/all_to_all | solution.py:237
  22.8 4.8 %all-to-all-start.1 = ((bf16[8,16,1280]{2,1,0:T(8,128)(2,1)}), bf16[8,16,1280]{2,1,0:T(8,128)(2,1)S(1)}, u32[]{:S(2)}, u32[]{:S(2)}) async-start(bf16[8,16,1280]{2,1,0:T(8,128)(2,1)} %shard_map.65), calls=%async_computation.1 | async-start | bytes 655360 | tf_op jit(solution)/shard_map/all_to_all | solution.py:254
  27.6 6.2 %collective-permute-start.3 = (bf16[8,104,128]{2,1,0:T(8,128)(2,1)S(1)}, bf16[8,104,128]{2,1,0:T(8,128)(2,1)S(1)}, u32[]{:S(2)}, u32[]{:S(2)}) collective-permute-start(bf16[8,104,128]{2,1,0:T(8,128)(2,1)S(1)} %all-to-all-done.refs_0_), channel_id=1, source_target_pairs={{0,384},{8,392},{16,400},{24,408},{32,416},{40,424},{48,432},{56,4... | collective-permute-start | bytes 638984 | tf_op jit(solution)/shard_map/ppermute | solution.py:212
  33.8 1.9 %collective-permute-start.2 = (bf16[8,104,128]{2,1,0:T(8,128)(2,1)S(1)}, bf16[8,104,128]{2,1,0:T(8,128)(2,1)S(1)}, u32[]{:S(2)}, u32[]{:S(2)}) collective-permute-start(bf16[8,104,128]{2,1,0:T(8,128)(2,1)S(1)} %all-to-all-done.refs_0_), channel_id=1, source_target_pairs={{0,128},{8,136},{16,144},{24,152},{32,160},{40,168},{48,176},{56,1... | collective-permute-start | bytes 638984 | tf_op jit(solution)/shard_map/ppermute | solution.py:212
  35.7 5.2 %collective-permute-start.1 = (bf16[8,104,128]{2,1,0:T(8,128)(2,1)S(1)}, bf16[8,104,128]{2,1,0:T(8,128)(2,1)S(1)}, u32[]{:S(2)}, u32[]{:S(2)}) collective-permute-start(bf16[8,104,128]{2,1,0:T(8,128)(2,1)S(1)} %all-to-all-done.refs_0_), channel_id=1, source_target_pairs={{0,448},{8,456},{16,464},{24,472},{32,480},{40,488},{48,496},{56,5... | collective-permute-start | bytes 638984 | tf_op jit(solution)/shard_map/ppermute | solution.py:212
  41.0 1.9 %collective-permute-start = (bf16[8,104,128]{2,1,0:T(8,128)(2,1)S(1)}, bf16[8,104,128]{2,1,0:T(8,128)(2,1)S(1)}, u32[]{:S(2)}, u32[]{:S(2)}) collective-permute-start(bf16[8,104,128]{2,1,0:T(8,128)(2,1)S(1)} %all-to-all-done.refs_0_), channel_id=1, source_target_pairs={{0,64},{8,72},{16,80},{24,88},{32,96},{40,104},{48,112},{56,120},{... | collective-permute-start | bytes 638984 | tf_op jit(solution)/shard_map/ppermute | solution.py:212
  42.9 0.0 all-to-all-done.1
  42.9 0.0 copy-done.4
  42.9 1.9 %shard_map.66 = bf16[512,320]{1,0:T(8,128)(2,1)} custom-call(s32[1,128]{1,0:T(1,128)S(1)} %bitcast.10, bf16[128,1280]{1,0:T(8,128)(2,1)S(1)} %bitcast.8), custom_call_target="tpu_custom_call" | custom-call | tf_op jit(solution)/shard_map/pallas_call | solution.py:256
  44.9 0.0 collective-permute-done.3.refs_3_
  44.9 4.6 %collective-permute-done.2.refs_2_ = bf16[8,104,128]{2,1,0:T(8,128)(2,1)S(1)} collective-permute-done((bf16[8,104,128]{2,1,0:T(8,128)(2,1)S(1)}, bf16[8,104,128]{2,1,0:T(8,128)(2,1)S(1)}, u32[]{:S(2)}, u32[]{:S(2)}) %collective-permute-start.2) | collective-permute-done | bytes 213024 | tf_op jit(solution)/shard_map/ppermute | solution.py:212
  49.5 0.0 collective-permute-done.1.refs_4_
  49.5 3.7 %collective-permute-done.refs_1_ = bf16[8,104,128]{2,1,0:T(8,128)(2,1)S(1)} collective-permute-done((bf16[8,104,128]{2,1,0:T(8,128)(2,1)S(1)}, bf16[8,104,128]{2,1,0:T(8,128)(2,1)S(1)}, u32[]{:S(2)}, u32[]{:S(2)}) %collective-permute-start) | collective-permute-done | bytes 213024 | tf_op jit(solution)/shard_map/ppermute | solution.py:212
  53.2 5.5 %all-to-all-start.2 = ((bf16[64,8,320]{2,1,0:T(8,128)(2,1)}), bf16[64,8,320]{2,1,0:T(8,128)(2,1)S(1)}, u32[]{:S(2)}, u32[]{:S(2)}) async-start(bf16[64,8,320]{2,1,0:T(8,128)(2,1)} %bitcast.4), calls=%async_computation.2 | async-start | bytes 786432 | tf_op jit(solution)/shard_map/all_to_all | solution.py:267
  58.7 3.5 %collective-permute-start.4 = (bf16[8,104,128]{2,1,0:T(8,128)(2,1)S(1)}, bf16[8,104,128]{2,1,0:T(8,128)(2,1)S(1)}, u32[]{:S(2)}, u32[]{:S(2)}) collective-permute-start(bf16[8,104,128]{2,1,0:T(8,128)(2,1)S(1)} %collective-permute-done.2.refs_2_), channel_id=1, source_target_pairs={{0,64},{8,72},{16,80},{24,88},{32,96},{40,104},{48,112},{56,120},{... | collective-permute-start | bytes 638984 | tf_op jit(solution)/shard_map/ppermute | solution.py:212
  62.2 3.6 %collective-permute-start.7 = (bf16[8,104,128]{2,1,0:T(8,128)(2,1)S(1)}, bf16[8,104,128]{2,1,0:T(8,128)(2,1)S(1)}, u32[]{:S(2)}, u32[]{:S(2)}) collective-permute-start(bf16[8,104,128]{2,1,0:T(8,128)(2,1)S(1)} %collective-permute-done.3.refs_3_), channel_id=1, source_target_pairs={{0,448},{8,456},{16,464},{24,472},{32,480},{40,488},{48,496},{56,5... | collective-permute-start | bytes 638984 | tf_op jit(solution)/shard_map/ppermute | solution.py:212
  65.8 4.6 %collective-permute-start.6 = (bf16[4,104,128]{2,1,0:T(8,128)(2,1)S(1)}, bf16[4,104,128]{2,1,0:T(8,128)(2,1)S(1)}, u32[]{:S(2)}, u32[]{:S(2)}) collective-permute-start(bf16[4,104,128]{2,1,0:T(8,128)(2,1)S(1)} %slice.7), channel_id=1, source_target_pairs={{0,384},{8,392},{16,400},{24,408},{32,416},{40,424},{48,432},{56,4... | collective-permute-start | bytes 319496 | tf_op jit(solution)/shard_map/ppermute | solution.py:212
  70.4 2.2 %collective-permute-start.5 = (bf16[4,104,128]{2,1,0:T(8,128)(2,1)S(1)}, bf16[4,104,128]{2,1,0:T(8,128)(2,1)S(1)}, u32[]{:S(2)}, u32[]{:S(2)}) collective-permute-start(bf16[4,104,128]{2,1,0:T(8,128)(2,1)S(1)} %slice.6), channel_id=1, source_target_pairs={{0,128},{8,136},{16,144},{24,152},{32,160},{40,168},{48,176},{56,1... | collective-permute-start | bytes 319496 | tf_op jit(solution)/shard_map/ppermute | solution.py:212
  72.5 3.9 %all-to-all-done.2 = bf16[64,8,320]{2,1,0:T(8,128)(2,1)S(1)} async-done(((bf16[64,8,320]{2,1,0:T(8,128)(2,1)}), bf16[64,8,320]{2,1,0:T(8,128)(2,1)S(1)}, u32[]{:S(2)}, u32[]{:S(2)}) %all-to-all-start.2) | async-done | bytes 327712 | tf_op jit(solution)/shard_map/all_to_all | solution.py:267
  76.4 0.0 copy-done.5
  76.4 2.0 %shard_map.67 = (bf16[2,704,768]{2,1,0:T(8,128)(2,1)S(1)}, f32[2,512,80]{2,1,0:T(8,128)S(1)}) custom-call(s32[1]{0:T(128)} %bitcast.owner_ref, s32[128]{0:T(128)S(1)} %copy-done.4, s32[128]{0:T(128)S(1)} %copy-done.5, bf16[512,320]{1,0:T(8,128)(2,1)S(1)} %bitcast.7), custom_call_target="tpu_custom_call" | custom-call | tf_op jit(solution)/shard_map/pallas_call | solution.py:275
  78.4 1.4 %shard_map.68.refs_0_ = f32[592,256]{1,0:T(8,128)S(1)} custom-call(s32[1]{0:T(128)} %bitcast.owner_ref, bf16[2,704,768]{2,1,0:T(8,128)(2,1)S(1)} %get-tuple-element.20.shifted_ref, bf16[8,104,128]{2,1,0:T(8,128)(2,1)S(1)} %all-to-all-done.refs_0_, bf16[8,104,128]{2,1,0:T(8,128)(2,1)S(1)} %collective-permute-done.refs_1_, ...), custom_call_target="tpu_custom_call" | custom-call | tf_op jit(solution)/shard_map/pallas_call | solution.py:287
  79.9 0.0 collective-permute-done.6.refs_3_.refs_7_
  79.9 0.5 collective-permute-done.5.refs_2_.refs_6_
  80.4 0.0 collective-permute-done.4.refs_1_.refs_5_
  80.4 0.0 collective-permute-done.7.refs_4_.refs_8_
  80.4 1.8 %shard_map.69 = bf16[80,512]{1,0:T(8,128)(2,1)S(1)} custom-call(s32[1]{0:T(128)} %bitcast.owner_ref, s32[128]{0:T(128)S(1)} %copy-done.4, s32[128]{0:T(128)S(1)} %copy-done.5, bf16[2,704,768]{2,1,0:T(8,128)(2,1)S(1)} %get-tuple-element.20.shifted_ref, f32[2,512,80]{2,1,0:T(8,128)S(1)} %get-tuple-element.26.packed_ref, f32[592,256]{1,0:T(8,128)S(1)} %shard_map.68.refs_0_, ...), custom_call_target="tpu_custom_call" | custom-call | tf_op jit(solution)/shard_map/pallas_call | solution.py:296
  82.2 3.3 %collective-permute-start.8 = (bf16[80,512]{1,0:T(8,128)(2,1)S(1)}, bf16[80,512]{1,0:T(8,128)(2,1)S(1)}, u32[]{:S(2)}, u32[]{:S(2)}) collective-permute-start(bf16[80,512]{1,0:T(8,128)(2,1)S(1)} %shard_map.69), channel_id=1, source_target_pairs={{0,8},{8,0},{16,24},{24,16},{32,40},{40,32},{48,56},{56,48},{64,72... | collective-permute-start | bytes 245768 | tf_op jit(solution)/shard_map/ppermute | solution.py:311
  85.5 3.5 %shard_map.70.own_hbm = bf16[160,512]{1,0:T(8,128)(2,1)} custom-call(s32[1]{0:T(128)} %bitcast.owner_ref, s32[128]{0:T(128)S(1)} %copy-done.4, s32[128]{0:T(128)S(1)} %copy-done.5, bf16[2,704,768]{2,1,0:T(8,128)(2,1)S(1)} %get-tuple-element.20.shifted_ref, f32[2,512,80]{2,1,0:T(8,128)S(1)} %get-tuple-element.26.packed_ref, ...), custom_call_target="tpu_custom_call" | custom-call | tf_op jit(solution)/shard_map/pallas_call | solution.py:296
  89.1 0.0 collective-permute-done.8.received_hbm
  89.1 0.7 shard_map.71
  (2 shorter events, 0.0 us)
Async XLA Ops:
  0.0 0.9 copy-start.3
  0.9 42.0 %copy-start.4 = (s32[128]{0:T(128)S(1)}, s32[128]{0:T(128)}, u32[]{:S(2)}) copy-start(s32[128]{0:T(128)} %order_ref.5) | copy-start | bytes 1540
  1.7 21.1 %all-to-all-start = ((bf16[8,104,128]{2,1,0:T(8,128)(2,1)}), bf16[8,104,128]{2,1,0:T(8,128)(2,1)S(1)}, u32[]{:S(2)}, u32[]{:S(2)}) async-start(bf16[8,104,128]{2,1,0:T(8,128)(2,1)} %shard_map.64), calls=%async_computation | async-start | bytes 425984 | tf_op jit(solution)/shard_map/all_to_all | solution.py:237
  12.0 1.3 %copy-start = (bf16[512,1280]{1,0:T(8,128)(2,1)S(1)}, bf16[512,1280]{1,0:T(8,128)(2,1)}, u32[]{:S(2)}) copy-start(bf16[512,1280]{1,0:T(8,128)(2,1)} %proj_hbm.1) | copy-start | bytes 3932164
  13.3 1.2 %copy-start.1 = (bf16[2,512,512]{2,1,0:T(8,128)(2,1)S(1)}, bf16[2,512,512]{2,1,0:T(8,128)(2,1)}, u32[]{:S(2)}) copy-start(bf16[2,512,512]{2,1,0:T(8,128)(2,1)} %conv_hbm.1) | copy-start | bytes 3145732
  14.5 0.9 %copy-start.2 = (bf16[16,16,512]{2,1,0:T(8,128)(2,1)S(1)}, bf16[16,16,512]{2,1,0:T(8,128)(2,1)}, u32[]{:S(2)}) copy-start(bf16[16,16,512]{2,1,0:T(8,128)(2,1)} %param.6) | copy-start | bytes 786436
  15.5 60.9 %copy-start.5 = (s32[128]{0:T(128)S(1)}, s32[128]{0:T(128)}, u32[]{:S(2)}) copy-start(s32[128]{0:T(128)} %len_ref.5) | copy-start | bytes 1540
  22.8 20.1 %all-to-all-start.1 = ((bf16[8,16,1280]{2,1,0:T(8,128)(2,1)}), bf16[8,16,1280]{2,1,0:T(8,128)(2,1)S(1)}, u32[]{:S(2)}, u32[]{:S(2)}) async-start(bf16[8,16,1280]{2,1,0:T(8,128)(2,1)} %shard_map.65), calls=%async_computation.1 | async-start | bytes 655360 | tf_op jit(solution)/shard_map/all_to_all | solution.py:254
  27.6 17.2 %collective-permute-start.3 = (bf16[8,104,128]{2,1,0:T(8,128)(2,1)S(1)}, bf16[8,104,128]{2,1,0:T(8,128)(2,1)S(1)}, u32[]{:S(2)}, u32[]{:S(2)}) collective-permute-start(bf16[8,104,128]{2,1,0:T(8,128)(2,1)S(1)} %all-to-all-done.refs_0_), channel_id=1, source_target_pairs={{0,384},{8,392},{16,400},{24,408},{32,416},{40,424},{48,432},{56,4... | collective-permute-start | bytes 638984 | tf_op jit(solution)/shard_map/ppermute | solution.py:212
  33.8 15.7 %collective-permute-start.2 = (bf16[8,104,128]{2,1,0:T(8,128)(2,1)S(1)}, bf16[8,104,128]{2,1,0:T(8,128)(2,1)S(1)}, u32[]{:S(2)}, u32[]{:S(2)}) collective-permute-start(bf16[8,104,128]{2,1,0:T(8,128)(2,1)S(1)} %all-to-all-done.refs_0_), channel_id=1, source_target_pairs={{0,128},{8,136},{16,144},{24,152},{32,160},{40,168},{48,176},{56,1... | collective-permute-start | bytes 638984 | tf_op jit(solution)/shard_map/ppermute | solution.py:212
  35.7 13.8 %collective-permute-start.1 = (bf16[8,104,128]{2,1,0:T(8,128)(2,1)S(1)}, bf16[8,104,128]{2,1,0:T(8,128)(2,1)S(1)}, u32[]{:S(2)}, u32[]{:S(2)}) collective-permute-start(bf16[8,104,128]{2,1,0:T(8,128)(2,1)S(1)} %all-to-all-done.refs_0_), channel_id=1, source_target_pairs={{0,448},{8,456},{16,464},{24,472},{32,480},{40,488},{48,496},{56,5... | collective-permute-start | bytes 638984 | tf_op jit(solution)/shard_map/ppermute | solution.py:212
  41.0 12.2 %collective-permute-start = (bf16[8,104,128]{2,1,0:T(8,128)(2,1)S(1)}, bf16[8,104,128]{2,1,0:T(8,128)(2,1)S(1)}, u32[]{:S(2)}, u32[]{:S(2)}) collective-permute-start(bf16[8,104,128]{2,1,0:T(8,128)(2,1)S(1)} %all-to-all-done.refs_0_), channel_id=1, source_target_pairs={{0,64},{8,72},{16,80},{24,88},{32,96},{40,104},{48,112},{56,120},{... | collective-permute-start | bytes 638984 | tf_op jit(solution)/shard_map/ppermute | solution.py:212
  53.2 23.2 %all-to-all-start.2 = ((bf16[64,8,320]{2,1,0:T(8,128)(2,1)}), bf16[64,8,320]{2,1,0:T(8,128)(2,1)S(1)}, u32[]{:S(2)}, u32[]{:S(2)}) async-start(bf16[64,8,320]{2,1,0:T(8,128)(2,1)} %bitcast.4), calls=%async_computation.2 | async-start | bytes 786432 | tf_op jit(solution)/shard_map/all_to_all | solution.py:267
  58.7 21.7 %collective-permute-start.4 = (bf16[8,104,128]{2,1,0:T(8,128)(2,1)S(1)}, bf16[8,104,128]{2,1,0:T(8,128)(2,1)S(1)}, u32[]{:S(2)}, u32[]{:S(2)}) collective-permute-start(bf16[8,104,128]{2,1,0:T(8,128)(2,1)S(1)} %collective-permute-done.2.refs_2_), channel_id=1, source_target_pairs={{0,64},{8,72},{16,80},{24,88},{32,96},{40,104},{48,112},{56,120},{... | collective-permute-start | bytes 638984 | tf_op jit(solution)/shard_map/ppermute | solution.py:212
  62.2 18.2 %collective-permute-start.7 = (bf16[8,104,128]{2,1,0:T(8,128)(2,1)S(1)}, bf16[8,104,128]{2,1,0:T(8,128)(2,1)S(1)}, u32[]{:S(2)}, u32[]{:S(2)}) collective-permute-start(bf16[8,104,128]{2,1,0:T(8,128)(2,1)S(1)} %collective-permute-done.3.refs_3_), channel_id=1, source_target_pairs={{0,448},{8,456},{16,464},{24,472},{32,480},{40,488},{48,496},{56,5... | collective-permute-start | bytes 638984 | tf_op jit(solution)/shard_map/ppermute | solution.py:212
  65.8 14.1 %collective-permute-start.6 = (bf16[4,104,128]{2,1,0:T(8,128)(2,1)S(1)}, bf16[4,104,128]{2,1,0:T(8,128)(2,1)S(1)}, u32[]{:S(2)}, u32[]{:S(2)}) collective-permute-start(bf16[4,104,128]{2,1,0:T(8,128)(2,1)S(1)} %slice.7), channel_id=1, source_target_pairs={{0,384},{8,392},{16,400},{24,408},{32,416},{40,424},{48,432},{56,4... | collective-permute-start | bytes 319496 | tf_op jit(solution)/shard_map/ppermute | solution.py:212
  70.4 10.0 %collective-permute-start.5 = (bf16[4,104,128]{2,1,0:T(8,128)(2,1)S(1)}, bf16[4,104,128]{2,1,0:T(8,128)(2,1)S(1)}, u32[]{:S(2)}, u32[]{:S(2)}) collective-permute-start(bf16[4,104,128]{2,1,0:T(8,128)(2,1)S(1)} %slice.6), channel_id=1, source_target_pairs={{0,128},{8,136},{16,144},{24,152},{32,160},{40,168},{48,176},{56,1... | collective-permute-start | bytes 319496 | tf_op jit(solution)/shard_map/ppermute | solution.py:212
  82.2 6.9 %collective-permute-start.8 = (bf16[80,512]{1,0:T(8,128)(2,1)S(1)}, bf16[80,512]{1,0:T(8,128)(2,1)S(1)}, u32[]{:S(2)}, u32[]{:S(2)}) collective-permute-start(bf16[80,512]{1,0:T(8,128)(2,1)S(1)} %shard_map.69), channel_id=1, source_target_pairs={{0,8},{8,0},{16,24},{24,16},{32,40},{40,32},{48,56},{56,48},{64,72... | collective-permute-start | bytes 245768 | tf_op jit(solution)/shard_map/ppermute | solution.py:311
